TPU v7x, 32 devices: a whole 2x2x4 slice. The times are simulated.
32 devices in a mesh: seq: 8 (over y, x, core), head: 4 (over z).
Axes of the slice: x: 2, y: 2, z: 4, core: 2. Of those that a mesh axis runs over, the one named last changes fastest.
Arguments:
- queries: bfloat16 [16384, 8192], P('seq', 'head'), may hold values from -6 to 6
- key_vectors: bfloat16 [16384, 8192], P('seq', 'head'), may hold values from -6 to 6
- value_vectors: bfloat16 [16384, 8192], P('seq', 'head'), may hold values from -6 to 6
- level_weights: float32 [64, 16, 16384], P('head', None, 'seq'), may hold values from 0.22 to 13.45, as said below
- norm_gain: float32 [8192], P('head'), may hold values from 0.25 to 1.75
Outputs:
- normed: bfloat16 [16384, 8192], P('seq', 'head')
Inputs may be any that keep to these rules, and one draw needn't show every extreme that they name: `level_weights`: positive.
All inputs are finite; a program needn't handle non-finite values.
Results may differ from a plain program's by a relative error of at most 0.0056.
Values may be sent and summed in bfloat16 or wider, within the bound.
No kernel may reach another device: no remote copies, remote signals or barrier semaphores. Data moves between devices by JAX's collectives and lax.ppermute only.
A program may use at most 256 MiB of HBM per device.

v0:
```python
import jax
import jax.numpy as jnp
from jax import lax
from jax.sharding import PartitionSpec as P

HEADS = 64
HEAD_DIM = 128
VALUE_DIM = 128


def bit_length(numbers, count):
    counted = jnp.zeros(numbers.shape, jnp.int32)
    for exponent in range(count):
        counted = counted + (numbers >= 1 << exponent).astype(jnp.int32)
    return counted


def body(queries, key_vectors, value_vectors, level_weights, norm_gain):
    rows_here = queries.shape[0]
    heads_here = level_weights.shape[0]
    query_rows = queries.reshape(rows_here, heads_here, HEAD_DIM)
    key_rows = key_vectors.reshape(rows_here, heads_here, HEAD_DIM)
    value_rows = value_vectors.reshape(rows_here, heads_here, VALUE_DIM)
    scaling = HEAD_DIM ** (-0.5)
    local_bits = rows_here.bit_length() - 1
    cross_bits = lax.axis_size("seq").bit_length() - 1
    position = lax.axis_index("seq")
    block_state = jnp.einsum(
        "thd,the->hde", key_rows, value_rows, preferred_element_type=jnp.float32
    ).astype(jnp.bfloat16)
    shards = lax.all_gather(block_state[None], "seq", axis=0, tiled=True)
    piece_rows = shards.shape[0]
    owners = jnp.arange(piece_rows, dtype=jnp.int32)
    collect_levels = jnp.arange(cross_bits, dtype=jnp.int32)
    own_bit = position >> collect_levels & 1
    matches = (
        owners[None, :] >> collect_levels[:, None] == (position >> collect_levels ^ 1)[:, None]
    ) & (own_bit[:, None] == 1)
    buckets = jnp.einsum(
        "bi,ihde->bhde", matches.astype(jnp.bfloat16), shards, preferred_element_type=jnp.float32
    )
    rounded = buckets.astype(jnp.bfloat16)
    readout = (
        jnp.einsum("thd,bhde->bhte", query_rows, rounded, preferred_element_type=jnp.float32)
        * scaling
    )
    across = jnp.zeros((heads_here, rows_here, VALUE_DIM), jnp.float32)
    for bit_level in range(cross_bits):
        across = (
            across
            + level_weights[:, local_bits + 1 + bit_level, :][:, :, None] * readout[bit_level]
        )
    row_block = min(rows_here, 512)
    pieces = []
    for start_row in range(0, rows_here, row_block):
        end_row = start_row + row_block
        row_ids = jnp.arange(start_row, end_row, dtype=jnp.int32)
        col_ids = jnp.arange(0, end_row, dtype=jnp.int32)
        levels = bit_length(row_ids[:, None] ^ col_ids[None, :], local_bits)
        scores = (
            jnp.einsum(
                "thd,shd->hts",
                query_rows[start_row:end_row],
                key_rows[:end_row],
                preferred_element_type=jnp.float32,
            )
            * scaling
        )
        factors = jnp.zeros(scores.shape, jnp.float32)
        for depth_id in range(local_bits + 1):
            factors = jnp.where(
                levels[None] == depth_id,
                level_weights[:, depth_id, start_row:end_row][:, :, None],
                factors,
            )
        causal = (col_ids[None, :] <= row_ids[:, None])[None]
        weighted = jnp.where(causal, scores * factors, 0.0).astype(jnp.bfloat16)
        pieces.append(
            jnp.einsum(
                "hts,she->hte", weighted, value_rows[:end_row], preferred_element_type=jnp.float32
            )
        )
    inside = jnp.concatenate(pieces, axis=1)
    mixture = (inside + across).transpose(1, 0, 2).reshape(rows_here, heads_here * VALUE_DIM)
    square = jnp.sum(mixture * mixture, axis=1)
    summed = lax.psum(square, "head")
    normed = mixture * norm_gain * lax.rsqrt(summed[:, None] / (HEADS * VALUE_DIM) + 1e-05)
    return normed.astype(jnp.bfloat16)


def solution(mesh):
    placed = (
        P("seq", "head"),
        P("seq", "head"),
        P("seq", "head"),
        P("head", None, "seq"),
        P("head"),
    )
    return jax.shard_map(
        body, mesh=mesh, in_specs=placed, out_specs=P("seq", "head"), check_vma=False
    )
```

profile of v0, /device:TPU:0, one launch (start us, length us, event | category | flops | bytes accessed | tf_op | source)
XLA Modules:
  0.0 554.6 jit_solution(16083339789716437701)
XLA Ops:
  6.5 12.2 %copy.297 = bf16[2048,2048]{0,1:T(8,128)(2,1)} copy(bf16[2048,2048]{1,0:T(8,128)(2,1)} %param.6) | data formatting | bytes 16777216 | tf_op jit(solution)/shard_map/reshape | solution.py:22
  18.8 9.4 %fusion.60 = bf16[16,128,128]{2,1,0:T(8,128)(2,1)} fusion(bf16[2048,16,128]{0,2,1:T(8,128)(2,1)} %bitcast.246, bf16[2048,2048]{1,0:T(8,128)(2,1)} %param.7), kind=kOutput, calls=%fused_computation.101 | convolution fusion | flops 1074003968 | bytes 17301504 | tf_op jit(solution)/shard_map/thd,the->hde/dot_general | solution.py:28
  29.6 0.9 fusion.92
  30.5 1.0 fusion.93
  31.5 1.2 broadcast_compare_fusion.45
  32.7 1.1 broadcast_compare_fusion.43
  33.8 1.1 broadcast_compare_fusion.41
  35.0 1.2 broadcast_compare_fusion.39
  36.1 1.1 broadcast_compare_fusion.37
  37.2 1.1 iota_compare_fusion.3
  38.4 1.3 fusion.91
  39.6 1.2 fusion.90
  40.9 3.4 slice.238
  44.3 5.2 slice.242
  49.5 2.4 slice.256
  52.0 1.6 slice-done.1
  53.6 3.3 slice.260
  56.8 6.7 %slice.274 = bf16[1536,2048]{1,0:T(8,128)(2,1)} slice(bf16[2048,2048]{1,0:T(8,128)(2,1)} %param.7), slice={[0:1536], [0:2048]} | slice | bytes 12582912 | tf_op jit(solution)/shard_map/slice | solution.py:80
  63.6 0.7 copy.374
  64.3 2.5 copy.237
  66.8 2.9 copy.250
  69.6 6.4 %copy.252 = bf16[1024,2048]{0,1:T(8,128)(2,1)} copy(bf16[1024,2048]{1,0:T(8,128)(2,1)} %slice.242) | data formatting | bytes 8388608
  76.0 6.4 %copy.265 = bf16[1024,2048]{0,1:T(8,128)(2,1)} copy(bf16[1024,2048]{1,0:T(8,128)(2,1)} %slice.256) | data formatting | bytes 8388608
  82.4 8.6 %copy.267 = bf16[1536,2048]{0,1:T(8,128)(2,1)} copy(bf16[1536,2048]{1,0:T(8,128)(2,1)} %slice.260) | data formatting | bytes 12582912
  91.0 8.6 %copy.280 = bf16[1536,2048]{0,1:T(8,128)(2,1)} copy(bf16[1536,2048]{1,0:T(8,128)(2,1)} %slice.274) | data formatting | bytes 12582912
  99.6 8.7 %iota_compare_fusion.2 = (pred[512,1024]{1,0:T(8,128)(4,1)}, pred[512,1024]{1,0:T(8,128)(4,1)}, pred[512,1024]{1,0:T(8,128)(4,1)}, pred[512,1024]{1,0:T(8,128)(4...) fusion(s32[512]{0:T(512)S(1)} %iota_add_fusion.2), kind=kLoop, calls=%fused_computation.85 | loop fusion | flops 24117248 | bytes 6817792 | tf_op jit(solution)/shard_map/le | solution.py:76
  108.4 6.0 %fusion.89 = (bf16[512,2048]{1,0:T(8,128)(2,1)}, bf16[512,2048]{1,0:T(8,128)(2,1)}, bf16[512,2048]{1,0:T(8,128)(2,1)}, bf16[512,2048]{1,0:T(8,128)(2,1)}) fusion(bf16[2048,2048]{1,0:T(8,128)(2,1)} %param.5), kind=kLoop, calls=%fused_computation.211 | loop fusion | bytes 16777216 | tf_op jit(solution)/shard_map/slice | solution.py:63
  114.4 3.9 copy.236
  118.3 3.9 copy.266
  122.2 4.0 copy.251
  126.2 3.9 copy.281
  130.1 10.7 %iota_compare_fusion.1 = (pred[512,1536]{1,0:T(8,128)(4,1)}, pred[512,1536]{1,0:T(8,128)(4,1)}, pred[512,1536]{1,0:T(8,128)(4,1)}, pred[512,1536]{1,0:T(8,128)(4...) fusion(s32[512]{0:T(512)S(1)} %iota_add_fusion.1), kind=kLoop, calls=%fused_computation.59 | loop fusion | flops 36175872 | bytes 10225664 | tf_op jit(solution)/shard_map/le | solution.py:76
  141.2 14.9 %iota_compare_fusion = (pred[512,2048]{1,0:T(8,128)(4,1)S(1)}, pred[512,2048]{1,0:T(8,128)(4,1)}, pred[512,2048]{1,0:T(8,128)(4,1)}, pred[512,2048]{1,0:T(8,128)...) fusion(s32[512]{0:T(512)S(1)} %iota_add_fusion), kind=kLoop, calls=%fused_computation.45 | loop fusion | flops 48234496 | bytes 13633536 | tf_op jit(solution)/shard_map/le | solution.py:76
  156.1 0.8 copy_bitcast_fusion.47
  156.9 0.8 copy_bitcast_fusion.39
  157.7 0.8 copy_bitcast_fusion.41
  158.5 1.4 copy_bitcast_fusion.21
  159.9 1.4 copy_bitcast_fusion.23
  161.3 1.4 copy_bitcast_fusion.25
  162.7 1.4 copy_bitcast_fusion.27
  164.1 1.4 copy_bitcast_fusion.29
  165.5 1.4 copy_bitcast_fusion.31
  166.9 0.6 copy_bitcast_fusion.33
  167.5 0.6 copy_bitcast_fusion.35
  168.1 0.6 copy_bitcast_fusion.37
  169.4 0.6 copy_bitcast_fusion.5
  171.9 0.6 copy_bitcast_fusion.13
  172.6 0.6 copy_bitcast_fusion.15
  173.8 0.6 copy_bitcast_fusion.19
  174.6 21.0 %select_convert_fusion.4.clone.4 = bf16[16,512,512]{2,1,0:T(8,128)(2,1)S(1)} fusion(bf16[512,16,128]{0,2,1:T(8,128)(2,1)S(1)} %bitcast.257, bf16[512,16,128]{0,2,1:T(8,128)(2,1)S(1)} %bitcast.255, f32[16,512]{1,0:T(8,128)S(1)} %get-tuple-element.139, f32[16,512]{1,0:T(8,128)S(1)} %get-tuple-element.140, ...), kind=kOutput, calls=%fused_computation.20.clone.clone.clone.1 | convolution fusion | flops 1140850688 | bytes 16384000 | tf_op jit(solution)/shard_map/thd,shd->hts/dot_general | solution.py:61
  195.5 4.3 fusion.55
  199.9 87.1 %select_convert_fusion.11 = bf16[16,512,2048]{2,1,0:T(8,128)(2,1)} fusion(f32[16,512]{1,0:T(8,128)} %get-tuple-element.103, f32[16,512]{1,0:T(8,128)} %get-tuple-element.104, f32[16,512]{1,0:T(8,128)} %get-tuple-element.105, f32[16,512]{1,0:T(8,128)} %get-tuple-element.106, f32[16,512]{1,0:T(8,128)} %get-tuple-element.107, ...), kind=kOutput, calls=%fused_computation.clone.clone.2 | convolution fusion | flops 4563402752 | bytes 58064896 | tf_op jit(solution)/shard_map/thd,shd->hts/dot_general | solution.py:61
  287.3 44.2 %select_convert_fusion.12 = bf16[16,512,1024]{2,1,0:T(8,128)(2,1)} fusion(f32[16,512]{1,0:T(8,128)S(1)} %copy-done.54, f32[16,512]{1,0:T(8,128)S(1)} %copy-done.55, f32[16,512]{1,0:T(8,128)S(1)} %copy-done.56, f32[16,512]{1,0:T(8,128)S(1)} %copy-done.57, f32[16,512]{1,0:T(8,128)S(1)} %copy-done.58, f32[16,512]{1,0:T(8,128)S(1)} %copy-done.59, ...), kind=kOutput, calls=%fused_computation.3.clone.clone.1 | convolution fusion | flops 2281701376 | bytes 30277632 | tf_op jit(solution)/shard_map/thd,shd->hts/dot_general | solution.py:61
  331.6 63.0 %select_convert_fusion.1.clone.4 = bf16[16,512,1536]{2,1,0:T(8,128)(2,1)} fusion(bf16[512,16,128]{0,2,1:T(8,128)(2,1)S(1)} %bitcast.253, bf16[1536,16,128]{0,2,1:T(8,128)(2,1)S(1)} %bitcast.249, f32[16,512]{1,0:T(8,128)S(1)} %copy-done.66, f32[16,512]{1,0:T(8,128)S(1)} %copy-done.67, f32[16,512]{1,0:T(8,128)S(1)} %copy-done.68, ...), kind=kOutput, calls=%fused_computation.2.clone.clone.clone.1 | convolution fusion | flops 3422552064 | bytes 44171264 | tf_op jit(solution)/shard_map/thd,shd->hts/dot_general | solution.py:61
  394.7 14.7 %fusion.1 = f32[16,512,128]{2,1,0:T(8,128)} fusion(bf16[1536,16,128]{0,2,1:T(8,128)(2,1)} %bitcast.248, bf16[16,512,1536]{2,1,0:T(8,128)(2,1)} %select_convert_fusion.1.clone.4), kind=kOutput, calls=%fused_computation.5 | convolution fusion | flops 3221225472 | bytes 35651584 | tf_op jit(solution)/shard_map/hts,she->hte/dot_general | solution.py:79
  409.4 13.6 %fusion.11 = f32[16,512,128]{2,1,0:T(8,128)} fusion(bf16[1024,16,128]{0,2,1:T(8,128)(2,1)} %bitcast.251, bf16[16,512,1024]{2,1,0:T(8,128)(2,1)} %select_convert_fusion.12), kind=kOutput, calls=%fused_computation.21 | convolution fusion | flops 2147483648 | bytes 25165824 | tf_op jit(solution)/shard_map/hts,she->hte/dot_general | solution.py:79
  423.0 19.2 %fusion = f32[16,512,128]{2,1,0:T(8,128)} fusion(bf16[2048,2048]{1,0:T(8,128)(2,1)} %param.7, bf16[16,512,2048]{2,1,0:T(8,128)(2,1)} %select_convert_fusion.11), kind=kOutput, calls=%fused_computation.4 | convolution fusion | flops 4294967296 | bytes 46137344 | tf_op jit(solution)/shard_map/hts,she->hte/dot_general | solution.py:79
  442.3 5.0 fusion.56
  447.3 21.7 %multiply_bitcast_fusion = f32[3,16,2048,128]{3,2,1,0:T(8,128)} fusion(bf16[3,16,128,128]{3,0,2,1:T(4,128)(2,1)S(1)} %fusion.56, bf16[2048,2048]{1,0:T(8,128)(2,1)} %param.5), kind=kOutput, calls=%fused_computation.1 | convolution fusion | flops 3233808384 | bytes 60293120 | tf_op jit(solution)/shard_map/thd,bhde->bhte/dot_general | solution.py:44
  469.0 25.7 %multiply_reduce_fusion = (f32[2048]{0:T(1024)S(1)}, f32[2048,16,128]{2,0,1:T(8,128)}) fusion(f32[3,16,2048,128]{3,2,1,0:T(8,128)} %multiply_bitcast_fusion, f32[16,2048]{1,0:T(8,128)S(1)} %get-tuple-element.101, f32[16,2048]{1,0:T(8,128)S(1)} %get-tuple-element.102, f32[16,2048]{1,0:T(8,128)S(1)} %bitcast.258, f32[16,512,128]{2,1,0:T(8,128)} %fusion, ...), kind=kLoop, calls=%fused_computation.19 | loop fusion | flops 46135296 | bytes 84287488 | tf_op jit(solution)/shard_map/reduce_sum | solution.py:85
  494.7 13.3 %psum.7 = f32[2048]{0:T(1024)S(1)} all-reduce(f32[2048]{0:T(1024)S(1)} %get-tuple-element.5), channel_id=1, replica_groups=mesh['seq'=8,'head'=4] {'head'}, use_global_device_ids=true, to_apply=%region_1.2 | all-reduce | flops 2048 | bytes 16384 | tf_op jit(solution)/shard_map/psum | solution.py:86
  508.0 17.7 %copy.220 = f32[2048,16,128]{0,2,1:T(8,128)} copy(f32[2048,16,128]{2,0,1:T(8,128)} %get-tuple-element.6) | data formatting | bytes 33554432 | tf_op jit(solution)/shard_map/transpose | solution.py:84
  525.6 9.5 %fusion.10 = bf16[2048,2048]{0,1:T(8,128)(2,1)} fusion(f32[2048,16,128]{0,2,1:T(8,128)} %copy.220, f32[2048]{0:T(1024)S(1)} %add_rsqrt_fusion, f32[2048]{0:T(1024)S(1)} %copy-done.69), kind=kLoop, calls=%fused_computation.18 | loop fusion | flops 12582912 | bytes 25182208 | tf_op jit(solution)/shard_map/convert_element_type | solution.py:88
  535.1 12.2 %copy.221 = bf16[2048,2048]{1,0:T(8,128)(2,1)} copy(bf16[2048,2048]{0,1:T(8,128)(2,1)} %fusion.10) | data formatting | bytes 16777216 | tf_op jit(solution)/shard_map/convert_element_type | solution.py:88
  (174 shorter events, 5.0 us)
Async XLA Ops:
  6.5 435.7 %all-gather.3.cloned.1.call-start = ((), (), s32[]{:S(2)}) async-start(), calls=%async_computation | async-start | bytes 4718592 | tf_op jit(solution)/shard_map/all_gather | solution.py:31
  140.8 26.1 %copy-start.44 = (f32[16,1,512]{2,1,0:T(1,128)S(1)}, f32[16,1,512]{2,1,0:T(1,128)}, u32[]{:S(2)}) copy-start(f32[16,1,512]{2,1,0:T(1,128)} %get-tuple-element.43) | copy-start | bytes 98308
  140.8 26.0 %copy-start.45 = (f32[16,1,512]{2,1,0:T(1,128)S(1)}, f32[16,1,512]{2,1,0:T(1,128)}, u32[]{:S(2)}) copy-start(f32[16,1,512]{2,1,0:T(1,128)} %get-tuple-element.44) | copy-start | bytes 98308
  140.8 26.7 %copy-start.40 = (f32[16,1,512]{2,1,0:T(1,128)S(1)}, f32[16,1,512]{2,1,0:T(1,128)}, u32[]{:S(2)}) copy-start(f32[16,1,512]{2,1,0:T(1,128)} %get-tuple-element.45) | copy-start | bytes 98308
  140.8 26.7 %copy-start.41 = (f32[16,1,512]{2,1,0:T(1,128)S(1)}, f32[16,1,512]{2,1,0:T(1,128)}, u32[]{:S(2)}) copy-start(f32[16,1,512]{2,1,0:T(1,128)} %get-tuple-element.46) | copy-start | bytes 98308
  140.9 27.3 %copy-start.38 = (f32[16,1,512]{2,1,0:T(1,128)S(1)}, f32[16,1,512]{2,1,0:T(1,128)}, u32[]{:S(2)}) copy-start(f32[16,1,512]{2,1,0:T(1,128)} %get-tuple-element.47) | copy-start | bytes 98308
  140.9 27.3 %copy-start.39 = (f32[16,1,512]{2,1,0:T(1,128)S(1)}, f32[16,1,512]{2,1,0:T(1,128)}, u32[]{:S(2)}) copy-start(f32[16,1,512]{2,1,0:T(1,128)} %get-tuple-element.48) | copy-start | bytes 98308
  140.9 27.9 %copy-start.36 = (f32[16,1,512]{2,1,0:T(1,128)S(1)}, f32[16,1,512]{2,1,0:T(1,128)}, u32[]{:S(2)}) copy-start(f32[16,1,512]{2,1,0:T(1,128)} %get-tuple-element.30) | copy-start | bytes 98308
  140.9 27.9 %copy-start.37 = (f32[16,1,512]{2,1,0:T(1,128)S(1)}, f32[16,1,512]{2,1,0:T(1,128)}, u32[]{:S(2)}) copy-start(f32[16,1,512]{2,1,0:T(1,128)} %get-tuple-element.11) | copy-start | bytes 98308
  140.9 27.9 %copy-start.34 = (f32[16,1,512]{2,1,0:T(1,128)S(1)}, f32[16,1,512]{2,1,0:T(1,128)}, u32[]{:S(2)}) copy-start(f32[16,1,512]{2,1,0:T(1,128)} %get-tuple-element.12) | copy-start | bytes 98308
  140.9 27.9 %copy-start.35 = (f32[16,1,512]{2,1,0:T(1,128)S(1)}, f32[16,1,512]{2,1,0:T(1,128)}, u32[]{:S(2)}) copy-start(f32[16,1,512]{2,1,0:T(1,128)} %get-tuple-element.13) | copy-start | bytes 98308
  140.9 28.5 %copy-start.32 = (f32[16,1,512]{2,1,0:T(1,128)S(1)}, f32[16,1,512]{2,1,0:T(1,128)}, u32[]{:S(2)}) copy-start(f32[16,1,512]{2,1,0:T(1,128)} %get-tuple-element.14) | copy-start | bytes 98308
  140.9 28.5 %copy-start.33 = (f32[16,1,512]{2,1,0:T(1,128)S(1)}, f32[16,1,512]{2,1,0:T(1,128)}, u32[]{:S(2)}) copy-start(f32[16,1,512]{2,1,0:T(1,128)} %get-tuple-element.15) | copy-start | bytes 98308
  140.9 29.1 %copy-start.30 = (f32[16,1,512]{2,1,0:T(1,128)S(1)}, f32[16,1,512]{2,1,0:T(1,128)}, u32[]{:S(2)}) copy-start(f32[16,1,512]{2,1,0:T(1,128)} %get-tuple-element.16) | copy-start | bytes 98308
  140.9 29.1 %copy-start.31 = (f32[16,1,512]{2,1,0:T(1,128)S(1)}, f32[16,1,512]{2,1,0:T(1,128)}, u32[]{:S(2)}) copy-start(f32[16,1,512]{2,1,0:T(1,128)} %get-tuple-element.17) | copy-start | bytes 98308
  141.0 29.7 %copy-start.28 = (f32[16,1,512]{2,1,0:T(1,128)S(1)}, f32[16,1,512]{2,1,0:T(1,128)}, u32[]{:S(2)}) copy-start(f32[16,1,512]{2,1,0:T(1,128)} %get-tuple-element.18) | copy-start | bytes 98308
  141.0 29.7 %copy-start.29 = (f32[16,1,512]{2,1,0:T(1,128)S(1)}, f32[16,1,512]{2,1,0:T(1,128)}, u32[]{:S(2)}) copy-start(f32[16,1,512]{2,1,0:T(1,128)} %get-tuple-element.19) | copy-start | bytes 98308
  141.0 30.3 %copy-start.26 = (f32[16,1,512]{2,1,0:T(1,128)S(1)}, f32[16,1,512]{2,1,0:T(1,128)}, u32[]{:S(2)}) copy-start(f32[16,1,512]{2,1,0:T(1,128)} %get-tuple-element.20) | copy-start | bytes 98308
  141.0 30.3 %copy-start.27 = (f32[16,1,512]{2,1,0:T(1,128)S(1)}, f32[16,1,512]{2,1,0:T(1,128)}, u32[]{:S(2)}) copy-start(f32[16,1,512]{2,1,0:T(1,128)} %get-tuple-element.21) | copy-start | bytes 98308
  141.0 30.9 %copy-start.24 = (f32[16,1,512]{2,1,0:T(1,128)S(1)}, f32[16,1,512]{2,1,0:T(1,128)}, u32[]{:S(2)}) copy-start(f32[16,1,512]{2,1,0:T(1,128)} %get-tuple-element.22) | copy-start | bytes 98308
  141.0 30.9 %copy-start.25 = (f32[16,1,512]{2,1,0:T(1,128)S(1)}, f32[16,1,512]{2,1,0:T(1,128)}, u32[]{:S(2)}) copy-start(f32[16,1,512]{2,1,0:T(1,128)} %get-tuple-element.23) | copy-start | bytes 98308
  141.0 31.5 %copy-start.22 = (f32[16,1,512]{2,1,0:T(1,128)S(1)}, f32[16,1,512]{2,1,0:T(1,128)}, u32[]{:S(2)}) copy-start(f32[16,1,512]{2,1,0:T(1,128)} %get-tuple-element.24) | copy-start | bytes 98308
  141.0 31.5 %copy-start.23 = (f32[16,1,512]{2,1,0:T(1,128)S(1)}, f32[16,1,512]{2,1,0:T(1,128)}, u32[]{:S(2)}) copy-start(f32[16,1,512]{2,1,0:T(1,128)} %get-tuple-element.25) | copy-start | bytes 98308
  141.0 33.4 %copy-start.3 = (bf16[512,2048]{0,1:T(8,128)(2,1)S(1)}, bf16[512,2048]{0,1:T(8,128)(2,1)}, u32[]{:S(2)}) copy-start(bf16[512,2048]{0,1:T(8,128)(2,1)} %copy.237) | copy-start | bytes 6291460
  141.0 33.4 %copy-start.4 = (bf16[512,2048]{0,1:T(8,128)(2,1)S(1)}, bf16[512,2048]{0,1:T(8,128)(2,1)}, u32[]{:S(2)}) copy-start(bf16[512,2048]{0,1:T(8,128)(2,1)} %copy.236) | copy-start | bytes 6291460
  141.1 33.4 %copy-start.10 = (pred[512,512]{1,0:T(8,128)(4,1)S(1)}, pred[512,512]{1,0:T(8,128)(4,1)}, u32[]{:S(2)}) copy-start(pred[512,512]{1,0:T(8,128)(4,1)} %get-tuple-element.159) | copy-start | bytes 786436
  141.1 33.4 %copy-start.11 = (pred[512,512]{1,0:T(8,128)(4,1)S(1)}, pred[512,512]{1,0:T(8,128)(4,1)}, u32[]{:S(2)}) copy-start(pred[512,512]{1,0:T(8,128)(4,1)} %get-tuple-element.160) | copy-start | bytes 786436
  141.1 33.4 %copy-start.12 = (pred[512,512]{1,0:T(8,128)(4,1)S(1)}, pred[512,512]{1,0:T(8,128)(4,1)}, u32[]{:S(2)}) copy-start(pred[512,512]{1,0:T(8,128)(4,1)} %get-tuple-element.157) | copy-start | bytes 786436
  141.1 33.4 %copy-start.13 = (pred[512,512]{1,0:T(8,128)(4,1)S(1)}, pred[512,512]{1,0:T(8,128)(4,1)}, u32[]{:S(2)}) copy-start(pred[512,512]{1,0:T(8,128)(4,1)} %get-tuple-element.158) | copy-start | bytes 786436
  141.1 33.4 %copy-start.14 = (pred[512,512]{1,0:T(8,128)(4,1)S(1)}, pred[512,512]{1,0:T(8,128)(4,1)}, u32[]{:S(2)}) copy-start(pred[512,512]{1,0:T(8,128)(4,1)} %get-tuple-element.155) | copy-start | bytes 786436
  141.1 33.4 %copy-start.15 = (pred[512,512]{1,0:T(8,128)(4,1)S(1)}, pred[512,512]{1,0:T(8,128)(4,1)}, u32[]{:S(2)}) copy-start(pred[512,512]{1,0:T(8,128)(4,1)} %get-tuple-element.156) | copy-start | bytes 786436
  141.1 33.4 %copy-start.16 = (pred[512,512]{1,0:T(8,128)(4,1)S(1)}, pred[512,512]{1,0:T(8,128)(4,1)}, u32[]{:S(2)}) copy-start(pred[512,512]{1,0:T(8,128)(4,1)} %get-tuple-element.153) | copy-start | bytes 786436
  141.1 33.4 %copy-start.17 = (pred[512,512]{1,0:T(8,128)(4,1)S(1)}, pred[512,512]{1,0:T(8,128)(4,1)}, u32[]{:S(2)}) copy-start(pred[512,512]{1,0:T(8,128)(4,1)} %get-tuple-element.154) | copy-start | bytes 786436
  141.1 33.4 %copy-start.18 = (pred[512,512]{1,0:T(8,128)(4,1)S(1)}, pred[512,512]{1,0:T(8,128)(4,1)}, u32[]{:S(2)}) copy-start(pred[512,512]{1,0:T(8,128)(4,1)} %get-tuple-element.151) | copy-start | bytes 786436
  141.1 33.4 %copy-start.19 = (pred[512,512]{1,0:T(8,128)(4,1)S(1)}, pred[512,512]{1,0:T(8,128)(4,1)}, u32[]{:S(2)}) copy-start(pred[512,512]{1,0:T(8,128)(4,1)} %get-tuple-element.152) | copy-start | bytes 786436
  141.2 33.4 %copy-start.20 = (pred[512,512]{1,0:T(8,128)(4,1)S(1)}, pred[512,512]{1,0:T(8,128)(4,1)}, u32[]{:S(2)}) copy-start(pred[512,512]{1,0:T(8,128)(4,1)} %get-tuple-element.149) | copy-start | bytes 786436
  141.2 33.4 %copy-start.21 = (pred[512,512]{1,0:T(8,128)(4,1)S(1)}, pred[512,512]{1,0:T(8,128)(4,1)}, u32[]{:S(2)}) copy-start(pred[512,512]{1,0:T(8,128)(4,1)} %get-tuple-element.150) | copy-start | bytes 786436
  199.8 87.2 %copy-start.54 = (f32[16,512]{1,0:T(8,128)S(1)}, f32[16,512]{1,0:T(8,128)}, u32[]{:S(2)}) copy-start(f32[16,512]{1,0:T(8,128)} %get-tuple-element.127) | copy-start | bytes 98308
  199.8 87.2 %copy-start.55 = (f32[16,512]{1,0:T(8,128)S(1)}, f32[16,512]{1,0:T(8,128)}, u32[]{:S(2)}) copy-start(f32[16,512]{1,0:T(8,128)} %get-tuple-element.128) | copy-start | bytes 98308
  199.8 87.3 %copy-start.56 = (f32[16,512]{1,0:T(8,128)S(1)}, f32[16,512]{1,0:T(8,128)}, u32[]{:S(2)}) copy-start(f32[16,512]{1,0:T(8,128)} %get-tuple-element.129) | copy-start | bytes 98308
  199.8 87.3 %copy-start.57 = (f32[16,512]{1,0:T(8,128)S(1)}, f32[16,512]{1,0:T(8,128)}, u32[]{:S(2)}) copy-start(f32[16,512]{1,0:T(8,128)} %get-tuple-element.130) | copy-start | bytes 98308
  199.8 87.3 %copy-start.58 = (f32[16,512]{1,0:T(8,128)S(1)}, f32[16,512]{1,0:T(8,128)}, u32[]{:S(2)}) copy-start(f32[16,512]{1,0:T(8,128)} %get-tuple-element.131) | copy-start | bytes 98308
  199.8 87.3 %copy-start.59 = (f32[16,512]{1,0:T(8,128)S(1)}, f32[16,512]{1,0:T(8,128)}, u32[]{:S(2)}) copy-start(f32[16,512]{1,0:T(8,128)} %get-tuple-element.132) | copy-start | bytes 98308
  199.8 87.3 %copy-start.60 = (f32[16,512]{1,0:T(8,128)S(1)}, f32[16,512]{1,0:T(8,128)}, u32[]{:S(2)}) copy-start(f32[16,512]{1,0:T(8,128)} %get-tuple-element.133) | copy-start | bytes 98308
  199.8 87.3 %copy-start.61 = (f32[16,512]{1,0:T(8,128)S(1)}, f32[16,512]{1,0:T(8,128)}, u32[]{:S(2)}) copy-start(f32[16,512]{1,0:T(8,128)} %get-tuple-element.134) | copy-start | bytes 98308
  199.8 87.3 %copy-start.62 = (f32[16,512]{1,0:T(8,128)S(1)}, f32[16,512]{1,0:T(8,128)}, u32[]{:S(2)}) copy-start(f32[16,512]{1,0:T(8,128)} %get-tuple-element.135) | copy-start | bytes 98308
  199.9 87.3 %copy-start.63 = (f32[16,512]{1,0:T(8,128)S(1)}, f32[16,512]{1,0:T(8,128)}, u32[]{:S(2)}) copy-start(f32[16,512]{1,0:T(8,128)} %get-tuple-element.136) | copy-start | bytes 98308
  199.9 87.3 %copy-start.64 = (f32[16,512]{1,0:T(8,128)S(1)}, f32[16,512]{1,0:T(8,128)}, u32[]{:S(2)}) copy-start(f32[16,512]{1,0:T(8,128)} %get-tuple-element.137) | copy-start | bytes 98308
  199.9 87.3 %copy-start.65 = (f32[16,512]{1,0:T(8,128)S(1)}, f32[16,512]{1,0:T(8,128)}, u32[]{:S(2)}) copy-start(f32[16,512]{1,0:T(8,128)} %get-tuple-element.138) | copy-start | bytes 98308
  287.2 44.4 %copy-start.1 = (bf16[1536,2048]{0,1:T(8,128)(2,1)S(1)}, bf16[1536,2048]{0,1:T(8,128)(2,1)}, u32[]{:S(2)}) copy-start(bf16[1536,2048]{0,1:T(8,128)(2,1)} %copy.267) | copy-start | bytes 18874372
  287.2 44.4 %copy-start.2 = (bf16[512,2048]{0,1:T(8,128)(2,1)S(1)}, bf16[512,2048]{0,1:T(8,128)(2,1)}, u32[]{:S(2)}) copy-start(bf16[512,2048]{0,1:T(8,128)(2,1)} %copy.266) | copy-start | bytes 6291460
  287.2 44.4 %copy-start.6 = (pred[512,1536]{1,0:T(8,128)(4,1)S(1)}, pred[512,1536]{1,0:T(8,128)(4,1)}, u32[]{:S(2)}) copy-start(pred[512,1536]{1,0:T(8,128)(4,1)} %get-tuple-element.75) | copy-start | bytes 2359300
  287.2 44.4 %copy-start.48 = (f32[16,512]{1,0:T(8,128)S(1)}, f32[16,512]{1,0:T(8,128)}, u32[]{:S(2)}) copy-start(f32[16,512]{1,0:T(8,128)} %get-tuple-element.121) | copy-start | bytes 98308
  287.2 44.4 %copy-start.49 = (f32[16,512]{1,0:T(8,128)S(1)}, f32[16,512]{1,0:T(8,128)}, u32[]{:S(2)}) copy-start(f32[16,512]{1,0:T(8,128)} %get-tuple-element.122) | copy-start | bytes 98308
  287.2 44.4 %copy-start.50 = (f32[16,512]{1,0:T(8,128)S(1)}, f32[16,512]{1,0:T(8,128)}, u32[]{:S(2)}) copy-start(f32[16,512]{1,0:T(8,128)} %get-tuple-element.123) | copy-start | bytes 98308
  287.2 44.4 %copy-start.51 = (f32[16,512]{1,0:T(8,128)S(1)}, f32[16,512]{1,0:T(8,128)}, u32[]{:S(2)}) copy-start(f32[16,512]{1,0:T(8,128)} %get-tuple-element.124) | copy-start | bytes 98308
  287.2 44.4 %copy-start.52 = (f32[16,512]{1,0:T(8,128)S(1)}, f32[16,512]{1,0:T(8,128)}, u32[]{:S(2)}) copy-start(f32[16,512]{1,0:T(8,128)} %get-tuple-element.125) | copy-start | bytes 98308
  287.2 44.4 %copy-start.53 = (f32[16,512]{1,0:T(8,128)S(1)}, f32[16,512]{1,0:T(8,128)}, u32[]{:S(2)}) copy-start(f32[16,512]{1,0:T(8,128)} %get-tuple-element.126) | copy-start | bytes 98308
  287.2 44.4 %copy-start.66 = (f32[16,512]{1,0:T(8,128)S(1)}, f32[16,512]{1,0:T(8,128)}, u32[]{:S(2)}) copy-start(f32[16,512]{1,0:T(8,128)} %get-tuple-element.115) | copy-start | bytes 98308
  287.3 44.4 %copy-start.67 = (f32[16,512]{1,0:T(8,128)S(1)}, f32[16,512]{1,0:T(8,128)}, u32[]{:S(2)}) copy-start(f32[16,512]{1,0:T(8,128)} %get-tuple-element.116) | copy-start | bytes 98308
  287.3 44.4 %copy-start.68 = (f32[16,512]{1,0:T(8,128)S(1)}, f32[16,512]{1,0:T(8,128)}, u32[]{:S(2)}) copy-start(f32[16,512]{1,0:T(8,128)} %get-tuple-element.117) | copy-start | bytes 98308
  331.6 63.0 %copy-start.8 = (f32[16,1,2048]{2,1,0:T(1,128)S(1)}, f32[16,1,2048]{2,1,0:T(1,128)}, u32[]{:S(2)}) copy-start(f32[16,1,2048]{2,1,0:T(1,128)} %get-tuple-element.60) | copy-start | bytes 393220
  331.6 63.0 %copy-start.9 = (f32[16,1,2048]{2,1,0:T(1,128)S(1)}, f32[16,1,2048]{2,1,0:T(1,128)}, u32[]{:S(2)}) copy-start(f32[16,1,2048]{2,1,0:T(1,128)} %get-tuple-element.61) | copy-start | bytes 393220
  447.3 21.7 %copy-start = (f32[16,512,128]{2,1,0:T(8,128)S(1)}, f32[16,512,128]{2,1,0:T(8,128)}, u32[]{:S(2)}) copy-start(f32[16,512,128]{2,1,0:T(8,128)} %fusion.55) | copy-start | bytes 12582916
  (14 other events, 195.7 us)
Sparse Core Ops, SparseCore 0:
  28.3 39.4 all-gather.2
where the time goes:
time: 565 us; the launch traced here: 555 us
  matrix products  303 us (54%)
  local copies, waits for them, and re-layouts  146 us (26%)
  other arithmetic  77.8 us (14%)
  between operations  14.9 us (3%)
  blocking collectives  13.3 us (2%)
    dot_general x4, matrix products, body(): jnp.einsum('thd,shd->hts', query_rows[start_row:end_row], key_rows[:end_r...  215 us
    unnamed x163, local copies, waits for them, and re-layouts  53.7 us
    dot_general x4, matrix products, body(): jnp.einsum('hts,she->hte', weighted, value_rows[:end_row], preferred_elem...  51.7 us
    le x4, other arithmetic, body(): causal = (col_ids[None, :] <= row_ids[:, None])[None]  35.5 us
    reduce_sum x1, other arithmetic, body(): square = jnp.sum(mixture * mixture, axis=1)  25.7 us
    dot_general x1, matrix products, body(): jnp.einsum('thd,bhde->bhte', query_rows, rounded, preferred_element_type=...  21.7 us
    broadcast_in_dim x24, local copies, waits for them, and re-layouts, body(): jnp.where(levels[None] == depth_id, level_weights[:, depth_id, start_row:...  18.2 us
    transpose x1, local copies, waits for them, and re-layouts, body(): (inside + across).transpose(1, 0, 2)  17.7 us
  transfers between devices with their start and end apart: 1, of which 0 were waited for; matrix products, arithmetic and copies ran while one was open for 74% of the time, Pallas kernels for 0%

commit v1 on v0

v1 whole, which is shorter than its diff:
```python
import functools

import jax
import jax.numpy as jnp
from jax import lax
from jax.experimental import pallas as pl
from jax.experimental.pallas import tpu as pltpu
from jax.sharding import PartitionSpec as P

HEADS = 64
HEAD_DIM = 128
VALUE_DIM = 128
CHUNK = 256
HALF = 128
GROUP = 8
B_PARTS = 4
C_PARTS = 2
SCALING = HEAD_DIM ** (-0.5)

TT = (((1,), (1,)), ((), ()))
LT = (((0,), (0,)), ((), ()))
NN = (((1,), (0,)), ((), ()))


def dot(a, b, dims):
    return lax.dot_general(a, b, dims, preferred_element_type=jnp.float32)


def bucket_slot(depth_count, depth, chunk):
    before = sum(1 << (depth_count - d - 1) for d in range(depth))
    return before + (((chunk >> depth) - 1) >> 1)


def state_kernel(k_ref, v_ref, local_ref, block_ref):
    rows = k_ref.shape[0]
    chunks = rows // CHUNK
    depth_count = chunks.bit_length() - 1
    sums = []
    for c in range(chunks):
        here = pl.ds(c * CHUNK, CHUNK)
        sums.append(dot(v_ref[here, :], k_ref[here, :], LT))
    slot = 0
    for _ in range(depth_count):
        for m in range(0, len(sums), 2):
            local_ref[0, slot] = sums[m].astype(jnp.bfloat16)
            slot += 1
        sums = [sums[m] + sums[m + 1] for m in range(0, len(sums), 2)]
    block_ref[0] = sums[0].astype(jnp.bfloat16)


def local_factors(w_ref, start):
    def row(level):
        return w_ref[0, level : level + 1, start : start + HALF] * SCALING

    groups = HALF // GROUP
    group_id = lax.broadcasted_iota(jnp.int32, (groups, HALF), 0)
    lane_group = lax.broadcasted_iota(jnp.int32, (groups, HALF), 1) >> 3
    apart = group_id ^ lane_group
    coarse = jnp.broadcast_to(row(4), (groups, HALF))
    for level in range(5, 8):
        coarse = jnp.where(apart >= 1 << (level - 4), row(level), coarse)
    coarse = jnp.where(lane_group > group_id, coarse, 0.0)
    sub = lax.broadcasted_iota(jnp.int32, (GROUP, HALF), 0)
    lane = lax.broadcasted_iota(jnp.int32, (GROUP, HALF), 1)
    low = sub ^ (lane & 7)
    fine = jnp.broadcast_to(row(0), (GROUP, HALF))
    for level in range(1, 4):
        fine = jnp.where(low >= 1 << (level - 1), row(level), fine)
    fine = jnp.where(sub <= (lane & 7), fine, 0.0)
    pieces = []
    for g in range(groups):
        wide = jnp.broadcast_to(coarse[g : g + 1, :], (GROUP, HALF))
        pieces.append(jnp.where(lane >> 3 == g, fine, wide))
    return jnp.concatenate(pieces, axis=0)


def local_kernel(*refs):
    q_ref, k_ref, v_ref, w_ref, local_ref = refs[:5]
    out_ref = refs[-1]
    rows = q_ref.shape[0]
    chunks = rows // CHUNK
    depth_count = chunks.bit_length() - 1
    base_level = CHUNK.bit_length()
    for c in range(chunks):
        start = c * CHUNK
        here = pl.ds(start, CHUNK)
        q = q_ref[here, :]
        depths = [d for d in range(depth_count) if c >> d & 1]
        stream = [k_ref[here, :]] + [
            local_ref[0, bucket_slot(depth_count, d, c)] for d in depths
        ]
        result = dot(jnp.concatenate(stream, axis=0), q, TT)
        upper = (result[:HALF, :HALF] * local_factors(w_ref, start)).astype(jnp.bfloat16)
        lower = (result[HALF:CHUNK, HALF:] * local_factors(w_ref, start + HALF)).astype(
            jnp.bfloat16
        )
        middle_row = w_ref[0, 8:9, start + HALF : start + CHUNK] * SCALING
        middle = (result[:HALF, HALF:] * middle_row).astype(jnp.bfloat16)
        weighted = jnp.concatenate(
            [
                jnp.concatenate([upper, middle], axis=1),
                jnp.concatenate([jnp.zeros_like(upper), lower], axis=1),
            ],
            axis=0,
        )
        total = dot(v_ref[here, :], weighted, LT)
        for i, d in enumerate(depths):
            piece = result[CHUNK + i * VALUE_DIM : CHUNK + (i + 1) * VALUE_DIM]
            level = base_level + d
            total += piece * (w_ref[0, level : level + 1, start : start + CHUNK] * SCALING)
        out_ref[0, :, start : start + CHUNK] = total.astype(out_ref.dtype)


def across_kernel(cross_bits, half_heads, first_level, pos_ref, q_ref, w_ref, in_ref, *refs):
    mix_ref, square_ref = refs[-2:]
    state_refs = refs[: 2 * cross_bits - 1]
    head = pl.program_id(0)
    position = pos_ref[0]
    states = []
    for b in range(cross_bits):
        if b == 0:
            state = state_refs[0][0]
        else:
            own = (head // half_heads) == (position & 1)
            state = jnp.where(own, state_refs[2 * b - 1][0], state_refs[2 * b][0])
        present = (position >> b & 1) == 1
        states.append(jnp.where(present, state, jnp.zeros_like(state)))
    stream = jnp.concatenate(states, axis=0)
    rows = q_ref.shape[0]

    @pl.when(head == 0)
    def _():
        square_ref[...] = jnp.zeros_like(square_ref)

    for start in range(0, rows, CHUNK):
        result = dot(stream, q_ref[start : start + CHUNK, :], TT)
        total = in_ref[0, :, start : start + CHUNK].astype(jnp.float32)
        for b in range(cross_bits):
            level = first_level + b
            total += result[b * VALUE_DIM : (b + 1) * VALUE_DIM] * (
                w_ref[0, level : level + 1, start : start + CHUNK] * SCALING
            )
        square_ref[:, start : start + CHUNK] += jnp.sum(total * total, axis=0, keepdims=True)
        mix_ref[start : start + CHUNK, :] = total.T.astype(mix_ref.dtype)


def norm_kernel(width, mix_ref, gain_ref, square_ref, *refs):
    out_ref = refs[-1]
    rows = mix_ref.shape[0]
    factor = lax.rsqrt(square_ref[...] / width + 1e-05)
    column = jnp.broadcast_to(factor, (GROUP, rows)).T[:, :1]
    out_ref[...] = (mix_ref[...].astype(jnp.float32) * gain_ref[...] * column).astype(
        out_ref.dtype
    )


def body(queries, key_vectors, value_vectors, level_weights, norm_gain):
    rows = queries.shape[0]
    heads = level_weights.shape[0]
    levels = level_weights.shape[1]
    chunks = rows // CHUNK
    depth_count = chunks.bit_length() - 1
    local_bits = rows.bit_length() - 1
    seq_size = lax.axis_size("seq")
    cross_bits = seq_size.bit_length() - 1
    position = lax.axis_index("seq").astype(jnp.int32)
    bf16 = jnp.bfloat16

    head_block = pl.BlockSpec((rows, HEAD_DIM), lambda h: (0, h))
    local_states, block_state = pl.pallas_call(
        state_kernel,
        grid=(heads,),
        in_specs=[head_block, head_block],
        out_specs=[
            pl.BlockSpec((1, chunks - 1, VALUE_DIM, HEAD_DIM), lambda h: (h, 0, 0, 0)),
            pl.BlockSpec((1, VALUE_DIM, HEAD_DIM), lambda h: (h, 0, 0)),
        ],
        out_shape=[
            jax.ShapeDtypeStruct((heads, chunks - 1, VALUE_DIM, HEAD_DIM), bf16),
            jax.ShapeDtypeStruct((heads, VALUE_DIM, HEAD_DIM), bf16),
        ],
        cost_estimate=pl.CostEstimate(
            flops=2 * heads * rows * HEAD_DIM * VALUE_DIM,
            bytes_accessed=4 * rows * heads * HEAD_DIM,
            transcendentals=0,
        ),
        name="states",
    )(key_vectors, value_vectors)

    def swap(array, bit):
        return lax.ppermute(array, "seq", [(i, i ^ (1 << bit)) for i in range(seq_size)])

    half = heads // 2
    buckets = []
    received = swap(block_state, 0)
    buckets.append(received)
    if cross_bits > 1:
        first = (position & 1) * half
        mine = lax.dynamic_slice_in_dim(block_state, first, half, 0)
        pair = lax.dynamic_slice_in_dim(received, first, half, 0)
        running = (mine.astype(jnp.float32) + pair.astype(jnp.float32)).astype(bf16)
        for b in range(1, cross_bits):
            received = swap(running, b)
            buckets += [received, swap(received, 0)]
            running = (running.astype(jnp.float32) + received.astype(jnp.float32)).astype(bf16)

    part = heads // B_PARTS
    inside = None
    for p in range(B_PARTS):
        block = pl.BlockSpec((rows, HEAD_DIM), lambda h, p=p: (0, h + p * part))
        operands = [queries, key_vectors, value_vectors, level_weights, local_states]
        in_specs = [
            block,
            block,
            block,
            pl.BlockSpec((1, levels, rows), lambda h, p=p: (h + p * part, 0, 0)),
            pl.BlockSpec(
                (1, chunks - 1, VALUE_DIM, HEAD_DIM), lambda h, p=p: (h + p * part, 0, 0, 0)
            ),
        ]
        aliases = {}
        if inside is not None:
            operands.append(inside)
            in_specs.append(pl.BlockSpec(memory_space=pl.ANY))
            aliases = {5: 0}
        inside = pl.pallas_call(
            local_kernel,
            grid=(part,),
            in_specs=in_specs,
            out_specs=pl.BlockSpec((1, VALUE_DIM, rows), lambda h, p=p: (h + p * part, 0, 0)),
            out_shape=jax.ShapeDtypeStruct((heads, VALUE_DIM, rows), bf16),
            input_output_aliases=aliases,
            cost_estimate=pl.CostEstimate(
                flops=part * rows * HEAD_DIM * 16 * 256,
                bytes_accessed=8 * rows * part * HEAD_DIM,
                transcendentals=0,
            ),
            name="local",
        )(*operands)

    span = rows // C_PARTS
    first_level = local_bits + 1
    low = first_level // 8 * 8
    count = 8 if (first_level + cross_bits - 1) // 8 * 8 == low else levels
    level_block = low // 8 if count == 8 else 0
    first_level = first_level - low if count == 8 else first_level
    mixes, squares = [], []
    for p in range(C_PARTS):
        operands = [position.reshape(1), queries, level_weights, inside] + buckets
        in_specs = [
            pl.BlockSpec(memory_space=pltpu.SMEM),
            pl.BlockSpec((span, HEAD_DIM), lambda h, p=p: (p, h)),
            pl.BlockSpec((1, count, span), lambda h, p=p: (h, level_block, p)),
            pl.BlockSpec((1, VALUE_DIM, span), lambda h, p=p: (h, 0, p)),
            pl.BlockSpec((1, VALUE_DIM, HEAD_DIM), lambda h: (h, 0, 0)),
        ] + [pl.BlockSpec((1, VALUE_DIM, HEAD_DIM), lambda h: (h % half, 0, 0))] * (
            2 * cross_bits - 2
        )
        mix, square = pl.pallas_call(
            functools.partial(across_kernel, cross_bits, half, first_level),
            grid=(heads,),
            in_specs=in_specs,
            out_specs=[
                pl.BlockSpec((span, VALUE_DIM), lambda h: (0, h)),
                pl.BlockSpec((1, span), lambda h: (0, 0)),
            ],
            out_shape=[
                jax.ShapeDtypeStruct((span, heads * VALUE_DIM), bf16),
                jax.ShapeDtypeStruct((1, span), jnp.float32),
            ],
            cost_estimate=pl.CostEstimate(
                flops=heads * span * HEAD_DIM * 2 * 128 * cross_bits * 4,
                bytes_accessed=6 * span * heads * HEAD_DIM,
                transcendentals=0,
            ),
            name="across",
        )(*operands)
        mixes.append(mix)
        squares.append(lax.psum(square, "head"))

    out = None
    step = 256
    width = HEADS * VALUE_DIM
    gain = norm_gain.reshape(1, -1)
    columns = heads * VALUE_DIM
    for p in range(C_PARTS):
        operands = [mixes[p], gain, squares[p]]
        in_specs = [
            pl.BlockSpec((step, columns), lambda i: (i, 0)),
            pl.BlockSpec((1, columns), lambda i: (0, 0)),
            pl.BlockSpec((1, step), lambda i: (0, i)),
        ]
        aliases = {}
        if out is not None:
            operands.append(out)
            in_specs.append(pl.BlockSpec(memory_space=pl.ANY))
            aliases = {3: 0}
        out = pl.pallas_call(
            functools.partial(norm_kernel, width),
            grid=(span // step,),
            in_specs=in_specs,
            out_specs=pl.BlockSpec((step, columns), lambda i, p=p: (i + p * (span // step), 0)),
            out_shape=jax.ShapeDtypeStruct((rows, columns), bf16),
            input_output_aliases=aliases,
            cost_estimate=pl.CostEstimate(
                flops=3 * span * columns, bytes_accessed=4 * span * columns, transcendentals=0
            ),
            name="norm",
        )(*operands)
    return out


def solution(mesh):
    placed = (
        P("seq", "head"),
        P("seq", "head"),
        P("seq", "head"),
        P("head", None, "seq"),
        P("head"),
    )
    return jax.shard_map(
        body, mesh=mesh, in_specs=placed, out_specs=P("seq", "head"), check_vma=False
    )
```

time: 565 us -> 115 us (0.20); the launches traced: 555 us -> 113 us
  matrix products: 303 us -> 0 us
  local copies, waits for them, and re-layouts: 146 us -> 0.8 us
  Pallas kernels: 0 us -> 94.6 us
  other arithmetic: 77.8 us -> 0.15 us
  between operations: 14.9 us -> 0.1 us
    dot_general x11 -> x0, matrix products: 303 us -> none  [the longest x4 215 us: body(): jnp.einsum('thd,shd->hts', query_rows[start_row:end_row], key_rows[:end_r...]
    pallas_call x0 -> x9, Pallas kernels: none -> 94.6 us  [the longest x4 38.6 us: body(): pl.pallas_call(local_kernel, grid=(part,), in_specs=in_specs, out_specs=p...]
    unnamed x163 -> x14, local copies, waits for them, and re-layouts: 53.7 us -> 0.8 us
    le x4 -> x0, other arithmetic: 35.5 us -> none  [body(): causal = (col_ids[None, :] <= row_ids[:, None])[None]]
    slice x12 -> x0, local copies, waits for them, and re-layouts: 31.5 us -> none  [the longest x3 12.5 us: body(): value_rows[:end_row]]
    reduce_sum x1 -> x0, other arithmetic: 25.7 us -> none  [body(): square = jnp.sum(mixture * mixture, axis=1)]
    broadcast_in_dim x24 -> x0, local copies, waits for them, and re-layouts: 18.2 us -> none  [body(): jnp.where(levels[None] == depth_id, level_weights[:, depth_id, start_row:...]
    transpose x1 -> x0, local copies, waits for them, and re-layouts: 17.7 us -> none  [body(): (inside + across).transpose(1, 0, 2)]
  transfers between devices with their start and end apart: 1 -> 5, of which waited for: 0 -> 0; matrix products, arithmetic and copies ran while one was open for 74% -> 0% of each run, Pallas kernels for 0% -> 34%
where the time goes in v1:
time: 115 us; the launch traced here: 113 us
  Pallas kernels  94.6 us (82%)
  blocking collectives  12.7 us (11%)
  starting transfers between devices  5.1 us (4%)
    pallas_call x4, Pallas kernels, body(): pl.pallas_call(local_kernel, grid=(part,), in_specs=in_specs, out_specs=p...  38.6 us
    pallas_call x2, Pallas kernels, body(): pl.pallas_call(functools.partial(across_kernel, cross_bits, half, first_l...  30.2 us
    pallas_call x1, Pallas kernels, body(): pl.pallas_call(state_kernel, grid=(heads,), in_specs=[head_block, head_bl...  15.1 us
    psum x1, blocking collectives, body(): squares.append(lax.psum(square, 'head'))  12.7 us
    pallas_call x2, Pallas kernels, body(): pl.pallas_call(functools.partial(norm_kernel, width), grid=(span // step,...  10.7 us
    ppermute x5, starting transfers between devices, swap(): lax.ppermute(array, 'seq', [(i, i ^ 1 << bit) for i in range(seq_size)])  5.1 us
  transfers between devices with their start and end apart: 5, of which 0 were waited for; matrix products, arithmetic and copies ran while one was open for 0% of the time, Pallas kernels for 34%

profile of v1, /device:TPU:0, one launch (start us, length us, event | category | flops | bytes accessed | tf_op | source)
XLA Modules:
  0.0 113.5 jit_solution(6790097780309156295)
XLA Ops:
  0.0 15.1 %states.1 = (bf16[16,7,128,128]{3,2,1,0:T(8,128)(2,1)}, bf16[16,128,128]{2,1,0:T(8,128)(2,1)}) custom-call(bf16[2048,2048]{1,0:T(8,128)(2,1)} %refs_1_.7, bf16[2048,2048]{1,0:T(8,128)(2,1)} %refs_2_.7), custom_call_target="tpu_custom_call" | custom-call | flops 1073741824 | bytes 16777216 | tf_op jit(solution)/shard_map/states/pallas_call | solution.py:170
  15.1 0.4 collective-permute-start
  15.6 0.0 copy-start.2
  15.6 9.7 %local.4.refs_5_ = bf16[16,128,2048]{2,1,0:T(8,128)(2,1)} custom-call(bf16[2048,2048]{1,0:T(8,128)(2,1)} %q_ref.3, bf16[2048,2048]{1,0:T(8,128)(2,1)} %refs_1_.7, bf16[2048,2048]{1,0:T(8,128)(2,1)} %refs_2_.7, f32[16,16,2048]{2,1,0:T(8,128)} %w_ref.3, bf16[16,7,128,128]{3,2,1,0:T(8,128)(2,1)} %get-tuple-element.11.refs_4_), custom_call_target="tpu_custom_call" | custom-call | flops 4294967296 | bytes 8388608 | tf_op jit(solution)/shard_map/local/pallas_call | solution.py:226
  25.3 0.0 collective-permute-done.refs_0_
  25.3 0.0 copy-done.2
  25.3 0.0 copy-start.1
  25.3 0.1 add_convert_fusion.1
  25.4 2.6 %collective-permute-start.1 = (bf16[8,128,128]{2,1,0:T(8,128)(2,1)S(1)}, bf16[8,128,128]{2,1,0:T(8,128)(2,1)S(1)}, u32[]{:S(2)}, u32[]{:S(2)}) collective-permute-start(bf16[8,128,128]{2,1,0:T(8,128)(2,1)S(1)} %add_convert_fusion.1), channel_id=1, source_target_pairs={{0,8},{4,12},{8,0},{12,4},{16,24},{20,28},{24,16},{28,20},{1,9},{5... | collective-permute-start | bytes 786440 | tf_op jit(solution)/shard_map/ppermute | solution.py:191
  28.0 9.6 %local.5.refs_5_ = bf16[16,128,2048]{2,1,0:T(8,128)(2,1)} custom-call(bf16[2048,2048]{1,0:T(8,128)(2,1)} %q_ref.3, bf16[2048,2048]{1,0:T(8,128)(2,1)} %refs_1_.7, bf16[2048,2048]{1,0:T(8,128)(2,1)} %refs_2_.7, f32[16,16,2048]{2,1,0:T(8,128)} %w_ref.3, bf16[16,7,128,128]{3,2,1,0:T(8,128)(2,1)} %get-tuple-element.11.refs_4_, ...), custom_call_target="tpu_custom_call", output_to_operand_aliasing={{}: (5, {})} | custom-call | flops 4294967296 | bytes 8388608 | tf_op jit(solution)/shard_map/local/pallas_call | solution.py:226
  37.6 0.0 copy-done.1
  37.6 0.0 collective-permute-done.1.refs_1_
  37.6 0.0 copy-start
  37.6 0.1 add_convert_fusion
  37.7 1.6 %collective-permute-start.3 = (bf16[8,128,128]{2,1,0:T(8,128)(2,1)S(1)}, bf16[8,128,128]{2,1,0:T(8,128)(2,1)S(1)}, u32[]{:S(2)}, u32[]{:S(2)}) collective-permute-start(bf16[8,128,128]{2,1,0:T(8,128)(2,1)S(1)} %add_convert_fusion), channel_id=1, source_target_pairs={{0,16},{4,20},{8,24},{12,28},{16,0},{20,4},{24,8},{28,12},{1,17},{... | collective-permute-start | bytes 786440 | tf_op jit(solution)/shard_map/ppermute | solution.py:191
  39.3 9.6 %local.6.refs_5_ = bf16[16,128,2048]{2,1,0:T(8,128)(2,1)} custom-call(bf16[2048,2048]{1,0:T(8,128)(2,1)} %q_ref.3, bf16[2048,2048]{1,0:T(8,128)(2,1)} %refs_1_.7, bf16[2048,2048]{1,0:T(8,128)(2,1)} %refs_2_.7, f32[16,16,2048]{2,1,0:T(8,128)} %w_ref.3, bf16[16,7,128,128]{3,2,1,0:T(8,128)(2,1)} %get-tuple-element.11.refs_4_, ...), custom_call_target="tpu_custom_call", output_to_operand_aliasing={{}: (5, {})} | custom-call | flops 4294967296 | bytes 8388608 | tf_op jit(solution)/shard_map/local/pallas_call | solution.py:226
  48.9 0.0 copy-done
  48.9 0.0 collective-permute-start.2
  48.9 0.0 collective-permute-done.3.refs_3_
  48.9 0.0 copy-start.4
  49.0 0.5 collective-permute-start.4
  49.4 9.6 %local.7.in_ref = bf16[16,128,2048]{2,1,0:T(8,128)(2,1)} custom-call(bf16[2048,2048]{1,0:T(8,128)(2,1)} %q_ref.3, bf16[2048,2048]{1,0:T(8,128)(2,1)} %refs_1_.7, bf16[2048,2048]{1,0:T(8,128)(2,1)} %refs_2_.7, f32[16,16,2048]{2,1,0:T(8,128)} %w_ref.3, bf16[16,7,128,128]{3,2,1,0:T(8,128)(2,1)} %get-tuple-element.11.refs_4_, ...), custom_call_target="tpu_custom_call", output_to_operand_aliasing={{}: (5, {})} | custom-call | flops 4294967296 | bytes 8388608 | tf_op jit(solution)/shard_map/local/pallas_call | solution.py:226
  59.1 0.0 copy-done.4
  59.1 0.0 collective-permute-done.2.refs_2_
  59.1 0.0 copy-start.5
  59.1 0.0 collective-permute-done.4.refs_4_
  59.1 0.0 copy-start.6
  59.1 0.7 copy-done.5
  59.8 0.1 copy-done.6
  59.9 15.1 %across.2 = (bf16[1024,2048]{1,0:T(8,128)(2,1)}, f32[1,1024]{1,0:T(1,128)}) custom-call(s32[1]{0:T(128)} %bitcast.pos_ref, bf16[2048,2048]{1,0:T(8,128)(2,1)} %q_ref.3, f32[16,16,2048]{2,1,0:T(8,128)} %w_ref.3, bf16[16,128,2048]{2,1,0:T(8,128)(2,1)} %local.7.in_ref, bf16[16,128,128]{2,1,0:T(8,128)(2,1)} %copy-done.1, bf16[8,128,128]{2,1,0:T(8,128)(2,1)} %copy-done, ...), custom_call_target="tpu_custom_call" | custom-call | flops 6442450944 | bytes 12582912 | tf_op jit(solution)/shard_map/across/pallas_call | solution.py:259
  75.0 0.0 copy-start.3
  75.0 15.1 %across.3 = (bf16[1024,2048]{1,0:T(8,128)(2,1)}, f32[1,1024]{1,0:T(1,128)}) custom-call(s32[1]{0:T(128)} %bitcast.pos_ref, bf16[2048,2048]{1,0:T(8,128)(2,1)} %q_ref.3, f32[16,16,2048]{2,1,0:T(8,128)} %w_ref.3, bf16[16,128,2048]{2,1,0:T(8,128)(2,1)} %local.7.in_ref, bf16[16,128,128]{2,1,0:T(8,128)(2,1)} %copy-done.1, bf16[8,128,128]{2,1,0:T(8,128)(2,1)} %copy-done, ...), custom_call_target="tpu_custom_call" | custom-call | flops 6442450944 | bytes 12582912 | tf_op jit(solution)/shard_map/across/pallas_call | solution.py:259
  90.1 0.0 copy-done.3
  90.1 12.7 %all-reduce = (f32[1,1024]{1,0:T(1,128)}, f32[1,1024]{1,0:T(1,128)}) all-reduce(f32[1,1024]{1,0:T(1,128)S(1)} %copy-done.3, f32[1,1024]{1,0:T(1,128)} %get-tuple-element.16), channel_id=1, replica_groups=mesh['seq'=8,'head'=4] {'head'}, use_global_device_ids=true, to_apply=%region_0.0 | all-reduce | flops 2048 | bytes 16384 | tf_op jit(solution)/shard_map/psum | solution.py:279
  102.8 5.3 %norm.2.refs_0_ = bf16[2048,2048]{1,0:T(8,128)(2,1)} custom-call(bf16[1024,2048]{1,0:T(8,128)(2,1)} %get-tuple-element.15.mix_ref, f32[1,2048]{1,0:T(1,128)} %bitcast.2, f32[1,1024]{1,0:T(1,128)} %get-tuple-element.18.square_ref), custom_call_target="tpu_custom_call" | custom-call | flops 6291456 | bytes 8388608 | tf_op jit(solution)/shard_map/norm/pallas_call | solution.py:298
  108.2 5.3 %norm.3 = bf16[2048,2048]{1,0:T(8,128)(2,1)} custom-call(bf16[1024,2048]{1,0:T(8,128)(2,1)} %get-tuple-element.13.mix_ref, f32[1,2048]{1,0:T(1,128)} %bitcast.3, f32[1,1024]{1,0:T(1,128)} %get-tuple-element.17.square_ref, bf16[2048,2048]{1,0:T(8,128)(2,1)} %norm.2.refs_0_), custom_call_target="tpu_custom_call", output_to_operand_aliasing={{}: (3, {})} | custom-call | flops 6291456 | bytes 8388608 | tf_op jit(solution)/shard_map/norm/pallas_call | solution.py:298
Async XLA Ops:
  15.1 10.1 %collective-permute-start = (bf16[16,128,128]{2,1,0:T(8,128)(2,1)}, bf16[16,128,128]{2,1,0:T(8,128)(2,1)S(1)}, u32[]{:S(2)}, u32[]{:S(2)}) collective-permute-start(bf16[16,128,128]{2,1,0:T(8,128)(2,1)} %get-tuple-element.12), channel_id=1, source_target_pairs={{0,4},{4,0},{8,12},{12,8},{16,20},{20,16},{24,28},{28,24},{1,5},{5... | collective-permute-start | bytes 1572872 | tf_op jit(solution)/shard_map/ppermute | solution.py:191
  15.6 9.7 %copy-start.2 = (bf16[16,128,128]{2,1,0:T(8,128)(2,1)S(1)}, bf16[16,128,128]{2,1,0:T(8,128)(2,1)}, u32[]{:S(2)}) copy-start(bf16[16,128,128]{2,1,0:T(8,128)(2,1)} %get-tuple-element.12) | copy-start | bytes 1572868
  25.3 12.3 %copy-start.1 = (bf16[16,128,128]{2,1,0:T(8,128)(2,1)}, bf16[16,128,128]{2,1,0:T(8,128)(2,1)S(1)}, u32[]{:S(2)}) copy-start(bf16[16,128,128]{2,1,0:T(8,128)(2,1)S(1)} %collective-permute-done.refs_0_) | copy-start | bytes 1572868
  25.4 12.2 %collective-permute-start.1 = (bf16[8,128,128]{2,1,0:T(8,128)(2,1)S(1)}, bf16[8,128,128]{2,1,0:T(8,128)(2,1)S(1)}, u32[]{:S(2)}, u32[]{:S(2)}) collective-permute-start(bf16[8,128,128]{2,1,0:T(8,128)(2,1)S(1)} %add_convert_fusion.1), channel_id=1, source_target_pairs={{0,8},{4,12},{8,0},{12,4},{16,24},{20,28},{24,16},{28,20},{1,9},{5... | collective-permute-start | bytes 786440 | tf_op jit(solution)/shard_map/ppermute | solution.py:191
  37.6 11.3 %copy-start = (bf16[8,128,128]{2,1,0:T(8,128)(2,1)}, bf16[8,128,128]{2,1,0:T(8,128)(2,1)S(1)}, u32[]{:S(2)}) copy-start(bf16[8,128,128]{2,1,0:T(8,128)(2,1)S(1)} %collective-permute-done.1.refs_1_) | copy-start | bytes 786436
  37.7 11.2 %collective-permute-start.3 = (bf16[8,128,128]{2,1,0:T(8,128)(2,1)S(1)}, bf16[8,128,128]{2,1,0:T(8,128)(2,1)S(1)}, u32[]{:S(2)}, u32[]{:S(2)}) collective-permute-start(bf16[8,128,128]{2,1,0:T(8,128)(2,1)S(1)} %add_convert_fusion), channel_id=1, source_target_pairs={{0,16},{4,20},{8,24},{12,28},{16,0},{20,4},{24,8},{28,12},{1,17},{... | collective-permute-start | bytes 786440 | tf_op jit(solution)/shard_map/ppermute | solution.py:191
  48.9 10.2 %collective-permute-start.2 = (bf16[8,128,128]{2,1,0:T(8,128)(2,1)S(1)}, bf16[8,128,128]{2,1,0:T(8,128)(2,1)S(1)}, u32[]{:S(2)}, u32[]{:S(2)}) collective-permute-start(bf16[8,128,128]{2,1,0:T(8,128)(2,1)S(1)} %collective-permute-done.1.refs_1_), channel_id=1, source_target_pairs={{0,4},{4,0},{8,12},{12,8},{16,20},{20,16},{24,28},{28,24},{1,5},{5... | collective-permute-start | bytes 786440 | tf_op jit(solution)/shard_map/ppermute | solution.py:191
  48.9 10.1 %copy-start.4 = (bf16[8,128,128]{2,1,0:T(8,128)(2,1)}, bf16[8,128,128]{2,1,0:T(8,128)(2,1)S(1)}, u32[]{:S(2)}) copy-start(bf16[8,128,128]{2,1,0:T(8,128)(2,1)S(1)} %collective-permute-done.3.refs_3_) | copy-start | bytes 786436
  49.0 10.1 %collective-permute-start.4 = (bf16[8,128,128]{2,1,0:T(8,128)(2,1)S(1)}, bf16[8,128,128]{2,1,0:T(8,128)(2,1)S(1)}, u32[]{:S(2)}, u32[]{:S(2)}) collective-permute-start(bf16[8,128,128]{2,1,0:T(8,128)(2,1)S(1)} %collective-permute-done.3.refs_3_), channel_id=1, source_target_pairs={{0,4},{4,0},{8,12},{12,8},{16,20},{20,16},{24,28},{28,24},{1,5},{5... | collective-permute-start | bytes 786440 | tf_op jit(solution)/shard_map/ppermute | solution.py:191
  59.1 0.7 copy-start.5
  59.1 0.8 copy-start.6
  75.0 15.1 %copy-start.3 = (f32[1,1024]{1,0:T(1,128)S(1)}, f32[1,1024]{1,0:T(1,128)}, u32[]{:S(2)}) copy-start(f32[1,1024]{1,0:T(1,128)} %get-tuple-element.14) | copy-start | bytes 12292

commit v2 on v0

v2 whole, which is shorter than its diff:
```python
import functools

import jax
import jax.numpy as jnp
from jax import lax
from jax.experimental import pallas as pl
from jax.experimental.pallas import tpu as pltpu
from jax.sharding import PartitionSpec as P

HEADS = 64
HEAD_DIM = 128
VALUE_DIM = 128
CHUNK = 256
HALF = 128
GROUP = 8
SCALING = HEAD_DIM ** (-0.5)
MIB = 1 << 20
BF16 = jnp.bfloat16

TT = (((1,), (1,)), ((), ()))
LT = (((0,), (0,)), ((), ()))

WHOLE = pl.BlockSpec(memory_space=pltpu.VMEM)
ANYWHERE = pl.BlockSpec(memory_space=pl.ANY)


def dot(a, b, dims):
    return lax.dot_general(a, b, dims, preferred_element_type=jnp.float32)


def keep(array):
    return pltpu.with_memory_space_constraint(array, pltpu.VMEM)


def leave(array):
    return pltpu.with_memory_space_constraint(array, pltpu.HBM)


def columns_of(head):
    if isinstance(head, int):
        return slice(head * HEAD_DIM, (head + 1) * HEAD_DIM)
    return pl.ds(pl.multiple_of(head * HEAD_DIM, HEAD_DIM), HEAD_DIM)


def rows_of(chunk):
    return slice(chunk * CHUNK, (chunk + 1) * CHUNK)


def bucket_slot(depth_count, depth, chunk):
    before = sum(1 << (depth_count - d - 1) for d in range(depth))
    return before + (((chunk >> depth) - 1) >> 1)


def state_kernel(
    span, pos_ref, k_hbm, v_hbm, q_hbm, w_hbm,
    k_ref, v_ref, local_ref, block_ref, q_ref, w_ref, held, sems, more_sems,
):
    del pos_ref
    rows = k_ref.shape[0]
    heads = block_ref.shape[0]
    chunks = rows // CHUNK
    depth_count = chunks.bit_length() - 1
    copies = []
    for c in range(chunks):
        here = pl.ds(c * CHUNK, CHUNK)
        pair = [
            pltpu.make_async_copy(k_hbm.at[here], k_ref.at[here], sems.at[0, c]),
            pltpu.make_async_copy(v_hbm.at[here], v_ref.at[here], sems.at[1, c]),
        ]
        for copy in pair:
            copy.start()
        copies.append(pair)
    more = weight_copies(span, q_hbm, w_hbm, q_ref, w_ref, more_sems)
    for c in range(chunks):
        for copy in copies[c]:
            copy.wait()
        if c == chunks // 2:
            for copy in more:
                copy.start()
        for h in range(heads):
            state = dot(v_ref[rows_of(c), columns_of(h)], k_ref[rows_of(c), columns_of(h)], LT)
            depth = 0
            while c >> depth & 1:
                state += held[depth, h]
                depth += 1
            if depth < depth_count:
                held[depth, h] = state
                slot = bucket_slot(depth_count, depth, c | (1 << depth))
                local_ref[h, slot] = state.astype(BF16)
            else:
                block_ref[h] = state.astype(BF16)
    for copy in more:
        copy.wait()


def weight_copies(span, q_hbm, w_hbm, q_ref, w_ref, sems):
    here = pl.ds(span[0] * CHUNK, (span[1] - span[0]) * CHUNK)
    return [
        pltpu.make_async_copy(w_hbm.at[:, :, here], w_ref, sems.at[0]),
        pltpu.make_async_copy(q_hbm.at[here], q_ref, sems.at[1]),
    ]


def sum_kernel(whole, pos_ref, mine_ref, received_ref, out_ref):
    half = out_ref.shape[0]
    here = pl.ds((pos_ref[0] & 1) * half if whole else 0, half)
    total = mine_ref[here].astype(jnp.float32) + received_ref[here].astype(jnp.float32)
    out_ref[...] = total.astype(BF16)


def local_factors(w_ref, head, start):
    def row(level):
        return w_ref[head, level : level + 1, start : start + HALF] * SCALING

    groups = HALF // GROUP
    group_id = lax.broadcasted_iota(jnp.int32, (groups, HALF), 0)
    lane_group = lax.broadcasted_iota(jnp.int32, (groups, HALF), 1) >> 3
    apart = group_id ^ lane_group
    coarse = jnp.broadcast_to(row(4), (groups, HALF))
    for level in range(5, 8):
        coarse = jnp.where(apart >= 1 << (level - 4), row(level), coarse)
    coarse = jnp.where(lane_group > group_id, coarse, 0.0)
    sub = lax.broadcasted_iota(jnp.int32, (GROUP, HALF), 0)
    lane = lax.broadcasted_iota(jnp.int32, (GROUP, HALF), 1)
    low = sub ^ (lane & 7)
    fine = jnp.broadcast_to(row(0), (GROUP, HALF))
    for level in range(1, 4):
        fine = jnp.where(low >= 1 << (level - 1), row(level), fine)
    fine = jnp.where(sub <= (lane & 7), fine, 0.0)
    pieces = []
    for g in range(groups):
        wide = jnp.broadcast_to(coarse[g : g + 1, :], (GROUP, HALF))
        pieces.append(jnp.where(lane >> 3 == g, fine, wide))
    return jnp.concatenate(pieces, axis=0)


def local_kernel(span, after, lag, first_level, pos_ref, q_ref, k_ref, v_ref, w_ref, local_ref, *refs):
    refs = list(refs)
    heads = w_ref.shape[0]
    depth_count = (k_ref.shape[0] // CHUNK).bit_length() - 1
    base_level = CHUNK.bit_length()
    received_ref = refs.pop(0) if first_level is not None else None
    copies = []
    if after is not None:
        q_hbm, w_hbm, out_ref, q_next, w_next, sems = refs
        copies = weight_copies(after, q_hbm, w_hbm, q_next, w_next, sems)
        for copy in copies:
            copy.start()
    else:
        (out_ref,) = refs
    present = (pos_ref[0] & 1) == 1

    def scores(c, h):
        start = (c - span[0]) * CHUNK
        depths = [d for d in range(depth_count) if c >> d & 1]
        stream = [k_ref[rows_of(c), columns_of(h)]]
        stream += [local_ref[h, bucket_slot(depth_count, d, c)] for d in depths]
        levels = [base_level + d for d in depths]
        if received_ref is not None:
            state = received_ref[h]
            stream.append(jnp.where(present, state, jnp.zeros_like(state)))
            levels.append(first_level)
        result = dot(
            jnp.concatenate(stream, axis=0), q_ref[rows_of(c - span[0]), columns_of(h)], TT
        )
        upper = (result[:HALF, :HALF] * local_factors(w_ref, h, start)).astype(BF16)
        lower = (result[HALF:CHUNK, HALF:] * local_factors(w_ref, h, start + HALF)).astype(BF16)
        middle_row = w_ref[h, 8:9, start + HALF : start + CHUNK] * SCALING
        middle = (result[:HALF, HALF:] * middle_row).astype(BF16)
        weighted = jnp.concatenate(
            [
                jnp.concatenate([upper, middle], axis=1),
                jnp.concatenate([jnp.zeros_like(upper), lower], axis=1),
            ],
            axis=0,
        )
        total = None
        for i, level in enumerate(levels):
            piece = result[CHUNK + i * VALUE_DIM : CHUNK + (i + 1) * VALUE_DIM]
            piece = piece * (w_ref[h, level : level + 1, start : start + CHUNK] * SCALING)
            total = piece if total is None else total + piece
        return weighted, total

    def values(c, h, weighted, total):
        inside = dot(v_ref[rows_of(c), columns_of(h)], weighted, LT)
        if total is not None:
            inside += total
        out_ref[c - span[0], columns_of(h), :] = inside.astype(BF16)

    waiting = []
    for c in range(*span):
        for h in range(heads):
            waiting.append((c, h, *scores(c, h)))
            if len(waiting) > lag:
                values(*waiting.pop(0))
    for entry in waiting:
        values(*entry)
    for copy in copies:
        copy.wait()


def across_kernel(mine, bits, first_level, spans, part, pos_ref, *refs):
    refs = list(refs)
    q_refs = [refs.pop(0) for _ in spans]
    w_refs = [refs.pop(0) for _ in spans]
    in_refs = [refs.pop(0) for _ in spans]
    state_refs = [refs.pop(0) for _ in range(bits)]
    mix_ref, square_ref = refs[-2:]
    half = w_refs[0].shape[0] // 2
    position = pos_ref[0]
    own = (position & 1) * half
    first = own if mine else half - own
    squares = {}
    for i in range(half):
        head = first + i
        states = []
        for b in range(bits):
            state = state_refs[b][head if b == 0 else i]
            states.append(jnp.where((position >> b & 1) == 1, state, jnp.zeros_like(state)))
        for c in range(*part):
            s = [low <= c < high for low, high in spans].index(True)
            local = c - spans[s][0]
            start = local * CHUNK
            used = range(0 if s == 0 else 1, bits)
            total = in_refs[s][local, columns_of(head), :].astype(jnp.float32)
            if len(used):
                stream = jnp.concatenate([states[b] for b in used], axis=0)
                result = dot(stream, q_refs[s][rows_of(local), columns_of(head)], TT)
                for n, b in enumerate(used):
                    level = first_level + b
                    row = w_refs[s][head, level : level + 1, start : start + CHUNK] * SCALING
                    total += result[n * VALUE_DIM : (n + 1) * VALUE_DIM] * row
            square = jnp.sum((total * total).reshape(VALUE_DIM // GROUP, GROUP, CHUNK), axis=0)
            squares[c] = squares[c] + square if c in squares else square
            mix_ref[rows_of(c - part[0]), columns_of(i)] = total.astype(BF16).T
    for c in range(*part):
        here = rows_of(c - part[0])
        square = jnp.sum(squares[c], axis=0, keepdims=True)
        if not mine:
            square += refs[0][:, rows_of(c)]
        square_ref[:, here] = square


def norm_kernel(width, step, low, pos_ref, own_ref, other_ref, gain_ref, square_ref, *refs):
    out_ref = refs[-1]
    i = pl.program_id(0)
    half = own_ref.shape[1]
    own = (pos_ref[0] & 1) * half
    factor = lax.rsqrt(square_ref[...] / width + 1e-05)
    column = jnp.broadcast_to(factor, (GROUP, step)).T[:, :1]
    for mix_ref, at, first in ((own_ref, low + i, own), (other_ref, i, half - own)):
        here = pl.ds(pl.multiple_of(at * step, step), step)
        there = pl.ds(pl.multiple_of(first, HEAD_DIM), half)
        mixture = mix_ref[here, :].astype(jnp.float32)
        out_ref[:, there] = (mixture * gain_ref[:, there] * column).astype(out_ref.dtype)


def body(queries, key_vectors, value_vectors, level_weights, norm_gain):
    rows, columns = queries.shape
    heads = level_weights.shape[0]
    levels = level_weights.shape[1]
    half = heads // 2
    chunks = rows // CHUNK
    depth_count = chunks.bit_length() - 1
    first_level = rows.bit_length()
    seq_size = lax.axis_size("seq")
    head_size = lax.axis_size("head")
    cross_bits = seq_size.bit_length() - 1
    position = lax.axis_index("seq").astype(jnp.int32).reshape(1)
    scalar = pl.BlockSpec(memory_space=pltpu.SMEM)

    def call(kernel, name, operands, out_shape, flops=0, size=0, limit=8, in_specs=None, **settings):
        if in_specs is None:
            in_specs = [scalar] + [WHOLE] * (len(operands) - 1)
        if "out_specs" not in settings:
            settings["out_specs"] = jax.tree.map(lambda _: WHOLE, out_shape)
        return pl.pallas_call(
            kernel,
            name=name,
            in_specs=in_specs,
            out_shape=out_shape,
            compiler_params=pltpu.CompilerParams(vmem_limit_bytes=limit * MIB),
            cost_estimate=pl.CostEstimate(
                flops=int(flops), bytes_accessed=int(size), transcendentals=0
            ),
            **settings,
        )(*operands)

    cuts = sorted({0, chunks // 4, chunks * 7 // 8, chunks})
    spans = list(zip(cuts[:-1], cuts[1:]))

    def weight_shapes(span):
        count = (span[1] - span[0]) * CHUNK
        return [
            pltpu.VMEM((count, columns), BF16),
            pltpu.VMEM((heads, levels, count), jnp.float32),
        ]

    per_chunk = 2 * heads * CHUNK * 128 * 128
    queries, level_weights = leave(queries), leave(level_weights)
    keys, values, local_states, block_state, query, weight = call(
        functools.partial(state_kernel, spans[0]),
        "states",
        [position, leave(key_vectors), leave(value_vectors), queries, level_weights],
        [
            pltpu.VMEM((rows, columns), BF16),
            pltpu.VMEM((rows, columns), BF16),
            pltpu.VMEM((heads, chunks - 1, VALUE_DIM, HEAD_DIM), BF16),
            jax.ShapeDtypeStruct((heads, VALUE_DIM, HEAD_DIM), BF16),
        ]
        + weight_shapes(spans[0]),
        flops=chunks * per_chunk,
        size=4 * rows * columns,
        in_specs=[scalar] + [ANYWHERE] * 4,
        scratch_shapes=[
            pltpu.VMEM((depth_count, heads, VALUE_DIM, HEAD_DIM), jnp.float32),
            pltpu.SemaphoreType.DMA((2, chunks)),
            pltpu.SemaphoreType.DMA((2,)),
        ],
    )
    keys, values, local_states = keep(keys), keep(values), keep(local_states)

    def swap(array, bit):
        return lax.ppermute(array, "seq", [(i, i ^ (1 << bit)) for i in range(seq_size)])

    def add(mine, received, whole):
        return call(
            functools.partial(sum_kernel, whole),
            "sum",
            [position, mine, received],
            jax.ShapeDtypeStruct((half, VALUE_DIM, HEAD_DIM), BF16),
            limit=4,
        )

    received = swap(block_state, 0)
    own_buckets, other_buckets = [received], [received]
    running = add(block_state, received, True)
    for b in range(1, cross_bits):
        received = swap(running, b)
        own_buckets.append(received)
        other_buckets.append(swap(received, 0))
        if b + 1 < cross_bits:
            running = add(running, received, False)

    insides, query_parts, weight_parts = [], [], []
    for p, span in enumerate(spans):
        count = span[1] - span[0]
        after = spans[p + 1] if p + 1 < len(spans) else None
        query, weight = keep(query), keep(weight)
        query_parts.append(query)
        weight_parts.append(weight)
        operands = [position, query, keys, values, weight, local_states]
        if p > 0:
            operands.append(own_buckets[0])
        in_specs = [scalar] + [WHOLE] * (len(operands) - 1)
        out_shape = [pltpu.VMEM((count, columns, CHUNK), BF16)]
        scratch = []
        if after is not None:
            operands += [queries, level_weights]
            in_specs += [ANYWHERE] * 2
            out_shape += weight_shapes(after)
            scratch = [pltpu.SemaphoreType.DMA((2,))]
        results = call(
            functools.partial(local_kernel, span, after, 2, first_level if p else None),
            "local",
            operands,
            out_shape,
            flops=count * per_chunk * 18,
            in_specs=in_specs,
            scratch_shapes=scratch,
        )
        insides.append(keep(results[0]))
        if after is not None:
            query, weight = results[1:]

    shared = [position, *query_parts, *weight_parts, *insides]
    own_mix, own_square = call(
        functools.partial(across_kernel, True, cross_bits, first_level, spans, (0, chunks)),
        "across",
        shared + own_buckets,
        [
            pltpu.VMEM((rows, columns // 2), BF16),
            jax.ShapeDtypeStruct((1, rows), jnp.float32),
        ],
        flops=chunks * per_chunk * 6,
    )
    parts = [(0, chunks // 2), (chunks // 2, chunks)]
    mixes, squares = [], []
    for part in parts:
        count = part[1] - part[0]
        mix, square = call(
            functools.partial(across_kernel, False, cross_bits, first_level, spans, part),
            "across",
            shared + other_buckets + [own_square],
            [
                pltpu.VMEM((count * CHUNK, columns // 2), BF16),
                jax.ShapeDtypeStruct((1, count * CHUNK), jnp.float32),
            ],
            flops=count * per_chunk * 6,
        )
        mixes.append(mix)
        bit = 1
        while bit < head_size:
            square = square + lax.ppermute(
                square, "head", [(i, i ^ bit) for i in range(head_size)]
            )
            bit *= 2
        squares.append(square)

    out = None
    step = CHUNK
    width = HEADS * VALUE_DIM
    for part, mix, square in zip(parts, mixes, squares):
        steps = part[1] - part[0]
        operands = [position, keep(own_mix), keep(mix), norm_gain.reshape(1, -1), square]
        in_specs = [
            scalar,
            WHOLE,
            WHOLE,
            pl.BlockSpec((1, columns), lambda i: (0, 0)),
            pl.BlockSpec((1, step), lambda i: (0, i)),
        ]
        aliases = {}
        if out is not None:
            operands.append(out)
            in_specs.append(ANYWHERE)
            aliases = {5: 0}
        out = call(
            functools.partial(norm_kernel, width, step, part[0]),
            "norm",
            operands,
            jax.ShapeDtypeStruct((rows, columns), BF16),
            flops=3 * rows * columns,
            size=2 * steps * step * columns,
            in_specs=in_specs,
            out_specs=pl.BlockSpec((step, columns), lambda i, low=part[0]: (i + low, 0)),
            grid=(steps,),
            input_output_aliases=aliases,
        )
    return out


def solution(mesh):
    placed = (
        P("seq", "head"),
        P("seq", "head"),
        P("seq", "head"),
        P("head", None, "seq"),
        P("head"),
    )
    return jax.shard_map(
        body, mesh=mesh, in_specs=placed, out_specs=P("seq", "head"), check_vma=False
    )
```

time: 565 us -> 54.8 us (0.10); the launches traced: 555 us -> 54.7 us
  matrix products: 303 us -> 0 us
  local copies, waits for them, and re-layouts: 146 us -> 0.01 us
  other arithmetic: 77.8 us -> 0.02 us
  Pallas kernels: 0 us -> 38 us
  between operations: 14.9 us -> 0.12 us
  blocking collectives: 13.3 us -> 0 us
  starting transfers between devices: 0.01 us -> 13.2 us
    dot_general x11 -> x0, matrix products: 303 us -> none  [the longest x4 215 us: body(): jnp.einsum('thd,shd->hts', query_rows[start_row:end_row], key_rows[:end_r...]
    unnamed x163 -> x2, local copies, waits for them, and re-layouts: 53.7 us -> 0.01 us
    pallas_call x0 -> x11, Pallas kernels: none -> 38 us  [call(): pl.pallas_call(kernel, name=name, in_specs=in_specs, out_shape=out_shape,...]
    le x4 -> x0, other arithmetic: 35.5 us -> none  [body(): causal = (col_ids[None, :] <= row_ids[:, None])[None]]
    slice x12 -> x0, local copies, waits for them, and re-layouts: 31.5 us -> none  [the longest x3 12.5 us: body(): value_rows[:end_row]]
    reduce_sum x1 -> x0, other arithmetic: 25.7 us -> none  [body(): square = jnp.sum(mixture * mixture, axis=1)]
    broadcast_in_dim x24 -> x0, local copies, waits for them, and re-layouts: 18.2 us -> none  [body(): jnp.where(levels[None] == depth_id, level_weights[:, depth_id, start_row:...]
    transpose x1 -> x0, local copies, waits for them, and re-layouts: 17.7 us -> none  [body(): (inside + across).transpose(1, 0, 2)]
  transfers between devices with their start and end apart: 1 -> 9, of which waited for: 0 -> 3; matrix products, arithmetic and copies ran while one was open for 74% -> 0% of each run, Pallas kernels for 0% -> 47%
where the time goes in v2:
time: 54.8 us; the launch traced here: 54.7 us
  Pallas kernels  38 us (69%)
  starting transfers between devices  13.2 us (24%)
  waiting for transfers between devices  3.27 us (6%)
    pallas_call x11, Pallas kernels, call(): pl.pallas_call(kernel, name=name, in_specs=in_specs, out_shape=out_shape,...  38 us
    ppermute x4, starting transfers between devices, body(): lax.ppermute(square, 'head', [(i, i ^ bit) for i in range(head_size)])  7.38 us
    ppermute x5, starting transfers between devices, swap(): lax.ppermute(array, 'seq', [(i, i ^ 1 << bit) for i in range(seq_size)])  5.84 us
    ppermute x5, waiting for transfers between devices, swap(): lax.ppermute(array, 'seq', [(i, i ^ 1 << bit) for i in range(seq_size)])  2.74 us
  transfers between devices with their start and end apart: 9, of which 3 were waited for; matrix products, arithmetic and copies ran while one was open for 0% of the time, Pallas kernels for 47%

profile of v2, /device:TPU:0, one launch (start us, length us, event | category | flops | bytes accessed | tf_op | source)
XLA Modules:
  0.0 54.7 jit_solution(10998148249446262543)
XLA Ops:
  0.0 7.0 %states.1 = (bf16[2048,2048]{1,0:T(8,128)(2,1)S(1)}, bf16[2048,2048]{1,0:T(8,128)(2,1)S(1)}, bf16[16,7,128,128]{3,2,1,0:T(8,128)(2,1)S(1)}, bf16[16,128,128]{2,1...) custom-call(s32[1]{0:T(128)} %bitcast.pos_ref, bf16[2048,2048]{1,0:T(8,128)(2,1)} %k_hbm.1, ...), custom_call_target="tpu_custom_call" | custom-call | flops 1073741824 | bytes 16777216 | tf_op jit(solution)/shard_map/states/pallas_call | solution.py:277
  7.0 0.5 collective-permute-start
  7.5 1.5 %collective-permute-done.refs_0_.received_ref.refs_9_ = bf16[16,128,128]{2,1,0:T(8,128)(2,1)S(1)} collective-permute-done((bf16[16,128,128]{2,1,0:T(8,128)(2,1)S(1)}, bf16[16,128,128]{2,1,0:T(8,128)(2,1)S(1)}, u32[]{:S(2)}, u32[]{:S(2)}) %collective-permute-start) | collective-permute-done | bytes 524320 | tf_op jit(solution)/shard_map/ppermute | solution.py:324
  9.1 0.1 sum.2.mine_ref
  9.1 2.9 %collective-permute-start.1 = (bf16[8,128,128]{2,1,0:T(8,128)(2,1)S(1)}, bf16[8,128,128]{2,1,0:T(8,128)(2,1)S(1)}, u32[]{:S(2)}, u32[]{:S(2)}) collective-permute-start(bf16[8,128,128]{2,1,0:T(8,128)(2,1)S(1)} %sum.2.mine_ref), channel_id=1, source_target_pairs={{0,8},{4,12},{8,0},{12,4},{16,24},{20,28},{24,16},{28,20},{1,9},{5... | collective-permute-start | bytes 786440 | tf_op jit(solution)/shard_map/ppermute | solution.py:324
  12.1 5.4 %local.3 = (bf16[2,2048,256]{2,1,0:T(8,128)(2,1)S(1)}, bf16[1280,2048]{1,0:T(8,128)(2,1)S(1)}, f32[16,16,1280]{2,1,0:T(8,128)S(1)}) custom-call(s32[1]{0:T(128)} %bitcast.pos_ref, bf16[512,2048]{1,0:T(8,128)(2,1)S(1)} %get-tuple-element.23.q_ref.refs_0_, bf16[2048,2048]{1,0:T(8,128)(2,1)S(1)} %get-tuple-element.24.k_ref, ...), custom_call_target="tpu_custom_call" | custom-call | flops 4831838208 | tf_op jit(solution)/shard_map/local/pallas_call | solution.py:277
  17.5 1.2 %collective-permute-done.1.received_ref.refs_10_ = bf16[8,128,128]{2,1,0:T(8,128)(2,1)S(1)} collective-permute-done((bf16[8,128,128]{2,1,0:T(8,128)(2,1)S(1)}, bf16[8,128,128]{2,1,0:T(8,128)(2,1)S(1)}, u32[]{:S(2)}, u32[]{:S(2)}) %collective-permute-start.1) | collective-permute-done | bytes 262176 | tf_op jit(solution)/shard_map/ppermute | solution.py:324
  18.7 0.1 sum.3
  18.7 1.8 %collective-permute-start.2 = (bf16[8,128,128]{2,1,0:T(8,128)(2,1)S(1)}, bf16[8,128,128]{2,1,0:T(8,128)(2,1)S(1)}, u32[]{:S(2)}, u32[]{:S(2)}) collective-permute-start(bf16[8,128,128]{2,1,0:T(8,128)(2,1)S(1)} %sum.3), channel_id=1, source_target_pairs={{0,16},{4,20},{8,24},{12,28},{16,0},{20,4},{24,8},{28,12},{1,17},{... | collective-permute-start | bytes 786440 | tf_op jit(solution)/shard_map/ppermute | solution.py:324
  20.6 9.4 %local.4 = (bf16[5,2048,256]{2,1,0:T(8,128)(2,1)S(1)}, bf16[256,2048]{1,0:T(8,128)(2,1)S(1)}, f32[16,16,256]{2,1,0:T(8,128)S(1)}) custom-call(s32[1]{0:T(128)} %bitcast.pos_ref, bf16[1280,2048]{1,0:T(8,128)(2,1)S(1)} %get-tuple-element.28.q_ref.refs_1_, bf16[2048,2048]{1,0:T(8,128)(2,1)S(1)} %get-tuple-element.24.k_ref, ...), custom_call_target="tpu_custom_call" | custom-call | flops 12079595520 | tf_op jit(solution)/shard_map/local/pallas_call | solution.py:277
  30.0 2.1 %local.5.refs_8_ = bf16[1,2048,256]{2,1,0:T(8,128)(2,1)S(1)} custom-call(s32[1]{0:T(128)} %bitcast.pos_ref, bf16[256,2048]{1,0:T(8,128)(2,1)S(1)} %get-tuple-element.31.q_ref.refs_2_, bf16[2048,2048]{1,0:T(8,128)(2,1)S(1)} %get-tuple-element.24.k_ref, bf16[2048,2048]{1,0:T(8,128)(2,1)S(1)} %get-tuple-element.25.v_ref, ...), custom_call_target="tpu_custom_call" | custom-call | flops 2415919104 | tf_op jit(solution)/shard_map/local/pallas_call | solution.py:277
  32.1 0.1 collective-permute-start.3
  32.2 0.0 collective-permute-done.2.refs_11_
  32.2 0.5 collective-permute-start.4
  32.7 3.7 %across.3 = (bf16[2048,1024]{1,0:T(8,128)(2,1)S(1)}, f32[1,2048]{1,0:T(1,128)S(1)}) custom-call(s32[1]{0:T(128)} %bitcast.pos_ref, bf16[512,2048]{1,0:T(8,128)(2,1)S(1)} %get-tuple-element.23.q_ref.refs_0_, bf16[1280,2048]{1,0:T(8,128)(2,1)S(1)} %get-tuple-element.28.q_ref.refs_1_, bf16[256,2048]{1,0:T(8,128)(2,1)S(1)} %get-tuple-element.31.q_ref.refs_2_, ...), custom_call_target="tpu_custom_call" | custom-call | flops 6442450944 | tf_op jit(solution)/shard_map/across/pallas_call | solution.py:277
  36.4 0.0 collective-permute-done.3.refs_10_
  36.4 0.0 collective-permute-done.4.refs_11_
  36.4 2.1 %across.5 = (bf16[1024,1024]{1,0:T(8,128)(2,1)S(1)}, f32[1,1024]{1,0:T(1,128)S(1)}) custom-call(s32[1]{0:T(128)} %bitcast.pos_ref, bf16[512,2048]{1,0:T(8,128)(2,1)S(1)} %get-tuple-element.23.q_ref.refs_0_, bf16[1280,2048]{1,0:T(8,128)(2,1)S(1)} %get-tuple-element.28.q_ref.refs_1_, bf16[256,2048]{1,0:T(8,128)(2,1)S(1)} %get-tuple-element.31.q_ref.refs_2_, ...), custom_call_target="tpu_custom_call" | custom-call | flops 3221225472 | tf_op jit(solution)/shard_map/across/pallas_call | solution.py:277
  38.5 0.0 copy-start
  38.6 1.7 %collective-permute-start.7 = (f32[1,1024]{1,0:T(1,128)S(1)}, f32[1,1024]{1,0:T(1,128)S(1)}, u32[]{:S(2)}, u32[]{:S(2)}) collective-permute-start(f32[1,1024]{1,0:T(1,128)S(1)} %get-tuple-element.40), channel_id=1, source_target_pairs={{0,1},{1,0},{2,3},{3,2},{4,5},{5,4},{6,7},{7,6},{8,9},{9,8},{10,11... | collective-permute-start | bytes 12296 | tf_op jit(solution)/shard_map/ppermute | solution.py:404
  40.2 1.9 %across.4 = (bf16[1024,1024]{1,0:T(8,128)(2,1)S(1)}, f32[1,1024]{1,0:T(1,128)S(1)}) custom-call(s32[1]{0:T(128)} %bitcast.pos_ref, bf16[512,2048]{1,0:T(8,128)(2,1)S(1)} %get-tuple-element.23.q_ref.refs_0_, bf16[1280,2048]{1,0:T(8,128)(2,1)S(1)} %get-tuple-element.28.q_ref.refs_1_, bf16[256,2048]{1,0:T(8,128)(2,1)S(1)} %get-tuple-element.31.q_ref.refs_2_, ...), custom_call_target="tpu_custom_call" | custom-call | flops 3221225472 | tf_op jit(solution)/shard_map/across/pallas_call | solution.py:277
  42.1 0.5 collective-permute-start.5
  42.7 0.0 collective-permute-done.7
  42.7 2.7 %collective-permute-start.8 = (f32[1,1024]{1,0:T(1,128)S(1)}, f32[1,1024]{1,0:T(1,128)S(1)}, u32[]{:S(2)}, u32[]{:S(2)}) collective-permute-start(f32[1,1024]{1,0:T(1,128)S(1)} %add.14), channel_id=1, source_target_pairs={{0,2},{1,3},{2,0},{3,1},{4,6},{5,7},{6,4},{7,5},{8,10},{9,11},{10,... | collective-permute-start | bytes 12296 | tf_op jit(solution)/shard_map/ppermute | solution.py:404
  45.3 0.5 collective-permute-done.5
  45.8 2.6 %collective-permute-start.6 = (f32[1,1024]{1,0:T(1,128)S(1)}, f32[1,1024]{1,0:T(1,128)S(1)}, u32[]{:S(2)}, u32[]{:S(2)}) collective-permute-start(f32[1,1024]{1,0:T(1,128)S(1)} %add.12), channel_id=1, source_target_pairs={{0,2},{1,3},{2,0},{3,1},{4,6},{5,7},{6,4},{7,5},{8,10},{9,11},{10,... | collective-permute-start | bytes 12296 | tf_op jit(solution)/shard_map/ppermute | solution.py:404
  48.4 0.0 collective-permute-done.8
  48.4 0.0 copy-done
  48.4 3.1 %norm.2.refs_0_ = bf16[2048,2048]{1,0:T(8,128)(2,1)} custom-call(s32[1]{0:T(128)} %bitcast.pos_ref, bf16[2048,1024]{1,0:T(8,128)(2,1)S(1)} %get-tuple-element.35.own_ref, bf16[1024,1024]{1,0:T(8,128)(2,1)S(1)} %get-tuple-element.39.other_ref, f32[1,2048]{1,0:T(1,128)S(1)} %bitcast.2, f32[1,1024]{1,0:T(1,128)S(1)} %add.15.square_ref), custom_call_target="tpu_custom_call" | custom-call | flops 12582912 | bytes 4194304 | tf_op jit(solution)/shard_map/norm/pallas_call | solution.py:277
  51.5 0.0 collective-permute-done.6
  51.5 3.1 %norm.3 = bf16[2048,2048]{1,0:T(8,128)(2,1)} custom-call(s32[1]{0:T(128)} %bitcast.pos_ref, bf16[2048,1024]{1,0:T(8,128)(2,1)S(1)} %get-tuple-element.35.own_ref, bf16[1024,1024]{1,0:T(8,128)(2,1)S(1)} %get-tuple-element.37.other_ref, f32[1,2048]{1,0:T(1,128)S(1)} %bitcast.3, f32[1,1024]{1,0:T(1,128)S(1)} %add.13.square_ref, ...), custom_call_target="tpu_custom_call", output_to_operand_aliasing={{}: (5, {})} | custom-call | flops 12582912 | bytes 4194304 | tf_op jit(solution)/shard_map/norm/pallas_call | solution.py:277
  (4 shorter events, 0.0 us)
Async XLA Ops:
  7.0 2.1 %collective-permute-start = (bf16[16,128,128]{2,1,0:T(8,128)(2,1)S(1)}, bf16[16,128,128]{2,1,0:T(8,128)(2,1)S(1)}, u32[]{:S(2)}, u32[]{:S(2)}) collective-permute-start(bf16[16,128,128]{2,1,0:T(8,128)(2,1)S(1)} %get-tuple-element.30.mine_ref), channel_id=1, source_target_pairs={{0,4},{4,0},{8,12},{12,8},{16,20},{20,16},{24,28},{28,24},{1,5},{5... | collective-permute-start | bytes 1572872 | tf_op jit(solution)/shard_map/ppermute | solution.py:324
  9.1 9.5 %collective-permute-start.1 = (bf16[8,128,128]{2,1,0:T(8,128)(2,1)S(1)}, bf16[8,128,128]{2,1,0:T(8,128)(2,1)S(1)}, u32[]{:S(2)}, u32[]{:S(2)}) collective-permute-start(bf16[8,128,128]{2,1,0:T(8,128)(2,1)S(1)} %sum.2.mine_ref), channel_id=1, source_target_pairs={{0,8},{4,12},{8,0},{12,4},{16,24},{20,28},{24,16},{28,20},{1,9},{5... | collective-permute-start | bytes 786440 | tf_op jit(solution)/shard_map/ppermute | solution.py:324
  18.7 13.5 %collective-permute-start.2 = (bf16[8,128,128]{2,1,0:T(8,128)(2,1)S(1)}, bf16[8,128,128]{2,1,0:T(8,128)(2,1)S(1)}, u32[]{:S(2)}, u32[]{:S(2)}) collective-permute-start(bf16[8,128,128]{2,1,0:T(8,128)(2,1)S(1)} %sum.3), channel_id=1, source_target_pairs={{0,16},{4,20},{8,24},{12,28},{16,0},{20,4},{24,8},{28,12},{1,17},{... | collective-permute-start | bytes 786440 | tf_op jit(solution)/shard_map/ppermute | solution.py:324
  32.1 4.3 %collective-permute-start.3 = (bf16[8,128,128]{2,1,0:T(8,128)(2,1)S(1)}, bf16[8,128,128]{2,1,0:T(8,128)(2,1)S(1)}, u32[]{:S(2)}, u32[]{:S(2)}) collective-permute-start(bf16[8,128,128]{2,1,0:T(8,128)(2,1)S(1)} %collective-permute-done.1.received_ref.refs_10_), channel_id=1, source_target_pairs={{0,4},{4,0},{8,12},{12,8},{16,20},{20,16},{24,28},{28,24},{1,5},{5... | collective-permute-start | bytes 786440 | tf_op jit(solution)/shard_map/ppermute | solution.py:324
  32.2 4.2 %collective-permute-start.4 = (bf16[8,128,128]{2,1,0:T(8,128)(2,1)S(1)}, bf16[8,128,128]{2,1,0:T(8,128)(2,1)S(1)}, u32[]{:S(2)}, u32[]{:S(2)}) collective-permute-start(bf16[8,128,128]{2,1,0:T(8,128)(2,1)S(1)} %collective-permute-done.2.refs_11_), channel_id=1, source_target_pairs={{0,4},{4,0},{8,12},{12,8},{16,20},{20,16},{24,28},{28,24},{1,5},{5... | collective-permute-start | bytes 786440 | tf_op jit(solution)/shard_map/ppermute | solution.py:324
  38.5 9.9 %copy-start = (f32[2048]{0:T(1024)S(1)}, f32[2048]{0:T(1024)}, u32[]{:S(2)}) copy-start(f32[2048]{0:T(1024)} %param.9) | copy-start | bytes 24580
  38.6 4.1 %collective-permute-start.7 = (f32[1,1024]{1,0:T(1,128)S(1)}, f32[1,1024]{1,0:T(1,128)S(1)}, u32[]{:S(2)}, u32[]{:S(2)}) collective-permute-start(f32[1,1024]{1,0:T(1,128)S(1)} %get-tuple-element.40), channel_id=1, source_target_pairs={{0,1},{1,0},{2,3},{3,2},{4,5},{5,4},{6,7},{7,6},{8,9},{9,8},{10,11... | collective-permute-start | bytes 12296 | tf_op jit(solution)/shard_map/ppermute | solution.py:404
  42.1 3.7 %collective-permute-start.5 = (f32[1,1024]{1,0:T(1,128)S(1)}, f32[1,1024]{1,0:T(1,128)S(1)}, u32[]{:S(2)}, u32[]{:S(2)}) collective-permute-start(f32[1,1024]{1,0:T(1,128)S(1)} %get-tuple-element.38), channel_id=1, source_target_pairs={{0,1},{1,0},{2,3},{3,2},{4,5},{5,4},{6,7},{7,6},{8,9},{9,8},{10,11... | collective-permute-start | bytes 12296 | tf_op jit(solution)/shard_map/ppermute | solution.py:404
  42.7 5.8 %collective-permute-start.8 = (f32[1,1024]{1,0:T(1,128)S(1)}, f32[1,1024]{1,0:T(1,128)S(1)}, u32[]{:S(2)}, u32[]{:S(2)}) collective-permute-start(f32[1,1024]{1,0:T(1,128)S(1)} %add.14), channel_id=1, source_target_pairs={{0,2},{1,3},{2,0},{3,1},{4,6},{5,7},{6,4},{7,5},{8,10},{9,11},{10,... | collective-permute-start | bytes 12296 | tf_op jit(solution)/shard_map/ppermute | solution.py:404
  45.8 5.7 %collective-permute-start.6 = (f32[1,1024]{1,0:T(1,128)S(1)}, f32[1,1024]{1,0:T(1,128)S(1)}, u32[]{:S(2)}, u32[]{:S(2)}) collective-permute-start(f32[1,1024]{1,0:T(1,128)S(1)} %add.12), channel_id=1, source_target_pairs={{0,2},{1,3},{2,0},{3,1},{4,6},{5,7},{6,4},{7,5},{8,10},{9,11},{10,... | collective-permute-start | bytes 12296 | tf_op jit(solution)/shard_map/ppermute | solution.py:404

commit v3 on v2

--- a/solution.py
+++ b/solution.py
@@ -70,7 +70,10 @@
         for copy in pair:
             copy.start()
         copies.append(pair)
-    more = weight_copies(span, q_hbm, w_hbm, q_ref, w_ref, more_sems)
+    more = [
+        pltpu.make_async_copy(w_hbm, w_ref, more_sems.at[0]),
+        query_copy(span, q_hbm, q_ref, more_sems.at[1]),
+    ]
     for c in range(chunks):
         for copy in copies[c]:
             copy.wait()
@@ -93,15 +96,13 @@
         copy.wait()
 
 
-def weight_copies(span, q_hbm, w_hbm, q_ref, w_ref, sems):
+def query_copy(span, q_hbm, q_ref, sem):
     here = pl.ds(span[0] * CHUNK, (span[1] - span[0]) * CHUNK)
-    return [
-        pltpu.make_async_copy(w_hbm.at[:, :, here], w_ref, sems.at[0]),
-        pltpu.make_async_copy(q_hbm.at[here], q_ref, sems.at[1]),
-    ]
-
-
-def sum_kernel(whole, pos_ref, mine_ref, received_ref, out_ref):
+    return pltpu.make_async_copy(q_hbm.at[here], q_ref, sem)
+
+
+def sum_kernel(whole, pos_ref, mine_ref, received_ref, after_ref, out_ref):
+    del after_ref
     half = out_ref.shape[0]
     here = pl.ds((pos_ref[0] & 1) * half if whole else 0, half)
     total = mine_ref[here].astype(jnp.float32) + received_ref[here].astype(jnp.float32)
@@ -142,16 +143,15 @@
     received_ref = refs.pop(0) if first_level is not None else None
     copies = []
     if after is not None:
-        q_hbm, w_hbm, out_ref, q_next, w_next, sems = refs
-        copies = weight_copies(after, q_hbm, w_hbm, q_next, w_next, sems)
-        for copy in copies:
-            copy.start()
+        q_hbm, out_ref, q_next, sem = refs
+        copies = [query_copy(after, q_hbm, q_next, sem)]
+        copies[0].start()
     else:
         (out_ref,) = refs
     present = (pos_ref[0] & 1) == 1
 
     def scores(c, h):
-        start = (c - span[0]) * CHUNK
+        start = c * CHUNK
         depths = [d for d in range(depth_count) if c >> d & 1]
         stream = [k_ref[rows_of(c), columns_of(h)]]
         stream += [local_ref[h, bucket_slot(depth_count, d, c)] for d in depths]
@@ -202,11 +202,11 @@
 def across_kernel(mine, bits, first_level, spans, part, pos_ref, *refs):
     refs = list(refs)
     q_refs = [refs.pop(0) for _ in spans]
-    w_refs = [refs.pop(0) for _ in spans]
+    w_ref = refs.pop(0)
     in_refs = [refs.pop(0) for _ in spans]
     state_refs = [refs.pop(0) for _ in range(bits)]
     mix_ref, square_ref = refs[-2:]
-    half = w_refs[0].shape[0] // 2
+    half = w_ref.shape[0] // 2
     position = pos_ref[0]
     own = (position & 1) * half
     first = own if mine else half - own
@@ -220,7 +220,7 @@
         for c in range(*part):
             s = [low <= c < high for low, high in spans].index(True)
             local = c - spans[s][0]
-            start = local * CHUNK
+            start = c * CHUNK
             used = range(0 if s == 0 else 1, bits)
             total = in_refs[s][local, columns_of(head), :].astype(jnp.float32)
             if len(used):
@@ -228,7 +228,7 @@
                 result = dot(stream, q_refs[s][rows_of(local), columns_of(head)], TT)
                 for n, b in enumerate(used):
                     level = first_level + b
-                    row = w_refs[s][head, level : level + 1, start : start + CHUNK] * SCALING
+                    row = w_ref[head, level : level + 1, start : start + CHUNK] * SCALING
                     total += result[n * VALUE_DIM : (n + 1) * VALUE_DIM] * row
             square = jnp.sum((total * total).reshape(VALUE_DIM // GROUP, GROUP, CHUNK), axis=0)
             squares[c] = squares[c] + square if c in squares else square
@@ -241,18 +241,31 @@
         square_ref[:, here] = square
 
 
-def norm_kernel(width, step, low, pos_ref, own_ref, other_ref, gain_ref, square_ref, *refs):
-    out_ref = refs[-1]
-    i = pl.program_id(0)
-    half = own_ref.shape[1]
+def norm_kernel(
+    width, pos_ref, own_ref, other_ref, gain_ref, square_ref, received_ref, out_hbm, out_ref, sems
+):
+    rows, half = own_ref.shape
     own = (pos_ref[0] & 1) * half
-    factor = lax.rsqrt(square_ref[...] / width + 1e-05)
-    column = jnp.broadcast_to(factor, (GROUP, step)).T[:, :1]
-    for mix_ref, at, first in ((own_ref, low + i, own), (other_ref, i, half - own)):
-        here = pl.ds(pl.multiple_of(at * step, step), step)
-        there = pl.ds(pl.multiple_of(first, HEAD_DIM), half)
-        mixture = mix_ref[here, :].astype(jnp.float32)
-        out_ref[:, there] = (mixture * gain_ref[:, there] * column).astype(out_ref.dtype)
+    step = CHUNK // 2
+    slots = out_ref.shape[0] // step
+    copies = []
+    for i in range(rows // step):
+        here = pl.ds(i * step, step)
+        slot = pl.ds(i % slots * step, step)
+        if i >= slots:
+            copies[i - slots].wait()
+        square = square_ref[:, here] + received_ref[:, here]
+        factor = lax.rsqrt(square / width + 1e-05)
+        column = jnp.broadcast_to(factor, (GROUP, step)).T[:, :1]
+        for mix_ref, first in ((own_ref, own), (other_ref, half - own)):
+            there = pl.ds(pl.multiple_of(first, HEAD_DIM), half)
+            mixture = mix_ref[here, :].astype(jnp.float32)
+            out_ref[slot, there] = (mixture * gain_ref[:, there] * column).astype(out_ref.dtype)
+        copy = pltpu.make_async_copy(out_ref.at[slot], out_hbm.at[here], sems.at[i])
+        copy.start()
+        copies.append(copy)
+    for copy in copies[-slots:]:
+        copy.wait()
 
 
 def body(queries, key_vectors, value_vectors, level_weights, norm_gain):
@@ -286,15 +299,11 @@
             **settings,
         )(*operands)
 
-    cuts = sorted({0, chunks // 4, chunks * 7 // 8, chunks})
+    cuts = sorted({0, chunks // 8, chunks * 5 // 8, chunks})
     spans = list(zip(cuts[:-1], cuts[1:]))
 
-    def weight_shapes(span):
-        count = (span[1] - span[0]) * CHUNK
-        return [
-            pltpu.VMEM((count, columns), BF16),
-            pltpu.VMEM((heads, levels, count), jnp.float32),
-        ]
+    def query_shape(span):
+        return pltpu.VMEM(((span[1] - span[0]) * CHUNK, columns), BF16)
 
     per_chunk = 2 * heads * CHUNK * 128 * 128
     queries, level_weights = leave(queries), leave(level_weights)
@@ -308,7 +317,7 @@
             pltpu.VMEM((heads, chunks - 1, VALUE_DIM, HEAD_DIM), BF16),
             jax.ShapeDtypeStruct((heads, VALUE_DIM, HEAD_DIM), BF16),
         ]
-        + weight_shapes(spans[0]),
+        + [query_shape(spans[0]), pltpu.VMEM((heads, levels, rows), jnp.float32)],
         flops=chunks * per_chunk,
         size=4 * rows * columns,
         in_specs=[scalar] + [ANYWHERE] * 4,
@@ -318,37 +327,31 @@
             pltpu.SemaphoreType.DMA((2,)),
         ],
     )
+    weight = keep(weight)
     keys, values, local_states = keep(keys), keep(values), keep(local_states)
 
     def swap(array, bit):
         return lax.ppermute(array, "seq", [(i, i ^ (1 << bit)) for i in range(seq_size)])
 
-    def add(mine, received, whole):
+    def add(mine, received, after, whole):
         return call(
             functools.partial(sum_kernel, whole),
             "sum",
-            [position, mine, received],
+            [position, mine, received, after],
             jax.ShapeDtypeStruct((half, VALUE_DIM, HEAD_DIM), BF16),
             limit=4,
+            in_specs=[scalar, WHOLE, WHOLE, WHOLE],
         )
 
     received = swap(block_state, 0)
     own_buckets, other_buckets = [received], [received]
-    running = add(block_state, received, True)
-    for b in range(1, cross_bits):
-        received = swap(running, b)
-        own_buckets.append(received)
-        other_buckets.append(swap(received, 0))
-        if b + 1 < cross_bits:
-            running = add(running, received, False)
-
-    insides, query_parts, weight_parts = [], [], []
+    running = block_state
+    insides, query_parts = [], []
     for p, span in enumerate(spans):
         count = span[1] - span[0]
         after = spans[p + 1] if p + 1 < len(spans) else None
-        query, weight = keep(query), keep(weight)
+        query = keep(query)
         query_parts.append(query)
-        weight_parts.append(weight)
         operands = [position, query, keys, values, weight, local_states]
         if p > 0:
             operands.append(own_buckets[0])
@@ -356,10 +359,10 @@
         out_shape = [pltpu.VMEM((count, columns, CHUNK), BF16)]
         scratch = []
         if after is not None:
-            operands += [queries, level_weights]
-            in_specs += [ANYWHERE] * 2
-            out_shape += weight_shapes(after)
-            scratch = [pltpu.SemaphoreType.DMA((2,))]
+            operands.append(queries)
+            in_specs.append(ANYWHERE)
+            out_shape.append(query_shape(after))
+            scratch = [pltpu.SemaphoreType.DMA(())]
         results = call(
             functools.partial(local_kernel, span, after, 2, first_level if p else None),
             "local",
@@ -371,73 +374,54 @@
         )
         insides.append(keep(results[0]))
         if after is not None:
-            query, weight = results[1:]
-
-    shared = [position, *query_parts, *weight_parts, *insides]
-    own_mix, own_square = call(
-        functools.partial(across_kernel, True, cross_bits, first_level, spans, (0, chunks)),
-        "across",
-        shared + own_buckets,
-        [
-            pltpu.VMEM((rows, columns // 2), BF16),
-            jax.ShapeDtypeStruct((1, rows), jnp.float32),
+            query = results[1]
+        if p + 1 < cross_bits:
+            running = add(running, received, insides[-1], p == 0)
+            received = swap(running, p + 1)
+            own_buckets.append(received)
+            other_buckets.append(swap(received, 0))
+    for b in range(len(spans) + 1, cross_bits):
+        running = add(running, received, insides[-1], False)
+        received = swap(running, b)
+        own_buckets.append(received)
+        other_buckets.append(swap(received, 0))
+
+    shared = [position, *query_parts, weight, *insides]
+
+    def across(mine, operands):
+        return call(
+            functools.partial(across_kernel, mine, cross_bits, first_level, spans, (0, chunks)),
+            "across",
+            operands,
+            [
+                pltpu.VMEM((rows, columns // 2), BF16),
+                jax.ShapeDtypeStruct((1, rows), jnp.float32),
+            ],
+            flops=chunks * per_chunk * 6,
+        )
+
+    own_mix, square = across(True, shared + own_buckets)
+    other_mix, square = across(False, shared + other_buckets + [square])
+    received = jnp.zeros_like(square)
+    bit = 1
+    while bit < head_size:
+        if bit > 1:
+            square = square + received
+        received = lax.ppermute(square, "head", [(i, i ^ bit) for i in range(head_size)])
+        bit *= 2
+    return call(
+        functools.partial(norm_kernel, HEADS * VALUE_DIM),
+        "norm",
+        [position, keep(own_mix), keep(other_mix), norm_gain.reshape(1, -1), square, received],
+        jax.ShapeDtypeStruct((rows, columns), BF16),
+        flops=3 * rows * columns,
+        size=2 * rows * columns,
+        out_specs=ANYWHERE,
+        scratch_shapes=[
+            pltpu.VMEM((rows // 2, columns), BF16),
+            pltpu.SemaphoreType.DMA((2 * chunks,)),
         ],
-        flops=chunks * per_chunk * 6,
     )
-    parts = [(0, chunks // 2), (chunks // 2, chunks)]
-    mixes, squares = [], []
-    for part in parts:
-        count = part[1] - part[0]
-        mix, square = call(
-            functools.partial(across_kernel, False, cross_bits, first_level, spans, part),
-            "across",
-            shared + other_buckets + [own_square],
-            [
-                pltpu.VMEM((count * CHUNK, columns // 2), BF16),
-                jax.ShapeDtypeStruct((1, count * CHUNK), jnp.float32),
-            ],
-            flops=count * per_chunk * 6,
-        )
-        mixes.append(mix)
-        bit = 1
-        while bit < head_size:
-            square = square + lax.ppermute(
-                square, "head", [(i, i ^ bit) for i in range(head_size)]
-            )
-            bit *= 2
-        squares.append(square)
-
-    out = None
-    step = CHUNK
-    width = HEADS * VALUE_DIM
-    for part, mix, square in zip(parts, mixes, squares):
-        steps = part[1] - part[0]
-        operands = [position, keep(own_mix), keep(mix), norm_gain.reshape(1, -1), square]
-        in_specs = [
-            scalar,
-            WHOLE,
-            WHOLE,
-            pl.BlockSpec((1, columns), lambda i: (0, 0)),
-            pl.BlockSpec((1, step), lambda i: (0, i)),
-        ]
-        aliases = {}
-        if out is not None:
-            operands.append(out)
-            in_specs.append(ANYWHERE)
-            aliases = {5: 0}
-        out = call(
-            functools.partial(norm_kernel, width, step, part[0]),
-            "norm",
-            operands,
-            jax.ShapeDtypeStruct((rows, columns), BF16),
-            flops=3 * rows * columns,
-            size=2 * steps * step * columns,
-            in_specs=in_specs,
-            out_specs=pl.BlockSpec((step, columns), lambda i, low=part[0]: (i + low, 0)),
-            grid=(steps,),
-            input_output_aliases=aliases,
-        )
-    return out
 
 
 def solution(mesh):

time: 54.8 us -> 48.9 us (0.89)
  Pallas kernels: 38 us -> 34 us
  starting transfers between devices: 13.2 us -> 9.28 us
  waiting for transfers between devices: 3.27 us -> 5.09 us
    pallas_call x11 -> x9, Pallas kernels: 38 us -> 34 us  [call(): pl.pallas_call(kernel, name=name, in_specs=in_specs, out_shape=out_shape,...]
    ppermute x4 -> x2, waiting for transfers between devices: 0.53 us -> 4.02 us  [body(): lax.ppermute(square, 'head', [(i, i ^ bit) for i in range(head_size)])]
    ppermute x4 -> x2, starting transfers between devices: 7.38 us -> 4.53 us  [body(): lax.ppermute(square, 'head', [(i, i ^ bit) for i in range(head_size)])]
    ppermute x5, waiting for transfers between devices: 2.74 us -> 1.06 us  [swap(): lax.ppermute(array, 'seq', [(i, i ^ 1 << bit) for i in range(seq_size)])]
    ppermute x5, starting transfers between devices: 5.84 us -> 4.75 us  [swap(): lax.ppermute(array, 'seq', [(i, i ^ 1 << bit) for i in range(seq_size)])]
  transfers between devices with their start and end apart: 9 -> 7, of which waited for: 3 -> 3; matrix products, arithmetic and copies ran while one was open for 0% -> 0% of each run, Pallas kernels for 47% -> 40%
where the time goes in v3:
time: 48.9 us; the launch traced here: 48.7 us
  Pallas kernels  34 us (70%)
  starting transfers between devices  9.28 us (19%)
  waiting for transfers between devices  5.09 us (10%)
    pallas_call x9, Pallas kernels, call(): pl.pallas_call(kernel, name=name, in_specs=in_specs, out_shape=out_shape,...  34 us
    ppermute x5, starting transfers between devices, swap(): lax.ppermute(array, 'seq', [(i, i ^ 1 << bit) for i in range(seq_size)])  4.75 us
    ppermute x2, starting transfers between devices, body(): lax.ppermute(square, 'head', [(i, i ^ bit) for i in range(head_size)])  4.53 us
    ppermute x2, waiting for transfers between devices, body(): lax.ppermute(square, 'head', [(i, i ^ bit) for i in range(head_size)])  4.02 us
    ppermute x5, waiting for transfers between devices, swap(): lax.ppermute(array, 'seq', [(i, i ^ 1 << bit) for i in range(seq_size)])  1.06 us
  transfers between devices with their start and end apart: 7, of which 3 were waited for; matrix products, arithmetic and copies ran while one was open for 0% of the time, Pallas kernels for 40%

profile of v3, /device:TPU:0, one launch (start us, length us, event | category | flops | bytes accessed | tf_op | source)
XLA Modules:
  0.0 48.7 jit_solution(14457014005660847860)
XLA Ops:
  0.0 7.1 %states.1 = (bf16[2048,2048]{1,0:T(8,128)(2,1)S(1)}, bf16[2048,2048]{1,0:T(8,128)(2,1)S(1)}, bf16[16,7,128,128]{3,2,1,0:T(8,128)(2,1)S(1)}, bf16[16,128,128]{2,1...) custom-call(s32[1]{0:T(128)} %bitcast.pos_ref, bf16[2048,2048]{1,0:T(8,128)(2,1)} %k_hbm.1, ...), custom_call_target="tpu_custom_call" | custom-call | flops 1073741824 | bytes 16777216 | tf_op jit(solution)/shard_map/states/pallas_call | solution.py:290
  7.1 0.5 %collective-permute-start = (bf16[16,128,128]{2,1,0:T(8,128)(2,1)S(1)}, bf16[16,128,128]{2,1,0:T(8,128)(2,1)S(1)}, u32[]{:S(2)}, u32[]{:S(2)}) collective-permute-start(bf16[16,128,128]{2,1,0:T(8,128)(2,1)S(1)} %get-tuple-element.25.mine_ref), channel_id=1, source_target_pairs={{0,4},{4,0},{8,12},{12,8},{16,20},{20,16},{24,28},{28,24},{1,5},{5... | collective-permute-start | bytes 1572872 | tf_op jit(solution)/shard_map/ppermute | solution.py:334
  7.6 2.2 %local.3 = (bf16[1,2048,256]{2,1,0:T(8,128)(2,1)S(1)}, bf16[1024,2048]{1,0:T(8,128)(2,1)S(1)}) custom-call(s32[1]{0:T(128)} %bitcast.pos_ref, bf16[256,2048]{1,0:T(8,128)(2,1)S(1)} %get-tuple-element.19.q_ref.refs_0_, bf16[2048,2048]{1,0:T(8,128)(2,1)S(1)} %get-tuple-element.20.k_ref, bf16[2048,2048]{1,0:T(8,128)(2,1)S(1)} %get-tuple-element.21.v_ref, ...), custom_call_target="tpu_custom_call" | custom-call | flops 2415919104 | tf_op jit(solution)/shard_map/local/pallas_call | solution.py:290
  9.8 0.0 collective-permute-done.refs_0_.received_ref.refs_7_
  9.8 0.1 sum.2.mine_ref
  9.9 2.6 %collective-permute-start.1 = (bf16[8,128,128]{2,1,0:T(8,128)(2,1)S(1)}, bf16[8,128,128]{2,1,0:T(8,128)(2,1)S(1)}, u32[]{:S(2)}, u32[]{:S(2)}) collective-permute-start(bf16[8,128,128]{2,1,0:T(8,128)(2,1)S(1)} %sum.2.mine_ref), channel_id=1, source_target_pairs={{0,8},{4,12},{8,0},{12,4},{16,24},{20,28},{24,16},{28,20},{1,9},{5... | collective-permute-start | bytes 786440 | tf_op jit(solution)/shard_map/ppermute | solution.py:334
  12.4 7.8 %local.4 = (bf16[4,2048,256]{2,1,0:T(8,128)(2,1)S(1)}, bf16[768,2048]{1,0:T(8,128)(2,1)S(1)}) custom-call(s32[1]{0:T(128)} %bitcast.pos_ref, bf16[1024,2048]{1,0:T(8,128)(2,1)S(1)} %get-tuple-element.24.q_ref.refs_1_, bf16[2048,2048]{1,0:T(8,128)(2,1)S(1)} %get-tuple-element.20.k_ref, bf16[2048,2048]{1,0:T(8,128)(2,1)S(1)} %get-tuple-element.21.v_ref, ...), custom_call_target="tpu_custom_call" | custom-call | flops 9663676416 | tf_op jit(solution)/shard_map/local/pallas_call | solution.py:290
  20.2 0.0 collective-permute-done.1.received_ref.refs_8_
  20.3 0.1 sum.3
  20.3 1.6 %collective-permute-start.2 = (bf16[8,128,128]{2,1,0:T(8,128)(2,1)S(1)}, bf16[8,128,128]{2,1,0:T(8,128)(2,1)S(1)}, u32[]{:S(2)}, u32[]{:S(2)}) collective-permute-start(bf16[8,128,128]{2,1,0:T(8,128)(2,1)S(1)} %sum.3), channel_id=1, source_target_pairs={{0,16},{4,20},{8,24},{12,28},{16,0},{20,4},{24,8},{28,12},{1,17},{... | collective-permute-start | bytes 786440 | tf_op jit(solution)/shard_map/ppermute | solution.py:334
  21.9 5.8 %local.5.refs_6_ = bf16[3,2048,256]{2,1,0:T(8,128)(2,1)S(1)} custom-call(s32[1]{0:T(128)} %bitcast.pos_ref, bf16[768,2048]{1,0:T(8,128)(2,1)S(1)} %get-tuple-element.26.q_ref.refs_2_, bf16[2048,2048]{1,0:T(8,128)(2,1)S(1)} %get-tuple-element.20.k_ref, bf16[2048,2048]{1,0:T(8,128)(2,1)S(1)} %get-tuple-element.21.v_ref, ...), custom_call_target="tpu_custom_call" | custom-call | flops 7247757312 | tf_op jit(solution)/shard_map/local/pallas_call | solution.py:290
  27.7 0.1 collective-permute-start.3
  27.8 1.1 %collective-permute-done.2.refs_9_ = bf16[8,128,128]{2,1,0:T(8,128)(2,1)S(1)} collective-permute-done((bf16[8,128,128]{2,1,0:T(8,128)(2,1)S(1)}, bf16[8,128,128]{2,1,0:T(8,128)(2,1)S(1)}, u32[]{:S(2)}, u32[]{:S(2)}) %collective-permute-start.2) | collective-permute-done | bytes 262176 | tf_op jit(solution)/shard_map/ppermute | solution.py:334
  28.8 0.0 collective-permute-start.4
  28.8 3.6 %across.2 = (bf16[2048,1024]{1,0:T(8,128)(2,1)S(1)}, f32[1,2048]{1,0:T(1,128)S(1)}) custom-call(s32[1]{0:T(128)} %bitcast.pos_ref, bf16[256,2048]{1,0:T(8,128)(2,1)S(1)} %get-tuple-element.19.q_ref.refs_0_, bf16[1024,2048]{1,0:T(8,128)(2,1)S(1)} %get-tuple-element.24.q_ref.refs_1_, bf16[768,2048]{1,0:T(8,128)(2,1)S(1)} %get-tuple-element.26.q_ref.refs_2_, ...), custom_call_target="tpu_custom_call" | custom-call | flops 6442450944 | tf_op jit(solution)/shard_map/across/pallas_call | solution.py:290
  32.4 0.0 collective-permute-done.3.refs_8_
  32.4 0.0 collective-permute-done.4.refs_9_
  32.4 0.0 copy-start
  32.5 3.6 %across.3 = (bf16[2048,1024]{1,0:T(8,128)(2,1)S(1)}, f32[1,2048]{1,0:T(1,128)S(1)}) custom-call(s32[1]{0:T(128)} %bitcast.pos_ref, bf16[256,2048]{1,0:T(8,128)(2,1)S(1)} %get-tuple-element.19.q_ref.refs_0_, bf16[1024,2048]{1,0:T(8,128)(2,1)S(1)} %get-tuple-element.24.q_ref.refs_1_, bf16[768,2048]{1,0:T(8,128)(2,1)S(1)} %get-tuple-element.26.q_ref.refs_2_, ...), custom_call_target="tpu_custom_call" | custom-call | flops 6442450944 | tf_op jit(solution)/shard_map/across/pallas_call | solution.py:290
  36.0 1.9 %collective-permute-start.5 = (f32[1,2048]{1,0:T(1,128)S(1)}, f32[1,2048]{1,0:T(1,128)S(1)}, u32[]{:S(2)}, u32[]{:S(2)}) collective-permute-start(f32[1,2048]{1,0:T(1,128)S(1)} %get-tuple-element.32), channel_id=1, source_target_pairs={{0,1},{1,0},{2,3},{3,2},{4,5},{5,4},{6,7},{7,6},{8,9},{9,8},{10,11... | collective-permute-start | bytes 24584 | tf_op jit(solution)/shard_map/ppermute | solution.py:410
  37.9 2.1 %collective-permute-done.5 = f32[1,2048]{1,0:T(1,128)S(1)} collective-permute-done((f32[1,2048]{1,0:T(1,128)S(1)}, f32[1,2048]{1,0:T(1,128)S(1)}, u32[]{:S(2)}, u32[]{:S(2)}) %collective-permute-start.5) | collective-permute-done | bytes 8224 | tf_op jit(solution)/shard_map/ppermute | solution.py:410
  40.0 2.7 %collective-permute-start.6 = (f32[1,2048]{1,0:T(1,128)S(1)}, f32[1,2048]{1,0:T(1,128)S(1)}, u32[]{:S(2)}, u32[]{:S(2)}) collective-permute-start(f32[1,2048]{1,0:T(1,128)S(1)} %add.3.square_ref), channel_id=1, source_target_pairs={{0,2},{1,3},{2,0},{3,1},{4,6},{5,7},{6,4},{7,5},{8,10},{9,11},{10,... | collective-permute-start | bytes 24584 | tf_op jit(solution)/shard_map/ppermute | solution.py:410
  42.7 2.0 %collective-permute-done.6.received_ref = f32[1,2048]{1,0:T(1,128)S(1)} collective-permute-done((f32[1,2048]{1,0:T(1,128)S(1)}, f32[1,2048]{1,0:T(1,128)S(1)}, u32[]{:S(2)}, u32[]{:S(2)}) %collective-permute-start.6) | collective-permute-done | bytes 8224 | tf_op jit(solution)/shard_map/ppermute | solution.py:410
  44.6 0.0 copy-done
  44.6 3.9 %norm.1 = bf16[2048,2048]{1,0:T(8,128)(2,1)} custom-call(s32[1]{0:T(128)} %bitcast.pos_ref, bf16[2048,1024]{1,0:T(8,128)(2,1)S(1)} %get-tuple-element.29.own_ref, bf16[2048,1024]{1,0:T(8,128)(2,1)S(1)} %get-tuple-element.31.other_ref, f32[1,2048]{1,0:T(1,128)S(1)} %bitcast.2, f32[1,2048]{1,0:T(1,128)S(1)} %add.3.square_ref, ...), custom_call_target="tpu_custom_call" | custom-call | flops 12582912 | bytes 8388608 | tf_op jit(solution)/shard_map/norm/pallas_call | solution.py:290
  (1 shorter events, 0.0 us)
Async XLA Ops:
  7.1 2.7 %collective-permute-start = (bf16[16,128,128]{2,1,0:T(8,128)(2,1)S(1)}, bf16[16,128,128]{2,1,0:T(8,128)(2,1)S(1)}, u32[]{:S(2)}, u32[]{:S(2)}) collective-permute-start(bf16[16,128,128]{2,1,0:T(8,128)(2,1)S(1)} %get-tuple-element.25.mine_ref), channel_id=1, source_target_pairs={{0,4},{4,0},{8,12},{12,8},{16,20},{20,16},{24,28},{28,24},{1,5},{5... | collective-permute-start | bytes 1572872 | tf_op jit(solution)/shard_map/ppermute | solution.py:334
  9.9 10.4 %collective-permute-start.1 = (bf16[8,128,128]{2,1,0:T(8,128)(2,1)S(1)}, bf16[8,128,128]{2,1,0:T(8,128)(2,1)S(1)}, u32[]{:S(2)}, u32[]{:S(2)}) collective-permute-start(bf16[8,128,128]{2,1,0:T(8,128)(2,1)S(1)} %sum.2.mine_ref), channel_id=1, source_target_pairs={{0,8},{4,12},{8,0},{12,4},{16,24},{20,28},{24,16},{28,20},{1,9},{5... | collective-permute-start | bytes 786440 | tf_op jit(solution)/shard_map/ppermute | solution.py:334
  20.3 8.5 %collective-permute-start.2 = (bf16[8,128,128]{2,1,0:T(8,128)(2,1)S(1)}, bf16[8,128,128]{2,1,0:T(8,128)(2,1)S(1)}, u32[]{:S(2)}, u32[]{:S(2)}) collective-permute-start(bf16[8,128,128]{2,1,0:T(8,128)(2,1)S(1)} %sum.3), channel_id=1, source_target_pairs={{0,16},{4,20},{8,24},{12,28},{16,0},{20,4},{24,8},{28,12},{1,17},{... | collective-permute-start | bytes 786440 | tf_op jit(solution)/shard_map/ppermute | solution.py:334
  27.7 4.7 %collective-permute-start.3 = (bf16[8,128,128]{2,1,0:T(8,128)(2,1)S(1)}, bf16[8,128,128]{2,1,0:T(8,128)(2,1)S(1)}, u32[]{:S(2)}, u32[]{:S(2)}) collective-permute-start(bf16[8,128,128]{2,1,0:T(8,128)(2,1)S(1)} %collective-permute-done.1.received_ref.refs_8_), channel_id=1, source_target_pairs={{0,4},{4,0},{8,12},{12,8},{16,20},{20,16},{24,28},{28,24},{1,5},{5... | collective-permute-start | bytes 786440 | tf_op jit(solution)/shard_map/ppermute | solution.py:334
  28.8 3.6 %collective-permute-start.4 = (bf16[8,128,128]{2,1,0:T(8,128)(2,1)S(1)}, bf16[8,128,128]{2,1,0:T(8,128)(2,1)S(1)}, u32[]{:S(2)}, u32[]{:S(2)}) collective-permute-start(bf16[8,128,128]{2,1,0:T(8,128)(2,1)S(1)} %collective-permute-done.2.refs_9_), channel_id=1, source_target_pairs={{0,4},{4,0},{8,12},{12,8},{16,20},{20,16},{24,28},{28,24},{1,5},{5... | collective-permute-start | bytes 786440 | tf_op jit(solution)/shard_map/ppermute | solution.py:334
  32.4 12.2 %copy-start = (f32[2048]{0:T(1024)S(1)}, f32[2048]{0:T(1024)}, u32[]{:S(2)}) copy-start(f32[2048]{0:T(1024)} %param.9) | copy-start | bytes 24580
  36.0 3.9 %collective-permute-start.5 = (f32[1,2048]{1,0:T(1,128)S(1)}, f32[1,2048]{1,0:T(1,128)S(1)}, u32[]{:S(2)}, u32[]{:S(2)}) collective-permute-start(f32[1,2048]{1,0:T(1,128)S(1)} %get-tuple-element.32), channel_id=1, source_target_pairs={{0,1},{1,0},{2,3},{3,2},{4,5},{5,4},{6,7},{7,6},{8,9},{9,8},{10,11... | collective-permute-start | bytes 24584 | tf_op jit(solution)/shard_map/ppermute | solution.py:410
  40.0 4.6 %collective-permute-start.6 = (f32[1,2048]{1,0:T(1,128)S(1)}, f32[1,2048]{1,0:T(1,128)S(1)}, u32[]{:S(2)}, u32[]{:S(2)}) collective-permute-start(f32[1,2048]{1,0:T(1,128)S(1)} %add.3.square_ref), channel_id=1, source_target_pairs={{0,2},{1,3},{2,0},{3,1},{4,6},{5,7},{6,4},{7,5},{8,10},{9,11},{10,... | collective-permute-start | bytes 24584 | tf_op jit(solution)/shard_map/ppermute | solution.py:410

commit v4 on v3

--- a/solution.py
+++ b/solution.py
@@ -109,6 +109,12 @@
     out_ref[...] = total.astype(BF16)
 
 
+def stack_kernel(*refs):
+    out_ref = refs[-1]
+    for b, ref in enumerate(refs[:-1]):
+        out_ref[b] = ref[...]
+
+
 def local_factors(w_ref, head, start):
     def row(level):
         return w_ref[head, level : level + 1, start : start + HALF] * SCALING
@@ -204,7 +210,8 @@
     q_refs = [refs.pop(0) for _ in spans]
     w_ref = refs.pop(0)
     in_refs = [refs.pop(0) for _ in spans]
-    state_refs = [refs.pop(0) for _ in range(bits)]
+    first_ref = refs.pop(0)
+    rest_ref = refs.pop(0) if bits > 1 else None
     mix_ref, square_ref = refs[-2:]
     half = w_ref.shape[0] // 2
     position = pos_ref[0]
@@ -215,7 +222,7 @@
         head = first + i
         states = []
         for b in range(bits):
-            state = state_refs[b][head if b == 0 else i]
+            state = first_ref[head] if b == 0 else rest_ref[b - 1, i]
             states.append(jnp.where((position >> b & 1) == 1, state, jnp.zeros_like(state)))
         for c in range(*part):
             s = [low <= c < high for low, high in spans].index(True)
@@ -242,8 +249,9 @@
 
 
 def norm_kernel(
-    width, pos_ref, own_ref, other_ref, gain_ref, square_ref, received_ref, out_hbm, out_ref, sems
+    width, pos_ref, own_ref, other_ref, gain_ref, *refs
 ):
+    *square_refs, out_hbm, out_ref, sems = refs
     rows, half = own_ref.shape
     own = (pos_ref[0] & 1) * half
     step = CHUNK // 2
@@ -254,7 +262,7 @@
         slot = pl.ds(i % slots * step, step)
         if i >= slots:
             copies[i - slots].wait()
-        square = square_ref[:, here] + received_ref[:, here]
+        square = sum(ref[:, here] for ref in square_refs)
         factor = lax.rsqrt(square / width + 1e-05)
         column = jnp.broadcast_to(factor, (GROUP, step)).T[:, :1]
         for mix_ref, first in ((own_ref, own), (other_ref, half - own)):
@@ -344,7 +352,7 @@
         )
 
     received = swap(block_state, 0)
-    own_buckets, other_buckets = [received], [received]
+    buckets = [received]
     running = block_state
     insides, query_parts = [], []
     for p, span in enumerate(spans):
@@ -354,7 +362,7 @@
         query_parts.append(query)
         operands = [position, query, keys, values, weight, local_states]
         if p > 0:
-            operands.append(own_buckets[0])
+            operands.append(buckets[0])
         in_specs = [scalar] + [WHOLE] * (len(operands) - 1)
         out_shape = [pltpu.VMEM((count, columns, CHUNK), BF16)]
         scratch = []
@@ -378,13 +386,22 @@
         if p + 1 < cross_bits:
             running = add(running, received, insides[-1], p == 0)
             received = swap(running, p + 1)
-            own_buckets.append(received)
-            other_buckets.append(swap(received, 0))
+            buckets.append(received)
     for b in range(len(spans) + 1, cross_bits):
         running = add(running, received, insides[-1], False)
         received = swap(running, b)
-        own_buckets.append(received)
-        other_buckets.append(swap(received, 0))
+        buckets.append(received)
+    own_buckets = other_buckets = buckets[:1]
+    if cross_bits > 1:
+        own = call(
+            stack_kernel,
+            "stack",
+            buckets[1:],
+            jax.ShapeDtypeStruct((cross_bits - 1, half, VALUE_DIM, HEAD_DIM), BF16),
+            in_specs=[WHOLE] * (cross_bits - 1),
+        )
+        own_buckets = buckets[:1] + [own]
+        other_buckets = buckets[:1] + [swap(own, 0)]
 
     shared = [position, *query_parts, weight, *insides]
 
@@ -402,17 +419,15 @@
 
     own_mix, square = across(True, shared + own_buckets)
     other_mix, square = across(False, shared + other_buckets + [square])
-    received = jnp.zeros_like(square)
-    bit = 1
-    while bit < head_size:
-        if bit > 1:
-            square = square + received
-        received = lax.ppermute(square, "head", [(i, i ^ bit) for i in range(head_size)])
-        bit *= 2
+    squares = [square]
+    for other in range(1, head_size):
+        squares.append(
+            lax.ppermute(square, "head", [(i, i ^ other) for i in range(head_size)])
+        )
     return call(
         functools.partial(norm_kernel, HEADS * VALUE_DIM),
         "norm",
-        [position, keep(own_mix), keep(other_mix), norm_gain.reshape(1, -1), square, received],
+        [position, keep(own_mix), keep(other_mix), norm_gain.reshape(1, -1), *squares],
         jax.ShapeDtypeStruct((rows, columns), BF16),
         flops=3 * rows * columns,
         size=2 * rows * columns,

time: 48.9 us -> 48.6 us (level)
    ppermute x2 -> x3, waiting for transfers between devices: 4.02 us -> 3.69 us  [body(): lax.ppermute(square, 'head', [(i, i ^ other) for i in range(head_size)])]
    ppermute x5 -> x4, waiting for transfers between devices: 1.06 us -> 1.14 us  [swap(): lax.ppermute(array, 'seq', [(i, i ^ 1 << bit) for i in range(seq_size)])]
    pallas_call x9 -> x10, Pallas kernels: 34 us -> 34 us  [call(): pl.pallas_call(kernel, name=name, in_specs=in_specs, out_shape=out_shape,...]
    ppermute x2 -> x3, starting transfers between devices: 4.53 us -> 4.53 us  [body(): lax.ppermute(square, 'head', [(i, i ^ other) for i in range(head_size)])]
    ppermute x5 -> x4, starting transfers between devices: 4.75 us -> 4.75 us  [swap(): lax.ppermute(array, 'seq', [(i, i ^ 1 << bit) for i in range(seq_size)])]
where the time goes in v4:
time: 48.6 us; the launch traced here: 48.4 us
  Pallas kernels  34 us (70%)
  starting transfers between devices  9.28 us (19%)
  waiting for transfers between devices  4.83 us (10%)
    pallas_call x10, Pallas kernels, call(): pl.pallas_call(kernel, name=name, in_specs=in_specs, out_shape=out_shape,...  34 us
    ppermute x4, starting transfers between devices, swap(): lax.ppermute(array, 'seq', [(i, i ^ 1 << bit) for i in range(seq_size)])  4.75 us
    ppermute x3, starting transfers between devices, body(): lax.ppermute(square, 'head', [(i, i ^ other) for i in range(head_size)])  4.53 us
    ppermute x3, waiting for transfers between devices, body(): lax.ppermute(square, 'head', [(i, i ^ other) for i in range(head_size)])  3.69 us
    ppermute x4, waiting for transfers between devices, swap(): lax.ppermute(array, 'seq', [(i, i ^ 1 << bit) for i in range(seq_size)])  1.14 us
  transfers between devices with their start and end apart: 7, of which 3 were waited for; matrix products, arithmetic and copies ran while one was open for 0% of the time, Pallas kernels for 40%

profile of v4, /device:TPU:0, one launch (start us, length us, event | category | flops | bytes accessed | tf_op | source)
XLA Modules:
  0.0 48.4 jit_solution(15558897412480388851)
XLA Ops:
  0.0 7.1 %states.1 = (bf16[2048,2048]{1,0:T(8,128)(2,1)S(1)}, bf16[2048,2048]{1,0:T(8,128)(2,1)S(1)}, bf16[16,7,128,128]{3,2,1,0:T(8,128)(2,1)S(1)}, bf16[16,128,128]{2,1...) custom-call(s32[1]{0:T(128)} %bitcast.pos_ref, bf16[2048,2048]{1,0:T(8,128)(2,1)} %k_hbm.1, ...), custom_call_target="tpu_custom_call" | custom-call | flops 1073741824 | bytes 16777216 | tf_op jit(solution)/shard_map/states/pallas_call | solution.py:298
  7.1 0.5 %collective-permute-start = (bf16[16,128,128]{2,1,0:T(8,128)(2,1)S(1)}, bf16[16,128,128]{2,1,0:T(8,128)(2,1)S(1)}, u32[]{:S(2)}, u32[]{:S(2)}) collective-permute-start(bf16[16,128,128]{2,1,0:T(8,128)(2,1)S(1)} %get-tuple-element.25.mine_ref), channel_id=1, source_target_pairs={{0,4},{4,0},{8,12},{12,8},{16,20},{20,16},{24,28},{28,24},{1,5},{5... | collective-permute-start | bytes 1572872 | tf_op jit(solution)/shard_map/ppermute | solution.py:342
  7.6 2.2 %local.3 = (bf16[1,2048,256]{2,1,0:T(8,128)(2,1)S(1)}, bf16[1024,2048]{1,0:T(8,128)(2,1)S(1)}) custom-call(s32[1]{0:T(128)} %bitcast.pos_ref, bf16[256,2048]{1,0:T(8,128)(2,1)S(1)} %get-tuple-element.19.q_ref.refs_0_, bf16[2048,2048]{1,0:T(8,128)(2,1)S(1)} %get-tuple-element.20.k_ref, bf16[2048,2048]{1,0:T(8,128)(2,1)S(1)} %get-tuple-element.21.v_ref, ...), custom_call_target="tpu_custom_call" | custom-call | flops 2415919104 | tf_op jit(solution)/shard_map/local/pallas_call | solution.py:298
  9.8 0.0 collective-permute-done.refs_0_.received_ref.refs_7_
  9.8 0.1 sum.2.mine_ref
  9.9 2.6 %collective-permute-start.1 = (bf16[8,128,128]{2,1,0:T(8,128)(2,1)S(1)}, bf16[8,128,128]{2,1,0:T(8,128)(2,1)S(1)}, u32[]{:S(2)}, u32[]{:S(2)}) collective-permute-start(bf16[8,128,128]{2,1,0:T(8,128)(2,1)S(1)} %sum.2.mine_ref), channel_id=1, source_target_pairs={{0,8},{4,12},{8,0},{12,4},{16,24},{20,28},{24,16},{28,20},{1,9},{5... | collective-permute-start | bytes 786440 | tf_op jit(solution)/shard_map/ppermute | solution.py:342
  12.4 7.8 %local.4 = (bf16[4,2048,256]{2,1,0:T(8,128)(2,1)S(1)}, bf16[768,2048]{1,0:T(8,128)(2,1)S(1)}) custom-call(s32[1]{0:T(128)} %bitcast.pos_ref, bf16[1024,2048]{1,0:T(8,128)(2,1)S(1)} %get-tuple-element.24.q_ref.refs_1_, bf16[2048,2048]{1,0:T(8,128)(2,1)S(1)} %get-tuple-element.20.k_ref, bf16[2048,2048]{1,0:T(8,128)(2,1)S(1)} %get-tuple-element.21.v_ref, ...), custom_call_target="tpu_custom_call" | custom-call | flops 9663676416 | tf_op jit(solution)/shard_map/local/pallas_call | solution.py:298
  20.2 0.0 collective-permute-done.1.received_ref.refs_0_
  20.2 0.1 sum.3
  20.3 1.6 %collective-permute-start.2 = (bf16[8,128,128]{2,1,0:T(8,128)(2,1)S(1)}, bf16[8,128,128]{2,1,0:T(8,128)(2,1)S(1)}, u32[]{:S(2)}, u32[]{:S(2)}) collective-permute-start(bf16[8,128,128]{2,1,0:T(8,128)(2,1)S(1)} %sum.3), channel_id=1, source_target_pairs={{0,16},{4,20},{8,24},{12,28},{16,0},{20,4},{24,8},{28,12},{1,17},{... | collective-permute-start | bytes 786440 | tf_op jit(solution)/shard_map/ppermute | solution.py:342
  21.9 5.8 %local.5.refs_6_ = bf16[3,2048,256]{2,1,0:T(8,128)(2,1)S(1)} custom-call(s32[1]{0:T(128)} %bitcast.pos_ref, bf16[768,2048]{1,0:T(8,128)(2,1)S(1)} %get-tuple-element.26.q_ref.refs_2_, bf16[2048,2048]{1,0:T(8,128)(2,1)S(1)} %get-tuple-element.20.k_ref, bf16[2048,2048]{1,0:T(8,128)(2,1)S(1)} %get-tuple-element.21.v_ref, ...), custom_call_target="tpu_custom_call" | custom-call | flops 7247757312 | tf_op jit(solution)/shard_map/local/pallas_call | solution.py:298
  27.7 1.1 %collective-permute-done.2.refs_1_ = bf16[8,128,128]{2,1,0:T(8,128)(2,1)S(1)} collective-permute-done((bf16[8,128,128]{2,1,0:T(8,128)(2,1)S(1)}, bf16[8,128,128]{2,1,0:T(8,128)(2,1)S(1)}, u32[]{:S(2)}, u32[]{:S(2)}) %collective-permute-start.2) | collective-permute-done | bytes 262176 | tf_op jit(solution)/shard_map/ppermute | solution.py:342
  28.8 0.1 collective-permute-start.3
  28.9 3.6 %across.2 = (bf16[2048,1024]{1,0:T(8,128)(2,1)S(1)}, f32[1,2048]{1,0:T(1,128)S(1)}) custom-call(s32[1]{0:T(128)} %bitcast.pos_ref, bf16[256,2048]{1,0:T(8,128)(2,1)S(1)} %get-tuple-element.19.q_ref.refs_0_, bf16[1024,2048]{1,0:T(8,128)(2,1)S(1)} %get-tuple-element.24.q_ref.refs_1_, bf16[768,2048]{1,0:T(8,128)(2,1)S(1)} %get-tuple-element.26.q_ref.refs_2_, ...), custom_call_target="tpu_custom_call" | custom-call | flops 6442450944 | tf_op jit(solution)/shard_map/across/pallas_call | solution.py:298
  32.5 0.0 collective-permute-done.3.refs_8_
  32.5 0.0 copy-start
  32.5 3.6 %across.3 = (bf16[2048,1024]{1,0:T(8,128)(2,1)S(1)}, f32[1,2048]{1,0:T(1,128)S(1)}) custom-call(s32[1]{0:T(128)} %bitcast.pos_ref, bf16[256,2048]{1,0:T(8,128)(2,1)S(1)} %get-tuple-element.19.q_ref.refs_0_, bf16[1024,2048]{1,0:T(8,128)(2,1)S(1)} %get-tuple-element.24.q_ref.refs_1_, bf16[768,2048]{1,0:T(8,128)(2,1)S(1)} %get-tuple-element.26.q_ref.refs_2_, ...), custom_call_target="tpu_custom_call" | custom-call | flops 6442450944 | tf_op jit(solution)/shard_map/across/pallas_call | solution.py:298
  36.1 3.7 %collective-permute-start.6 = (f32[1,2048]{1,0:T(1,128)S(1)}, f32[1,2048]{1,0:T(1,128)S(1)}, u32[]{:S(2)}, u32[]{:S(2)}) collective-permute-start(f32[1,2048]{1,0:T(1,128)S(1)} %get-tuple-element.32.refs_0_), channel_id=1, source_target_pairs={{0,3},{1,2},{2,1},{3,0},{4,7},{5,6},{6,5},{7,4},{8,11},{9,10},{10,... | collective-permute-start | bytes 24584 | tf_op jit(solution)/shard_map/ppermute | solution.py:425
  39.8 0.0 collective-permute-start.5
  39.8 0.9 %collective-permute-start.4 = (f32[1,2048]{1,0:T(1,128)S(1)}, f32[1,2048]{1,0:T(1,128)S(1)}, u32[]{:S(2)}, u32[]{:S(2)}) collective-permute-start(f32[1,2048]{1,0:T(1,128)S(1)} %get-tuple-element.32.refs_0_), channel_id=1, source_target_pairs={{0,1},{1,0},{2,3},{3,2},{4,5},{5,4},{6,7},{7,6},{8,9},{9,8},{10,11... | collective-permute-start | bytes 24584 | tf_op jit(solution)/shard_map/ppermute | solution.py:425
  40.7 1.0 %collective-permute-done.6.refs_3_ = f32[1,2048]{1,0:T(1,128)S(1)} collective-permute-done((f32[1,2048]{1,0:T(1,128)S(1)}, f32[1,2048]{1,0:T(1,128)S(1)}, u32[]{:S(2)}, u32[]{:S(2)}) %collective-permute-start.6) | collective-permute-done | bytes 8224 | tf_op jit(solution)/shard_map/ppermute | solution.py:425
  41.6 2.7 %collective-permute-done.5.refs_2_ = f32[1,2048]{1,0:T(1,128)S(1)} collective-permute-done((f32[1,2048]{1,0:T(1,128)S(1)}, f32[1,2048]{1,0:T(1,128)S(1)}, u32[]{:S(2)}, u32[]{:S(2)}) %collective-permute-start.5) | collective-permute-done | bytes 8224 | tf_op jit(solution)/shard_map/ppermute | solution.py:425
  44.4 0.0 collective-permute-done.4.refs_1_
  44.4 0.0 copy-done
  44.4 3.9 %norm.1 = bf16[2048,2048]{1,0:T(8,128)(2,1)} custom-call(s32[1]{0:T(128)} %bitcast.pos_ref, bf16[2048,1024]{1,0:T(8,128)(2,1)S(1)} %get-tuple-element.29.own_ref, bf16[2048,1024]{1,0:T(8,128)(2,1)S(1)} %get-tuple-element.31.other_ref, f32[1,2048]{1,0:T(1,128)S(1)} %bitcast.2, f32[1,2048]{1,0:T(1,128)S(1)} %get-tuple-element.32.refs_0_, ...), custom_call_target="tpu_custom_call" | custom-call | flops 12582912 | bytes 8388608 | tf_op jit(solution)/shard_map/norm/pallas_call | solution.py:298
  (1 shorter events, 0.0 us)
Async XLA Ops:
  7.1 2.7 %collective-permute-start = (bf16[16,128,128]{2,1,0:T(8,128)(2,1)S(1)}, bf16[16,128,128]{2,1,0:T(8,128)(2,1)S(1)}, u32[]{:S(2)}, u32[]{:S(2)}) collective-permute-start(bf16[16,128,128]{2,1,0:T(8,128)(2,1)S(1)} %get-tuple-element.25.mine_ref), channel_id=1, source_target_pairs={{0,4},{4,0},{8,12},{12,8},{16,20},{20,16},{24,28},{28,24},{1,5},{5... | collective-permute-start | bytes 1572872 | tf_op jit(solution)/shard_map/ppermute | solution.py:342
  9.9 10.3 %collective-permute-start.1 = (bf16[8,128,128]{2,1,0:T(8,128)(2,1)S(1)}, bf16[8,128,128]{2,1,0:T(8,128)(2,1)S(1)}, u32[]{:S(2)}, u32[]{:S(2)}) collective-permute-start(bf16[8,128,128]{2,1,0:T(8,128)(2,1)S(1)} %sum.2.mine_ref), channel_id=1, source_target_pairs={{0,8},{4,12},{8,0},{12,4},{16,24},{20,28},{24,16},{28,20},{1,9},{5... | collective-permute-start | bytes 786440 | tf_op jit(solution)/shard_map/ppermute | solution.py:342
  20.3 8.5 %collective-permute-start.2 = (bf16[8,128,128]{2,1,0:T(8,128)(2,1)S(1)}, bf16[8,128,128]{2,1,0:T(8,128)(2,1)S(1)}, u32[]{:S(2)}, u32[]{:S(2)}) collective-permute-start(bf16[8,128,128]{2,1,0:T(8,128)(2,1)S(1)} %sum.3), channel_id=1, source_target_pairs={{0,16},{4,20},{8,24},{12,28},{16,0},{20,4},{24,8},{28,12},{1,17},{... | collective-permute-start | bytes 786440 | tf_op jit(solution)/shard_map/ppermute | solution.py:342
  28.8 3.7 %collective-permute-start.3 = (bf16[2,8,128,128]{3,2,1,0:T(8,128)(2,1)S(1)}, bf16[2,8,128,128]{3,2,1,0:T(8,128)(2,1)S(1)}, u32[]{:S(2)}, u32[]{:S(2)}) collective-permute-start(bf16[2,8,128,128]{3,2,1,0:T(8,128)(2,1)S(1)} %stack.1.refs_8_), channel_id=1, source_target_pairs={{0,4},{4,0},{8,12},{12,8},{16,20},{20,16},{24,28},{28,24},{1,5},{5... | collective-permute-start | bytes 1572872 | tf_op jit(solution)/shard_map/ppermute | solution.py:342
  32.5 11.8 %copy-start = (f32[2048]{0:T(1024)S(1)}, f32[2048]{0:T(1024)}, u32[]{:S(2)}) copy-start(f32[2048]{0:T(1024)} %param.9) | copy-start | bytes 24580
  36.1 5.5 %collective-permute-start.6 = (f32[1,2048]{1,0:T(1,128)S(1)}, f32[1,2048]{1,0:T(1,128)S(1)}, u32[]{:S(2)}, u32[]{:S(2)}) collective-permute-start(f32[1,2048]{1,0:T(1,128)S(1)} %get-tuple-element.32.refs_0_), channel_id=1, source_target_pairs={{0,3},{1,2},{2,1},{3,0},{4,7},{5,6},{6,5},{7,4},{8,11},{9,10},{10,... | collective-permute-start | bytes 24584 | tf_op jit(solution)/shard_map/ppermute | solution.py:425
  39.8 4.6 %collective-permute-start.5 = (f32[1,2048]{1,0:T(1,128)S(1)}, f32[1,2048]{1,0:T(1,128)S(1)}, u32[]{:S(2)}, u32[]{:S(2)}) collective-permute-start(f32[1,2048]{1,0:T(1,128)S(1)} %get-tuple-element.32.refs_0_), channel_id=1, source_target_pairs={{0,2},{1,3},{2,0},{3,1},{4,6},{5,7},{6,4},{7,5},{8,10},{9,11},{10,... | collective-permute-start | bytes 24584 | tf_op jit(solution)/shard_map/ppermute | solution.py:425
  39.8 4.5 %collective-permute-start.4 = (f32[1,2048]{1,0:T(1,128)S(1)}, f32[1,2048]{1,0:T(1,128)S(1)}, u32[]{:S(2)}, u32[]{:S(2)}) collective-permute-start(f32[1,2048]{1,0:T(1,128)S(1)} %get-tuple-element.32.refs_0_), channel_id=1, source_target_pairs={{0,1},{1,0},{2,3},{3,2},{4,5},{5,4},{6,7},{7,6},{8,9},{9,8},{10,11... | collective-permute-start | bytes 24584 | tf_op jit(solution)/shard_map/ppermute | solution.py:425

commit v5 on v4

--- a/solution.py
+++ b/solution.py
@@ -141,34 +141,48 @@
     return jnp.concatenate(pieces, axis=0)
 
 
-def local_kernel(span, after, lag, first_level, pos_ref, q_ref, k_ref, v_ref, w_ref, local_ref, *refs):
+def local_kernel(
+    span, given, loads, lag, first_level, buckets, pos_ref, k_ref, v_ref, w_ref, local_ref, *refs
+):
     refs = list(refs)
     heads = w_ref.shape[0]
+    half = heads // 2
     depth_count = (k_ref.shape[0] // CHUNK).bit_length() - 1
     base_level = CHUNK.bit_length()
-    received_ref = refs.pop(0) if first_level is not None else None
-    copies = []
-    if after is not None:
-        q_hbm, out_ref, q_next, sem = refs
-        copies = [query_copy(after, q_hbm, q_next, sem)]
-        copies[0].start()
-    else:
-        (out_ref,) = refs
-    present = (pos_ref[0] & 1) == 1
-
-    def scores(c, h):
+    bucket_refs = [refs.pop(0) for _ in range(buckets)]
+    q_refs = {part: refs.pop(0) for part in given}
+    q_hbm = refs.pop(0) if loads else None
+    out_ref = refs.pop(0)
+    waits = []
+    for i, part in enumerate(loads):
+        q_refs[part] = refs.pop(0)
+        waits.append((part, query_copy(part, q_hbm, q_refs[part], refs[-1].at[i])))
+    position = pos_ref[0]
+    own = (position & 1) * half
+
+    def arrive():
+        waits.pop(0)[1].wait()
+        if waits:
+            waits[0][1].start()
+
+    if waits:
+        waits[0][1].start()
+
+    def scores(c, i, h):
         start = c * CHUNK
         depths = [d for d in range(depth_count) if c >> d & 1]
         stream = [k_ref[rows_of(c), columns_of(h)]]
         stream += [local_ref[h, bucket_slot(depth_count, d, c)] for d in depths]
         levels = [base_level + d for d in depths]
-        if received_ref is not None:
-            state = received_ref[h]
-            stream.append(jnp.where(present, state, jnp.zeros_like(state)))
-            levels.append(first_level)
-        result = dot(
-            jnp.concatenate(stream, axis=0), q_ref[rows_of(c - span[0]), columns_of(h)], TT
-        )
+        for b, ref in enumerate(bucket_refs):
+            if b == 0 or i < half:
+                state = ref[h] if b == 0 else ref[i]
+                present = (position >> b & 1) == 1
+                stream.append(jnp.where(present, state, jnp.zeros_like(state)))
+                levels.append(first_level + b)
+        part = next(p for p in q_refs if p[0] <= c < p[1])
+        query = q_refs[part][rows_of(c - part[0]), columns_of(h)]
+        result = dot(jnp.concatenate(stream, axis=0), query, TT)
         upper = (result[:HALF, :HALF] * local_factors(w_ref, h, start)).astype(BF16)
         lower = (result[HALF:CHUNK, HALF:] * local_factors(w_ref, h, start + HALF)).astype(BF16)
         middle_row = w_ref[h, 8:9, start + HALF : start + CHUNK] * SCALING
@@ -181,8 +195,8 @@
             axis=0,
         )
         total = None
-        for i, level in enumerate(levels):
-            piece = result[CHUNK + i * VALUE_DIM : CHUNK + (i + 1) * VALUE_DIM]
+        for n, level in enumerate(levels):
+            piece = result[CHUNK + n * VALUE_DIM : CHUNK + (n + 1) * VALUE_DIM]
             piece = piece * (w_ref[h, level : level + 1, start : start + CHUNK] * SCALING)
             total = piece if total is None else total + piece
         return weighted, total
@@ -195,19 +209,24 @@
 
     waiting = []
     for c in range(*span):
-        for h in range(heads):
-            waiting.append((c, h, *scores(c, h)))
+        while waits and waits[0][0][0] <= c:
+            arrive()
+        for i in range(heads):
+            h = i
+            if buckets > 1:
+                h = own + i if i < half else i - own
+            waiting.append((c, h, *scores(c, i, h)))
             if len(waiting) > lag:
                 values(*waiting.pop(0))
     for entry in waiting:
         values(*entry)
-    for copy in copies:
-        copy.wait()
-
-
-def across_kernel(mine, bits, first_level, spans, part, pos_ref, *refs):
+    while waits:
+        arrive()
+
+
+def across_kernel(mine, bits, done, first_level, spans, parts, part, pos_ref, *refs):
     refs = list(refs)
-    q_refs = [refs.pop(0) for _ in spans]
+    q_refs = {p: refs.pop(0) for p in parts}
     w_ref = refs.pop(0)
     in_refs = [refs.pop(0) for _ in spans]
     first_ref = refs.pop(0)
@@ -228,11 +247,12 @@
             s = [low <= c < high for low, high in spans].index(True)
             local = c - spans[s][0]
             start = c * CHUNK
-            used = range(0 if s == 0 else 1, bits)
+            used = range(done[s] if mine else min(done[s], 1), bits)
+            place = next(p for p in parts if p[0] <= c < p[1])
             total = in_refs[s][local, columns_of(head), :].astype(jnp.float32)
             if len(used):
                 stream = jnp.concatenate([states[b] for b in used], axis=0)
-                result = dot(stream, q_refs[s][rows_of(local), columns_of(head)], TT)
+                result = dot(stream, q_refs[place][rows_of(c - place[0]), columns_of(head)], TT)
                 for n, b in enumerate(used):
                     level = first_level + b
                     row = w_ref[head, level : level + 1, start : start + CHUNK] * SCALING
@@ -309,6 +329,10 @@
 
     cuts = sorted({0, chunks // 8, chunks * 5 // 8, chunks})
     spans = list(zip(cuts[:-1], cuts[1:]))
+    middle = (spans[1][0] + spans[1][1]) // 2
+    parts = [spans[0], (spans[1][0], middle), (middle, spans[1][1]), spans[2]]
+    plan = [(parts[:1], parts[1:2]), (parts[1:2], parts[2:]), (parts[3:], [])]
+    done = [0, 1, min(2, cross_bits)]
 
     def query_shape(span):
         return pltpu.VMEM(((span[1] - span[0]) * CHUNK, columns), BF16)
@@ -354,25 +378,23 @@
     received = swap(block_state, 0)
     buckets = [received]
     running = block_state
-    insides, query_parts = [], []
+    insides = []
+    held = {parts[0]: keep(query)}
     for p, span in enumerate(spans):
         count = span[1] - span[0]
-        after = spans[p + 1] if p + 1 < len(spans) else None
-        query = keep(query)
-        query_parts.append(query)
-        operands = [position, query, keys, values, weight, local_states]
-        if p > 0:
-            operands.append(buckets[0])
+        given, loads = plan[p]
+        operands = [position, keys, values, weight, local_states]
+        operands += buckets[: done[p]] + [held[part] for part in given]
         in_specs = [scalar] + [WHOLE] * (len(operands) - 1)
         out_shape = [pltpu.VMEM((count, columns, CHUNK), BF16)]
         scratch = []
-        if after is not None:
+        if loads:
             operands.append(queries)
             in_specs.append(ANYWHERE)
-            out_shape.append(query_shape(after))
-            scratch = [pltpu.SemaphoreType.DMA(())]
+            out_shape += [query_shape(part) for part in loads]
+            scratch = [pltpu.SemaphoreType.DMA((len(loads),))]
         results = call(
-            functools.partial(local_kernel, span, after, 2, first_level if p else None),
+            functools.partial(local_kernel, span, given, loads, 2, first_level, done[p]),
             "local",
             operands,
             out_shape,
@@ -381,8 +403,7 @@
             scratch_shapes=scratch,
         )
         insides.append(keep(results[0]))
-        if after is not None:
-            query = results[1]
+        held.update((part, keep(array)) for part, array in zip(loads, results[1:]))
         if p + 1 < cross_bits:
             running = add(running, received, insides[-1], p == 0)
             received = swap(running, p + 1)
@@ -403,11 +424,13 @@
         own_buckets = buckets[:1] + [own]
         other_buckets = buckets[:1] + [swap(own, 0)]
 
-    shared = [position, *query_parts, weight, *insides]
+    shared = [position, *[held[part] for part in parts], weight, *insides]
 
     def across(mine, operands):
         return call(
-            functools.partial(across_kernel, mine, cross_bits, first_level, spans, (0, chunks)),
+            functools.partial(
+                across_kernel, mine, cross_bits, done, first_level, spans, parts, (0, chunks)
+            ),
             "across",
             operands,
             [

time: 48.6 us -> 48.3 us (level)
  Pallas kernels: 34 us -> 32.7 us
  waiting for transfers between devices: 4.83 us -> 5.51 us
    ppermute x3, waiting for transfers between devices: 3.69 us -> 5.22 us  [body(): lax.ppermute(square, 'head', [(i, i ^ other) for i in range(head_size)])]
    pallas_call x10, Pallas kernels: 34 us -> 32.7 us  [call(): pl.pallas_call(kernel, name=name, in_specs=in_specs, out_shape=out_shape,...]
    ppermute x4, waiting for transfers between devices: 1.14 us -> 0.29 us  [swap(): lax.ppermute(array, 'seq', [(i, i ^ 1 << bit) for i in range(seq_size)])]
    ppermute x4, starting transfers between devices: 4.75 us -> 5.26 us  [swap(): lax.ppermute(array, 'seq', [(i, i ^ 1 << bit) for i in range(seq_size)])]
  transfers between devices with their start and end apart: 7 -> 7, of which waited for: 3 -> 3; matrix products, arithmetic and copies ran while one was open for 0% -> 0% of each run, Pallas kernels for 40% -> 37%
where the time goes in v5:
time: 48.3 us; the launch traced here: 48.2 us
  Pallas kernels  32.7 us (68%)
  starting transfers between devices  9.71 us (20%)
  waiting for transfers between devices  5.51 us (11%)
    pallas_call x10, Pallas kernels, call(): pl.pallas_call(kernel, name=name, in_specs=in_specs, out_shape=out_shape,...  32.7 us
    ppermute x4, starting transfers between devices, swap(): lax.ppermute(array, 'seq', [(i, i ^ 1 << bit) for i in range(seq_size)])  5.26 us
    ppermute x3, waiting for transfers between devices, body(): lax.ppermute(square, 'head', [(i, i ^ other) for i in range(head_size)])  5.22 us
    ppermute x3, starting transfers between devices, body(): lax.ppermute(square, 'head', [(i, i ^ other) for i in range(head_size)])  4.45 us
  transfers between devices with their start and end apart: 7, of which 3 were waited for; matrix products, arithmetic and copies ran while one was open for 0% of the time, Pallas kernels for 37%

profile of v5, /device:TPU:0, one launch (start us, length us, event | category | flops | bytes accessed | tf_op | source)
XLA Modules:
  0.0 48.2 jit_solution(9223619147248455955)
XLA Ops:
  0.0 7.1 %states.1 = (bf16[2048,2048]{1,0:T(8,128)(2,1)S(1)}, bf16[2048,2048]{1,0:T(8,128)(2,1)S(1)}, bf16[16,7,128,128]{3,2,1,0:T(8,128)(2,1)S(1)}, bf16[16,128,128]{2,1...) custom-call(s32[1]{0:T(128)} %bitcast.pos_ref, bf16[2048,2048]{1,0:T(8,128)(2,1)} %k_hbm.1, ...), custom_call_target="tpu_custom_call" | custom-call | flops 1073741824 | bytes 16777216 | tf_op jit(solution)/shard_map/states/pallas_call | solution.py:318
  7.1 0.5 %collective-permute-start = (bf16[16,128,128]{2,1,0:T(8,128)(2,1)S(1)}, bf16[16,128,128]{2,1,0:T(8,128)(2,1)S(1)}, u32[]{:S(2)}, u32[]{:S(2)}) collective-permute-start(bf16[16,128,128]{2,1,0:T(8,128)(2,1)S(1)} %get-tuple-element.26.mine_ref), channel_id=1, source_target_pairs={{0,4},{4,0},{8,12},{12,8},{16,20},{20,16},{24,28},{28,24},{1,5},{5... | collective-permute-start | bytes 1572872 | tf_op jit(solution)/shard_map/ppermute | solution.py:366
  7.6 1.6 %local.3 = (bf16[1,2048,256]{2,1,0:T(8,128)(2,1)S(1)}, bf16[512,2048]{1,0:T(8,128)(2,1)S(1)}) custom-call(s32[1]{0:T(128)} %bitcast.pos_ref, bf16[2048,2048]{1,0:T(8,128)(2,1)S(1)} %get-tuple-element.21.k_ref, bf16[2048,2048]{1,0:T(8,128)(2,1)S(1)} %get-tuple-element.22.v_ref, f32[16,16,2048]{2,1,0:T(8,128)S(1)} %get-tuple-element.23.w_ref.refs_4_, ...), custom_call_target="tpu_custom_call" | custom-call | flops 2415919104 | tf_op jit(solution)/shard_map/local/pallas_call | solution.py:318
  9.2 0.0 collective-permute-done.refs_0_.received_ref.refs_8_
  9.2 0.1 sum.2.mine_ref
  9.3 2.8 %collective-permute-start.1 = (bf16[8,128,128]{2,1,0:T(8,128)(2,1)S(1)}, bf16[8,128,128]{2,1,0:T(8,128)(2,1)S(1)}, u32[]{:S(2)}, u32[]{:S(2)}) collective-permute-start(bf16[8,128,128]{2,1,0:T(8,128)(2,1)S(1)} %sum.2.mine_ref), channel_id=1, source_target_pairs={{0,8},{4,12},{8,0},{12,4},{16,24},{20,28},{24,16},{28,20},{1,9},{5... | collective-permute-start | bytes 786440 | tf_op jit(solution)/shard_map/ppermute | solution.py:366
  12.1 6.4 %local.4 = (bf16[4,2048,256]{2,1,0:T(8,128)(2,1)S(1)}, bf16[512,2048]{1,0:T(8,128)(2,1)S(1)}, bf16[768,2048]{1,0:T(8,128)(2,1)S(1)}) custom-call(s32[1]{0:T(128)} %bitcast.pos_ref, bf16[2048,2048]{1,0:T(8,128)(2,1)S(1)} %get-tuple-element.21.k_ref, bf16[2048,2048]{1,0:T(8,128)(2,1)S(1)} %get-tuple-element.22.v_ref, ...), custom_call_target="tpu_custom_call" | custom-call | flops 9663676416 | tf_op jit(solution)/shard_map/local/pallas_call | solution.py:318
  18.5 0.3 collective-permute-done.1.refs_1_.received_ref.refs_0_
  18.8 0.1 sum.3
  18.9 1.8 %collective-permute-start.2 = (bf16[8,128,128]{2,1,0:T(8,128)(2,1)S(1)}, bf16[8,128,128]{2,1,0:T(8,128)(2,1)S(1)}, u32[]{:S(2)}, u32[]{:S(2)}) collective-permute-start(bf16[8,128,128]{2,1,0:T(8,128)(2,1)S(1)} %sum.3), channel_id=1, source_target_pairs={{0,16},{4,20},{8,24},{12,28},{16,0},{20,4},{24,8},{28,12},{1,17},{... | collective-permute-start | bytes 786440 | tf_op jit(solution)/shard_map/ppermute | solution.py:366
  20.7 6.3 %local.5.refs_7_ = bf16[3,2048,256]{2,1,0:T(8,128)(2,1)S(1)} custom-call(s32[1]{0:T(128)} %bitcast.pos_ref, bf16[2048,2048]{1,0:T(8,128)(2,1)S(1)} %get-tuple-element.21.k_ref, bf16[2048,2048]{1,0:T(8,128)(2,1)S(1)} %get-tuple-element.22.v_ref, f32[16,16,2048]{2,1,0:T(8,128)S(1)} %get-tuple-element.23.w_ref.refs_4_, ...), custom_call_target="tpu_custom_call" | custom-call | flops 7247757312 | tf_op jit(solution)/shard_map/local/pallas_call | solution.py:318
  27.0 0.0 collective-permute-done.2.refs_1_
  27.0 0.1 collective-permute-start.3
  27.1 3.5 %across.2 = (bf16[2048,1024]{1,0:T(8,128)(2,1)S(1)}, f32[1,2048]{1,0:T(1,128)S(1)}) custom-call(s32[1]{0:T(128)} %bitcast.pos_ref, bf16[256,2048]{1,0:T(8,128)(2,1)S(1)} %get-tuple-element.20.refs_0_, bf16[512,2048]{1,0:T(8,128)(2,1)S(1)} %get-tuple-element.25.refs_1_, bf16[512,2048]{1,0:T(8,128)(2,1)S(1)} %get-tuple-element.27.refs_2_, ...), custom_call_target="tpu_custom_call" | custom-call | flops 6442450944 | tf_op jit(solution)/shard_map/across/pallas_call | solution.py:318
  30.6 0.0 collective-permute-done.3.refs_9_
  30.6 0.0 copy-start
  30.6 3.8 %across.3 = (bf16[2048,1024]{1,0:T(8,128)(2,1)S(1)}, f32[1,2048]{1,0:T(1,128)S(1)}) custom-call(s32[1]{0:T(128)} %bitcast.pos_ref, bf16[256,2048]{1,0:T(8,128)(2,1)S(1)} %get-tuple-element.20.refs_0_, bf16[512,2048]{1,0:T(8,128)(2,1)S(1)} %get-tuple-element.25.refs_1_, bf16[512,2048]{1,0:T(8,128)(2,1)S(1)} %get-tuple-element.27.refs_2_, ...), custom_call_target="tpu_custom_call" | custom-call | flops 6442450944 | tf_op jit(solution)/shard_map/across/pallas_call | solution.py:318
  34.5 1.6 %collective-permute-start.4 = (f32[1,2048]{1,0:T(1,128)S(1)}, f32[1,2048]{1,0:T(1,128)S(1)}, u32[]{:S(2)}, u32[]{:S(2)}) collective-permute-start(f32[1,2048]{1,0:T(1,128)S(1)} %get-tuple-element.34.refs_0_), channel_id=1, source_target_pairs={{0,1},{1,0},{2,3},{3,2},{4,5},{5,4},{6,7},{7,6},{8,9},{9,8},{10,11... | collective-permute-start | bytes 24584 | tf_op jit(solution)/shard_map/ppermute | solution.py:448
  36.1 2.6 %collective-permute-start.5 = (f32[1,2048]{1,0:T(1,128)S(1)}, f32[1,2048]{1,0:T(1,128)S(1)}, u32[]{:S(2)}, u32[]{:S(2)}) collective-permute-start(f32[1,2048]{1,0:T(1,128)S(1)} %get-tuple-element.34.refs_0_), channel_id=1, source_target_pairs={{0,2},{1,3},{2,0},{3,1},{4,6},{5,7},{6,4},{7,5},{8,10},{9,11},{10,... | collective-permute-start | bytes 24584 | tf_op jit(solution)/shard_map/ppermute | solution.py:448
  38.7 0.2 collective-permute-start.6
  38.9 0.0 collective-permute-done.4.refs_1_
  38.9 1.7 %collective-permute-done.5.refs_2_ = f32[1,2048]{1,0:T(1,128)S(1)} collective-permute-done((f32[1,2048]{1,0:T(1,128)S(1)}, f32[1,2048]{1,0:T(1,128)S(1)}, u32[]{:S(2)}, u32[]{:S(2)}) %collective-permute-start.5) | collective-permute-done | bytes 8224 | tf_op jit(solution)/shard_map/ppermute | solution.py:448
  40.6 3.5 %collective-permute-done.6.refs_3_ = f32[1,2048]{1,0:T(1,128)S(1)} collective-permute-done((f32[1,2048]{1,0:T(1,128)S(1)}, f32[1,2048]{1,0:T(1,128)S(1)}, u32[]{:S(2)}, u32[]{:S(2)}) %collective-permute-start.6) | collective-permute-done | bytes 8224 | tf_op jit(solution)/shard_map/ppermute | solution.py:448
  44.1 0.0 copy-done
  44.1 3.9 %norm.1 = bf16[2048,2048]{1,0:T(8,128)(2,1)} custom-call(s32[1]{0:T(128)} %bitcast.pos_ref, bf16[2048,1024]{1,0:T(8,128)(2,1)S(1)} %get-tuple-element.31.own_ref, bf16[2048,1024]{1,0:T(8,128)(2,1)S(1)} %get-tuple-element.33.other_ref, f32[1,2048]{1,0:T(1,128)S(1)} %bitcast.2, f32[1,2048]{1,0:T(1,128)S(1)} %get-tuple-element.34.refs_0_, ...), custom_call_target="tpu_custom_call" | custom-call | flops 12582912 | bytes 8388608 | tf_op jit(solution)/shard_map/norm/pallas_call | solution.py:318
  (1 shorter events, 0.0 us)
Async XLA Ops:
  7.1 2.1 %collective-permute-start = (bf16[16,128,128]{2,1,0:T(8,128)(2,1)S(1)}, bf16[16,128,128]{2,1,0:T(8,128)(2,1)S(1)}, u32[]{:S(2)}, u32[]{:S(2)}) collective-permute-start(bf16[16,128,128]{2,1,0:T(8,128)(2,1)S(1)} %get-tuple-element.26.mine_ref), channel_id=1, source_target_pairs={{0,4},{4,0},{8,12},{12,8},{16,20},{20,16},{24,28},{28,24},{1,5},{5... | collective-permute-start | bytes 1572872 | tf_op jit(solution)/shard_map/ppermute | solution.py:366
  9.3 9.5 %collective-permute-start.1 = (bf16[8,128,128]{2,1,0:T(8,128)(2,1)S(1)}, bf16[8,128,128]{2,1,0:T(8,128)(2,1)S(1)}, u32[]{:S(2)}, u32[]{:S(2)}) collective-permute-start(bf16[8,128,128]{2,1,0:T(8,128)(2,1)S(1)} %sum.2.mine_ref), channel_id=1, source_target_pairs={{0,8},{4,12},{8,0},{12,4},{16,24},{20,28},{24,16},{28,20},{1,9},{5... | collective-permute-start | bytes 786440 | tf_op jit(solution)/shard_map/ppermute | solution.py:366
  18.9 8.1 %collective-permute-start.2 = (bf16[8,128,128]{2,1,0:T(8,128)(2,1)S(1)}, bf16[8,128,128]{2,1,0:T(8,128)(2,1)S(1)}, u32[]{:S(2)}, u32[]{:S(2)}) collective-permute-start(bf16[8,128,128]{2,1,0:T(8,128)(2,1)S(1)} %sum.3), channel_id=1, source_target_pairs={{0,16},{4,20},{8,24},{12,28},{16,0},{20,4},{24,8},{28,12},{1,17},{... | collective-permute-start | bytes 786440 | tf_op jit(solution)/shard_map/ppermute | solution.py:366
  27.0 3.6 %collective-permute-start.3 = (bf16[2,8,128,128]{3,2,1,0:T(8,128)(2,1)S(1)}, bf16[2,8,128,128]{3,2,1,0:T(8,128)(2,1)S(1)}, u32[]{:S(2)}, u32[]{:S(2)}) collective-permute-start(bf16[2,8,128,128]{3,2,1,0:T(8,128)(2,1)S(1)} %stack.1.refs_9_), channel_id=1, source_target_pairs={{0,4},{4,0},{8,12},{12,8},{16,20},{20,16},{24,28},{28,24},{1,5},{5... | collective-permute-start | bytes 1572872 | tf_op jit(solution)/shard_map/ppermute | solution.py:366
  30.6 13.5 %copy-start = (f32[2048]{0:T(1024)S(1)}, f32[2048]{0:T(1024)}, u32[]{:S(2)}) copy-start(f32[2048]{0:T(1024)} %param.9) | copy-start | bytes 24580
  34.5 4.5 %collective-permute-start.4 = (f32[1,2048]{1,0:T(1,128)S(1)}, f32[1,2048]{1,0:T(1,128)S(1)}, u32[]{:S(2)}, u32[]{:S(2)}) collective-permute-start(f32[1,2048]{1,0:T(1,128)S(1)} %get-tuple-element.34.refs_0_), channel_id=1, source_target_pairs={{0,1},{1,0},{2,3},{3,2},{4,5},{5,4},{6,7},{7,6},{8,9},{9,8},{10,11... | collective-permute-start | bytes 24584 | tf_op jit(solution)/shard_map/ppermute | solution.py:448
  36.1 4.5 %collective-permute-start.5 = (f32[1,2048]{1,0:T(1,128)S(1)}, f32[1,2048]{1,0:T(1,128)S(1)}, u32[]{:S(2)}, u32[]{:S(2)}) collective-permute-start(f32[1,2048]{1,0:T(1,128)S(1)} %get-tuple-element.34.refs_0_), channel_id=1, source_target_pairs={{0,2},{1,3},{2,0},{3,1},{4,6},{5,7},{6,4},{7,5},{8,10},{9,11},{10,... | collective-permute-start | bytes 24584 | tf_op jit(solution)/shard_map/ppermute | solution.py:448
  38.7 5.4 %collective-permute-start.6 = (f32[1,2048]{1,0:T(1,128)S(1)}, f32[1,2048]{1,0:T(1,128)S(1)}, u32[]{:S(2)}, u32[]{:S(2)}) collective-permute-start(f32[1,2048]{1,0:T(1,128)S(1)} %get-tuple-element.34.refs_0_), channel_id=1, source_target_pairs={{0,3},{1,2},{2,1},{3,0},{4,7},{5,6},{6,5},{7,4},{8,11},{9,10},{10,... | collective-permute-start | bytes 24584 | tf_op jit(solution)/shard_map/ppermute | solution.py:448

commit v6 on v5

--- a/solution.py
+++ b/solution.py
@@ -71,7 +71,7 @@
             copy.start()
         copies.append(pair)
     more = [
-        pltpu.make_async_copy(w_hbm, w_ref, more_sems.at[0]),
+        weight_copy((0, w_ref.shape[2] // CHUNK), w_hbm, w_ref, more_sems.at[0]),
         query_copy(span, q_hbm, q_ref, more_sems.at[1]),
     ]
     for c in range(chunks):
@@ -101,6 +101,16 @@
     return pltpu.make_async_copy(q_hbm.at[here], q_ref, sem)
 
 
+def weight_copy(span, w_hbm, w_ref, sem):
+    here = pl.ds(span[0] * CHUNK, (span[1] - span[0]) * CHUNK)
+    return pltpu.make_async_copy(w_hbm.at[:, :, here], w_ref, sem)
+
+
+def weights_at(w_refs, chunk):
+    part = next(p for p in w_refs if p[0] <= chunk < p[1])
+    return w_refs[part], (chunk - part[0]) * CHUNK
+
+
 def sum_kernel(whole, pos_ref, mine_ref, received_ref, after_ref, out_ref):
     del after_ref
     half = out_ref.shape[0]
@@ -142,21 +152,28 @@
 
 
 def local_kernel(
-    span, given, loads, lag, first_level, buckets, pos_ref, k_ref, v_ref, w_ref, local_ref, *refs
+    span, given, loads, w_given, w_loads, lag, first_level, buckets,
+    pos_ref, k_ref, v_ref, local_ref, *refs,
 ):
     refs = list(refs)
-    heads = w_ref.shape[0]
+    heads = local_ref.shape[0]
     half = heads // 2
     depth_count = (k_ref.shape[0] // CHUNK).bit_length() - 1
     base_level = CHUNK.bit_length()
     bucket_refs = [refs.pop(0) for _ in range(buckets)]
     q_refs = {part: refs.pop(0) for part in given}
+    w_refs = {part: refs.pop(0) for part in w_given}
     q_hbm = refs.pop(0) if loads else None
+    w_hbm = refs.pop(0) if w_loads else None
     out_ref = refs.pop(0)
     waits = []
     for i, part in enumerate(loads):
         q_refs[part] = refs.pop(0)
         waits.append((part, query_copy(part, q_hbm, q_refs[part], refs[-1].at[i])))
+    for part in w_loads:
+        w_refs[part] = refs.pop(0)
+        copy = weight_copy(part, w_hbm, w_refs[part], refs[-1].at[len(waits)])
+        waits.insert(1, (part, copy))
     position = pos_ref[0]
     own = (position & 1) * half
 
@@ -169,7 +186,7 @@
         waits[0][1].start()
 
     def scores(c, i, h):
-        start = c * CHUNK
+        w_ref, start = weights_at(w_refs, c)
         depths = [d for d in range(depth_count) if c >> d & 1]
         stream = [k_ref[rows_of(c), columns_of(h)]]
         stream += [local_ref[h, bucket_slot(depth_count, d, c)] for d in depths]
@@ -224,15 +241,15 @@
         arrive()
 
 
-def across_kernel(mine, bits, done, first_level, spans, parts, part, pos_ref, *refs):
+def across_kernel(mine, bits, done, first_level, spans, parts, w_parts, part, pos_ref, *refs):
     refs = list(refs)
     q_refs = {p: refs.pop(0) for p in parts}
-    w_ref = refs.pop(0)
+    w_refs = {p: refs.pop(0) for p in w_parts}
     in_refs = [refs.pop(0) for _ in spans]
     first_ref = refs.pop(0)
     rest_ref = refs.pop(0) if bits > 1 else None
     mix_ref, square_ref = refs[-2:]
-    half = w_ref.shape[0] // 2
+    half = w_refs[w_parts[0]].shape[0] // 2
     position = pos_ref[0]
     own = (position & 1) * half
     first = own if mine else half - own
@@ -246,7 +263,7 @@
         for c in range(*part):
             s = [low <= c < high for low, high in spans].index(True)
             local = c - spans[s][0]
-            start = c * CHUNK
+            w_ref, start = weights_at(w_refs, c)
             used = range(done[s] if mine else min(done[s], 1), bits)
             place = next(p for p in parts if p[0] <= c < p[1])
             total = in_refs[s][local, columns_of(head), :].astype(jnp.float32)
@@ -332,7 +349,12 @@
     middle = (spans[1][0] + spans[1][1]) // 2
     parts = [spans[0], (spans[1][0], middle), (middle, spans[1][1]), spans[2]]
     plan = [(parts[:1], parts[1:2]), (parts[1:2], parts[2:]), (parts[3:], [])]
+    w_parts = [(0, middle), (middle, chunks)]
+    w_plan = [(w_parts[:1], []), (w_parts[:1], w_parts[1:]), (w_parts[1:], [])]
     done = [0, 1, min(2, cross_bits)]
+
+    def weight_shape(span):
+        return pltpu.VMEM((heads, levels, (span[1] - span[0]) * CHUNK), jnp.float32)
 
     def query_shape(span):
         return pltpu.VMEM(((span[1] - span[0]) * CHUNK, columns), BF16)
@@ -349,7 +371,7 @@
             pltpu.VMEM((heads, chunks - 1, VALUE_DIM, HEAD_DIM), BF16),
             jax.ShapeDtypeStruct((heads, VALUE_DIM, HEAD_DIM), BF16),
         ]
-        + [query_shape(spans[0]), pltpu.VMEM((heads, levels, rows), jnp.float32)],
+        + [query_shape(spans[0]), weight_shape(w_parts[0])],
         flops=chunks * per_chunk,
         size=4 * rows * columns,
         in_specs=[scalar] + [ANYWHERE] * 4,
@@ -359,7 +381,7 @@
             pltpu.SemaphoreType.DMA((2,)),
         ],
     )
-    weight = keep(weight)
+    weights = {w_parts[0]: keep(weight)}
     keys, values, local_states = keep(keys), keep(values), keep(local_states)
 
     def swap(array, bit):
@@ -383,8 +405,10 @@
     for p, span in enumerate(spans):
         count = span[1] - span[0]
         given, loads = plan[p]
-        operands = [position, keys, values, weight, local_states]
+        w_given, w_loads = w_plan[p]
+        operands = [position, keys, values, local_states]
         operands += buckets[: done[p]] + [held[part] for part in given]
+        operands += [weights[part] for part in w_given]
         in_specs = [scalar] + [WHOLE] * (len(operands) - 1)
         out_shape = [pltpu.VMEM((count, columns, CHUNK), BF16)]
         scratch = []
@@ -392,9 +416,15 @@
             operands.append(queries)
             in_specs.append(ANYWHERE)
             out_shape += [query_shape(part) for part in loads]
-            scratch = [pltpu.SemaphoreType.DMA((len(loads),))]
+            if w_loads:
+                operands.append(level_weights)
+                in_specs.append(ANYWHERE)
+                out_shape += [weight_shape(part) for part in w_loads]
+            scratch = [pltpu.SemaphoreType.DMA((len(loads) + len(w_loads),))]
         results = call(
-            functools.partial(local_kernel, span, given, loads, 2, first_level, done[p]),
+            functools.partial(
+                local_kernel, span, given, loads, w_given, w_loads, 2, first_level, done[p]
+            ),
             "local",
             operands,
             out_shape,
@@ -403,7 +433,9 @@
             scratch_shapes=scratch,
         )
         insides.append(keep(results[0]))
-        held.update((part, keep(array)) for part, array in zip(loads, results[1:]))
+        arrays = [keep(array) for array in results[1:]]
+        held.update(zip(loads, arrays))
+        weights.update(zip(w_loads, arrays[len(loads) :]))
         if p + 1 < cross_bits:
             running = add(running, received, insides[-1], p == 0)
             received = swap(running, p + 1)
@@ -424,12 +456,12 @@
         own_buckets = buckets[:1] + [own]
         other_buckets = buckets[:1] + [swap(own, 0)]
 
-    shared = [position, *[held[part] for part in parts], weight, *insides]
+    shared = [position, *[held[part] for part in parts], *weights.values(), *insides]
 
     def across(mine, operands):
         return call(
             functools.partial(
-                across_kernel, mine, cross_bits, done, first_level, spans, parts, (0, chunks)
+                across_kernel, mine, cross_bits, done, first_level, spans, parts, w_parts, (0, chunks)
             ),
             "across",
             operands,

time: 48.3 us -> 49.2 us (1.019)
  Pallas kernels: 32.7 us -> 33.6 us
    pallas_call x10, Pallas kernels: 32.7 us -> 33.6 us  [call(): pl.pallas_call(kernel, name=name, in_specs=in_specs, out_shape=out_shape,...]
  transfers between devices with their start and end apart: 7 -> 7, of which waited for: 3 -> 3; matrix products, arithmetic and copies ran while one was open for 0% -> 0% of each run, Pallas kernels for 37% -> 39%
where the time goes in v6:
time: 49.2 us; the launch traced here: 49 us
  Pallas kernels  33.6 us (68%)
  starting transfers between devices  9.47 us (19%)
  waiting for transfers between devices  5.58 us (11%)
    pallas_call x10, Pallas kernels, call(): pl.pallas_call(kernel, name=name, in_specs=in_specs, out_shape=out_shape,...  33.6 us
    ppermute x3, waiting for transfers between devices, body(): lax.ppermute(square, 'head', [(i, i ^ other) for i in range(head_size)])  5.21 us
    ppermute x4, starting transfers between devices, swap(): lax.ppermute(array, 'seq', [(i, i ^ 1 << bit) for i in range(seq_size)])  5.02 us
    ppermute x3, starting transfers between devices, body(): lax.ppermute(square, 'head', [(i, i ^ other) for i in range(head_size)])  4.45 us
  transfers between devices with their start and end apart: 7, of which 3 were waited for; matrix products, arithmetic and copies ran while one was open for 0% of the time, Pallas kernels for 39%

profile of v6, /device:TPU:0, one launch (start us, length us, event | category | flops | bytes accessed | tf_op | source)
XLA Modules:
  0.0 49.0 jit_solution(4601744830190052797)
XLA Ops:
  0.0 6.7 %states.1 = (bf16[2048,2048]{1,0:T(8,128)(2,1)S(1)}, bf16[2048,2048]{1,0:T(8,128)(2,1)S(1)}, bf16[16,7,128,128]{3,2,1,0:T(8,128)(2,1)S(1)}, bf16[16,128,128]{2,1...) custom-call(s32[1]{0:T(128)} %bitcast.pos_ref, bf16[2048,2048]{1,0:T(8,128)(2,1)} %k_hbm.1, ...), custom_call_target="tpu_custom_call" | custom-call | flops 1073741824 | bytes 16777216 | tf_op jit(solution)/shard_map/states/pallas_call | solution.py:335
  6.7 0.5 %collective-permute-start = (bf16[16,128,128]{2,1,0:T(8,128)(2,1)S(1)}, bf16[16,128,128]{2,1,0:T(8,128)(2,1)S(1)}, u32[]{:S(2)}, u32[]{:S(2)}) collective-permute-start(bf16[16,128,128]{2,1,0:T(8,128)(2,1)S(1)} %get-tuple-element.27.mine_ref), channel_id=1, source_target_pairs={{0,4},{4,0},{8,12},{12,8},{16,20},{20,16},{24,28},{28,24},{1,5},{5... | collective-permute-start | bytes 1572872 | tf_op jit(solution)/shard_map/ppermute | solution.py:388
  7.2 1.6 %local.3 = (bf16[1,2048,256]{2,1,0:T(8,128)(2,1)S(1)}, bf16[512,2048]{1,0:T(8,128)(2,1)S(1)}) custom-call(s32[1]{0:T(128)} %bitcast.pos_ref, bf16[2048,2048]{1,0:T(8,128)(2,1)S(1)} %get-tuple-element.22.k_ref, bf16[2048,2048]{1,0:T(8,128)(2,1)S(1)} %get-tuple-element.23.v_ref, bf16[16,7,128,128]{3,2,1,0:T(8,128)(2,1)S(1)} %get-tuple-element.24.local_ref, ...), custom_call_target="tpu_custom_call" | custom-call | flops 2415919104 | tf_op jit(solution)/shard_map/local/pallas_call | solution.py:335
  8.8 0.0 collective-permute-done.refs_0_.received_ref.refs_9_
  8.8 0.1 sum.2.mine_ref
  8.9 2.8 %collective-permute-start.1 = (bf16[8,128,128]{2,1,0:T(8,128)(2,1)S(1)}, bf16[8,128,128]{2,1,0:T(8,128)(2,1)S(1)}, u32[]{:S(2)}, u32[]{:S(2)}) collective-permute-start(bf16[8,128,128]{2,1,0:T(8,128)(2,1)S(1)} %sum.2.mine_ref), channel_id=1, source_target_pairs={{0,8},{4,12},{8,0},{12,4},{16,24},{20,28},{24,16},{28,20},{1,9},{5... | collective-permute-start | bytes 786440 | tf_op jit(solution)/shard_map/ppermute | solution.py:388
  11.7 7.7 %local.4 = (bf16[4,2048,256]{2,1,0:T(8,128)(2,1)S(1)}, bf16[512,2048]{1,0:T(8,128)(2,1)S(1)}, bf16[768,2048]{1,0:T(8,128)(2,1)S(1)}, f32[16,16,1280]{2,1,0:T(8,128)S(1)}) custom-call(s32[1]{0:T(128)} %bitcast.pos_ref, bf16[2048,2048]{1,0:T(8,128)(2,1)S(1)} %get-tuple-element.22.k_ref, bf16[2048,2048]{1,0:T(8,128)(2,1)S(1)} %get-tuple-element.23.v_ref, ...), custom_call_target="tpu_custom_call" | custom-call | flops 9663676416 | tf_op jit(solution)/shard_map/local/pallas_call | solution.py:335
  19.5 0.0 collective-permute-done.1.refs_1_.received_ref.refs_0_
  19.5 0.1 sum.3
  19.6 1.6 %collective-permute-start.2 = (bf16[8,128,128]{2,1,0:T(8,128)(2,1)S(1)}, bf16[8,128,128]{2,1,0:T(8,128)(2,1)S(1)}, u32[]{:S(2)}, u32[]{:S(2)}) collective-permute-start(bf16[8,128,128]{2,1,0:T(8,128)(2,1)S(1)} %sum.3), channel_id=1, source_target_pairs={{0,16},{4,20},{8,24},{12,28},{16,0},{20,4},{24,8},{28,12},{1,17},{... | collective-permute-start | bytes 786440 | tf_op jit(solution)/shard_map/ppermute | solution.py:388
  21.2 6.3 %local.5.refs_8_ = bf16[3,2048,256]{2,1,0:T(8,128)(2,1)S(1)} custom-call(s32[1]{0:T(128)} %bitcast.pos_ref, bf16[2048,2048]{1,0:T(8,128)(2,1)S(1)} %get-tuple-element.22.k_ref, bf16[2048,2048]{1,0:T(8,128)(2,1)S(1)} %get-tuple-element.23.v_ref, bf16[16,7,128,128]{3,2,1,0:T(8,128)(2,1)S(1)} %get-tuple-element.24.local_ref, ...), custom_call_target="tpu_custom_call" | custom-call | flops 7247757312 | tf_op jit(solution)/shard_map/local/pallas_call | solution.py:335
  27.4 0.4 collective-permute-done.2.refs_1_
  27.8 0.1 collective-permute-start.3
  27.9 3.5 %across.2 = (bf16[2048,1024]{1,0:T(8,128)(2,1)S(1)}, f32[1,2048]{1,0:T(1,128)S(1)}) custom-call(s32[1]{0:T(128)} %bitcast.pos_ref, bf16[256,2048]{1,0:T(8,128)(2,1)S(1)} %get-tuple-element.21.refs_0_, bf16[512,2048]{1,0:T(8,128)(2,1)S(1)} %get-tuple-element.26.refs_1_, bf16[512,2048]{1,0:T(8,128)(2,1)S(1)} %get-tuple-element.28.refs_2_, ...), custom_call_target="tpu_custom_call" | custom-call | flops 6442450944 | tf_op jit(solution)/shard_map/across/pallas_call | solution.py:335
  31.4 0.0 collective-permute-done.3.refs_10_
  31.4 0.0 copy-start
  31.4 3.8 %across.3 = (bf16[2048,1024]{1,0:T(8,128)(2,1)S(1)}, f32[1,2048]{1,0:T(1,128)S(1)}) custom-call(s32[1]{0:T(128)} %bitcast.pos_ref, bf16[256,2048]{1,0:T(8,128)(2,1)S(1)} %get-tuple-element.21.refs_0_, bf16[512,2048]{1,0:T(8,128)(2,1)S(1)} %get-tuple-element.26.refs_1_, bf16[512,2048]{1,0:T(8,128)(2,1)S(1)} %get-tuple-element.28.refs_2_, ...), custom_call_target="tpu_custom_call" | custom-call | flops 6442450944 | tf_op jit(solution)/shard_map/across/pallas_call | solution.py:335
  35.2 1.6 %collective-permute-start.4 = (f32[1,2048]{1,0:T(1,128)S(1)}, f32[1,2048]{1,0:T(1,128)S(1)}, u32[]{:S(2)}, u32[]{:S(2)}) collective-permute-start(f32[1,2048]{1,0:T(1,128)S(1)} %get-tuple-element.36.refs_0_), channel_id=1, source_target_pairs={{0,1},{1,0},{2,3},{3,2},{4,5},{5,4},{6,7},{7,6},{8,9},{9,8},{10,11... | collective-permute-start | bytes 24584 | tf_op jit(solution)/shard_map/ppermute | solution.py:480
  36.9 2.6 %collective-permute-start.5 = (f32[1,2048]{1,0:T(1,128)S(1)}, f32[1,2048]{1,0:T(1,128)S(1)}, u32[]{:S(2)}, u32[]{:S(2)}) collective-permute-start(f32[1,2048]{1,0:T(1,128)S(1)} %get-tuple-element.36.refs_0_), channel_id=1, source_target_pairs={{0,2},{1,3},{2,0},{3,1},{4,6},{5,7},{6,4},{7,5},{8,10},{9,11},{10,... | collective-permute-start | bytes 24584 | tf_op jit(solution)/shard_map/ppermute | solution.py:480
  39.5 0.2 collective-permute-start.6
  39.7 0.0 collective-permute-done.4.refs_1_
  39.7 1.7 %collective-permute-done.5.refs_2_ = f32[1,2048]{1,0:T(1,128)S(1)} collective-permute-done((f32[1,2048]{1,0:T(1,128)S(1)}, f32[1,2048]{1,0:T(1,128)S(1)}, u32[]{:S(2)}, u32[]{:S(2)}) %collective-permute-start.5) | collective-permute-done | bytes 8224 | tf_op jit(solution)/shard_map/ppermute | solution.py:480
  41.4 3.5 %collective-permute-done.6.refs_3_ = f32[1,2048]{1,0:T(1,128)S(1)} collective-permute-done((f32[1,2048]{1,0:T(1,128)S(1)}, f32[1,2048]{1,0:T(1,128)S(1)}, u32[]{:S(2)}, u32[]{:S(2)}) %collective-permute-start.6) | collective-permute-done | bytes 8224 | tf_op jit(solution)/shard_map/ppermute | solution.py:480
  44.9 0.0 copy-done
  44.9 3.9 %norm.1 = bf16[2048,2048]{1,0:T(8,128)(2,1)} custom-call(s32[1]{0:T(128)} %bitcast.pos_ref, bf16[2048,1024]{1,0:T(8,128)(2,1)S(1)} %get-tuple-element.33.own_ref, bf16[2048,1024]{1,0:T(8,128)(2,1)S(1)} %get-tuple-element.35.other_ref, f32[1,2048]{1,0:T(1,128)S(1)} %bitcast.2, f32[1,2048]{1,0:T(1,128)S(1)} %get-tuple-element.36.refs_0_, ...), custom_call_target="tpu_custom_call" | custom-call | flops 12582912 | bytes 8388608 | tf_op jit(solution)/shard_map/norm/pallas_call | solution.py:335
  (1 shorter events, 0.0 us)
Async XLA Ops:
  6.7 2.1 %collective-permute-start = (bf16[16,128,128]{2,1,0:T(8,128)(2,1)S(1)}, bf16[16,128,128]{2,1,0:T(8,128)(2,1)S(1)}, u32[]{:S(2)}, u32[]{:S(2)}) collective-permute-start(bf16[16,128,128]{2,1,0:T(8,128)(2,1)S(1)} %get-tuple-element.27.mine_ref), channel_id=1, source_target_pairs={{0,4},{4,0},{8,12},{12,8},{16,20},{20,16},{24,28},{28,24},{1,5},{5... | collective-permute-start | bytes 1572872 | tf_op jit(solution)/shard_map/ppermute | solution.py:388
  8.9 10.6 %collective-permute-start.1 = (bf16[8,128,128]{2,1,0:T(8,128)(2,1)S(1)}, bf16[8,128,128]{2,1,0:T(8,128)(2,1)S(1)}, u32[]{:S(2)}, u32[]{:S(2)}) collective-permute-start(bf16[8,128,128]{2,1,0:T(8,128)(2,1)S(1)} %sum.2.mine_ref), channel_id=1, source_target_pairs={{0,8},{4,12},{8,0},{12,4},{16,24},{20,28},{24,16},{28,20},{1,9},{5... | collective-permute-start | bytes 786440 | tf_op jit(solution)/shard_map/ppermute | solution.py:388
  19.6 8.2 %collective-permute-start.2 = (bf16[8,128,128]{2,1,0:T(8,128)(2,1)S(1)}, bf16[8,128,128]{2,1,0:T(8,128)(2,1)S(1)}, u32[]{:S(2)}, u32[]{:S(2)}) collective-permute-start(bf16[8,128,128]{2,1,0:T(8,128)(2,1)S(1)} %sum.3), channel_id=1, source_target_pairs={{0,16},{4,20},{8,24},{12,28},{16,0},{20,4},{24,8},{28,12},{1,17},{... | collective-permute-start | bytes 786440 | tf_op jit(solution)/shard_map/ppermute | solution.py:388
  27.8 3.6 %collective-permute-start.3 = (bf16[2,8,128,128]{3,2,1,0:T(8,128)(2,1)S(1)}, bf16[2,8,128,128]{3,2,1,0:T(8,128)(2,1)S(1)}, u32[]{:S(2)}, u32[]{:S(2)}) collective-permute-start(bf16[2,8,128,128]{3,2,1,0:T(8,128)(2,1)S(1)} %stack.1.refs_10_), channel_id=1, source_target_pairs={{0,4},{4,0},{8,12},{12,8},{16,20},{20,16},{24,28},{28,24},{1,5},{5... | collective-permute-start | bytes 1572872 | tf_op jit(solution)/shard_map/ppermute | solution.py:388
  31.4 13.5 %copy-start = (f32[2048]{0:T(1024)S(1)}, f32[2048]{0:T(1024)}, u32[]{:S(2)}) copy-start(f32[2048]{0:T(1024)} %param.9) | copy-start | bytes 24580
  35.2 4.5 %collective-permute-start.4 = (f32[1,2048]{1,0:T(1,128)S(1)}, f32[1,2048]{1,0:T(1,128)S(1)}, u32[]{:S(2)}, u32[]{:S(2)}) collective-permute-start(f32[1,2048]{1,0:T(1,128)S(1)} %get-tuple-element.36.refs_0_), channel_id=1, source_target_pairs={{0,1},{1,0},{2,3},{3,2},{4,5},{5,4},{6,7},{7,6},{8,9},{9,8},{10,11... | collective-permute-start | bytes 24584 | tf_op jit(solution)/shard_map/ppermute | solution.py:480
  36.9 4.5 %collective-permute-start.5 = (f32[1,2048]{1,0:T(1,128)S(1)}, f32[1,2048]{1,0:T(1,128)S(1)}, u32[]{:S(2)}, u32[]{:S(2)}) collective-permute-start(f32[1,2048]{1,0:T(1,128)S(1)} %get-tuple-element.36.refs_0_), channel_id=1, source_target_pairs={{0,2},{1,3},{2,0},{3,1},{4,6},{5,7},{6,4},{7,5},{8,10},{9,11},{10,... | collective-permute-start | bytes 24584 | tf_op jit(solution)/shard_map/ppermute | solution.py:480
  39.5 5.4 %collective-permute-start.6 = (f32[1,2048]{1,0:T(1,128)S(1)}, f32[1,2048]{1,0:T(1,128)S(1)}, u32[]{:S(2)}, u32[]{:S(2)}) collective-permute-start(f32[1,2048]{1,0:T(1,128)S(1)} %get-tuple-element.36.refs_0_), channel_id=1, source_target_pairs={{0,3},{1,2},{2,1},{3,0},{4,7},{5,6},{6,5},{7,4},{8,11},{9,10},{10,... | collective-permute-start | bytes 24584 | tf_op jit(solution)/shard_map/ppermute | solution.py:480
